TPU v7x, 256 devices: a whole 4x4x8 slice. The times are simulated.
256 devices in a mesh: section: 16 (over x_hi, y, core), dp: 16 (over z, x_lo).
Axes of the slice: x: 4 (x_hi: 2, x_lo: 2; x = x_hi * 2 + x_lo), y: 4, z: 8, core: 2. Of those that a mesh axis runs over, the one named last changes fastest.
Arguments:
- handed: bfloat16 [16, 2048, 4096], P('section', 'dp'), may hold values from -6 to 6
- lengths: int32 [16, 16, 4], P('section', 'dp'), may hold values from 1 to 64, as said below
- placement: int32 [16, 4, 2], replicated, may hold values from 0 to 3, as said below
- frozen: bfloat16 [16, 4096, 4096], P('section', None, 'dp'), may hold values from -0.09375 to 0.09375
- adapter_down_weight: bfloat16 [16, 4, 64, 4096], P('section'), may hold values from -0.09375 to 0.09375
- adapter_up_weight: bfloat16 [16, 4, 64, 4096], P('section'), may hold values from -0.75 to 0.75
- cotangent: bfloat16 [16, 2048, 4096], P('section', 'dp'), may hold values from -0.29882812 to 0.29882812
Outputs:
- passed: bfloat16 [16, 2048, 4096], P('section', 'dp')
- grad_a: float32 [16, 4, 64, 4096], P('section', None, None, 'dp')
- grad_b: float32 [16, 4, 64, 4096], P('section', None, None, 'dp')
Inputs may be any that keep to these rules, and one draw needn't show every extreme that they name: placement[s, j] = (o, k) names slot k of section s + o - 1 as the host of job j's adapter at section s's layer; o is 1 for all jobs but at most one with o = 2 (host: the next section) and at most one with o = 0 (host: the previous section), never past the first or last section; every slot of every section hosts exactly one adapter. Each block's lengths sum to 128, each at least 1. In every section below the last some block has 64 rows of the job whose adapter the next section hosts; in every section above the first some block has 64 rows of the job whose adapter the previous section hosts.
All inputs are finite; a program needn't handle non-finite values.
Results may differ from a plain program's by a relative error of at most 0.0053.
Values may be sent and summed in bfloat16 or wider, within the bound.
No kernel may reach another device: no remote copies, remote signals or barrier semaphores. Data moves between devices by JAX's collectives and lax.ppermute only.
A program may use at most 128 MiB of HBM per device.

v0:
```python
import jax
import jax.numpy as jnp
from jax import lax
from jax.sharding import PartitionSpec as P

ADAPTER_RANK = 64
ADJUST_JOBS = 4
MOST = 64


ADAPTER_SCALE = 0.5
CONTRACT_ROWS = (((0,), (0,)), ((), ()))
CONTRACT_FEATURES = (((1,), (1,)), ((), ()))


def from_behind(value, axis, by):
    length = lax.axis_size(axis)
    return lax.ppermute(value, axis, [(i, (i + by) % length) for i in range(length)])


def shifted(block, axis, distance):
    devices = range(lax.axis_size(axis))
    route = [(i - distance, i) for i in devices if i - distance in devices]
    return lax.ppermute(block, axis, route)


def slot_columns(slot_ids, keep_rows):
    column_slot = jnp.arange(ADJUST_JOBS * ADAPTER_RANK, dtype=jnp.int32) // ADAPTER_RANK
    return ((slot_ids[:, None] == column_slot[None, :]) & keep_rows[:, None]).astype(jnp.float32)


def low_rank(row_inputs, row_grads, chosen_slots, joined_down_maps, joined_up_maps):
    rank_codes = (
        lax.dot_general(
            row_inputs, joined_down_maps, CONTRACT_FEATURES, preferred_element_type=jnp.float32
        )
        * chosen_slots
    ).astype(jnp.bfloat16)
    adapted_output = lax.optimization_barrier(
        (
            ADAPTER_SCALE * jnp.dot(rank_codes, joined_up_maps, preferred_element_type=jnp.float32)
        ).astype(jnp.bfloat16)
    )
    gradient_signals = (
        ADAPTER_SCALE
        * lax.dot_general(
            row_grads, joined_up_maps, CONTRACT_FEATURES, preferred_element_type=jnp.float32
        )
        * chosen_slots
    ).astype(jnp.bfloat16)
    return (adapted_output, rank_codes, gradient_signals)


def plan_slot(placement, section_id, code):
    section_plan = lax.dynamic_index_in_dim(placement, section_id, 0, keepdims=False)
    return jnp.sum(jnp.where(section_plan[:, 0] == code, section_plan[:, 1], 0))


def on_device(
    handed, lengths, placement, frozen, adapter_down_weight, adapter_up_weight, cotangent
):
    incoming = from_behind(handed[0], "section", 1)
    upstream_gradient = cotangent[0]
    row_count = incoming.shape[0]
    section_id = lax.axis_index("section")
    section_count = lax.axis_size("section")
    section_plan = lax.dynamic_index_in_dim(placement, section_id, 0, keepdims=False)
    offsets = section_plan[:, 0] - 1
    counts = lengths[0, 0]
    row_ends = jnp.cumsum(counts)
    row_starts = row_ends - counts
    positions = jnp.arange(row_count, dtype=jnp.int32)
    job_ids = jnp.sum((positions[:, None] >= row_ends[None, :]).astype(jnp.int32), axis=1)
    job_match = job_ids[:, None] == jnp.arange(ADJUST_JOBS, dtype=jnp.int32)[None, :]
    row_offset = jnp.sum(jnp.where(job_match, offsets[None, :], 0), axis=1)
    row_slot = jnp.sum(jnp.where(job_match, section_plan[None, :, 1], 0), axis=1)
    joined_down_maps = adapter_down_weight[0].reshape(ADJUST_JOBS * ADAPTER_RANK, -1)
    joined_up_maps = adapter_up_weight[0].reshape(ADJUST_JOBS * ADAPTER_RANK, -1)
    both_rows = jnp.stack([incoming, upstream_gradient])

    def pick_rows(code):
        sending = offsets == code
        first_row = jnp.sum(jnp.where(sending, row_starts, 0))
        row_total = jnp.sum(jnp.where(sending, counts, 0))
        steps_in = jnp.arange(MOST, dtype=jnp.int32)
        taken = jnp.take(both_rows, jnp.clip(first_row + steps_in, 0, row_count - 1), axis=1)
        return (
            jnp.where((steps_in < row_total)[None, :, None], taken, jnp.zeros_like(taken)),
            first_row,
        )

    send_up, first_up = pick_rows(1)
    send_down, first_down = pick_rows(-1)
    slot_below = plan_slot(placement, jnp.maximum(section_id - 1, 0), 2)
    slot_above = plan_slot(placement, jnp.minimum(section_id + 1, section_count - 1), 0)
    from_below = shifted(send_up, "section", 1)
    from_above = shifted(send_down, "section", -1)
    guest_inputs = jnp.concatenate([from_below[0], from_above[0]])
    guest_grads = jnp.concatenate([from_below[1], from_above[1]])
    guest_slots = jnp.concatenate(
        [jnp.full((MOST,), slot_below, jnp.int32), jnp.full((MOST,), slot_above, jnp.int32)]
    )
    guest_out, guest_codes, guest_signals = low_rank(
        guest_inputs,
        guest_grads,
        slot_columns(guest_slots, guest_slots >= 0),
        joined_down_maps,
        joined_up_maps,
    )
    to_below = guest_out[:MOST]
    to_above = guest_out[MOST:]
    done_up = shifted(to_below, "section", -1)
    done_down = shifted(to_above, "section", 1)
    own_out, own_codes, own_signals = low_rank(
        incoming,
        upstream_gradient,
        slot_columns(row_slot, row_offset == 0),
        joined_down_maps,
        joined_up_maps,
    )
    up_rows = jnp.take(done_up, jnp.clip(positions - first_up, 0, MOST - 1), axis=0)
    down_rows = jnp.take(done_down, jnp.clip(positions - first_down, 0, MOST - 1), axis=0)
    adapted_output = jnp.where(
        (row_offset == 1)[:, None],
        up_rows,
        jnp.where((row_offset == -1)[:, None], down_rows, own_out),
    )
    columns = jnp.dot(
        lax.all_gather(incoming, "dp", axis=0, tiled=True),
        frozen[0],
        preferred_element_type=jnp.float32,
    ).astype(jnp.bfloat16)
    base_out = lax.all_to_all(columns, "dp", split_axis=0, concat_axis=1, tiled=True)
    passed = (base_out.astype(jnp.float32) + adapted_output.astype(jnp.float32)).astype(
        jnp.bfloat16
    )
    all_inputs = jnp.concatenate([incoming, guest_inputs])
    all_grads = jnp.concatenate([upstream_gradient, guest_grads])
    all_codes = jnp.concatenate([own_codes, guest_codes])
    all_signals = jnp.concatenate([own_signals, guest_signals])
    part_down = lax.dot_general(
        all_signals, all_inputs, CONTRACT_ROWS, preferred_element_type=jnp.float32
    )
    partial_up_output = ADAPTER_SCALE * lax.dot_general(
        all_codes, all_grads, CONTRACT_ROWS, preferred_element_type=jnp.float32
    )
    grad_down, grad_up = (
        lax.psum_scatter(part_down, "dp", scatter_dimension=1, tiled=True),
        lax.psum_scatter(partial_up_output, "dp", scatter_dimension=1, tiled=True),
    )
    return (
        passed[None],
        grad_down.reshape(1, ADJUST_JOBS, ADAPTER_RANK, -1),
        grad_up.reshape(1, ADJUST_JOBS, ADAPTER_RANK, -1),
    )


def solution(mesh):
    in_specs = (
        P("section", "dp", None),
        P("section", "dp", None),
        P(),
        P("section", None, "dp"),
        P("section", None, None, None),
        P("section", None, None, None),
        P("section", "dp", None),
    )
    out_specs = (
        P("section", "dp", None),
        P("section", None, None, "dp"),
        P("section", None, None, "dp"),
    )
    return jax.shard_map(
        on_device, mesh=mesh, in_specs=in_specs, out_specs=out_specs, check_vma=False
    )
```

profile of v0, /device:TPU:6, one launch (start us, length us, event | category | flops | bytes accessed | tf_op | source)
XLA Modules:
  0.0 619.2 jit_solution(1967064135054940960)
XLA Ops:
  7.3 18.0 %collective-permute-done = bf16[128,4096]{1,0:T(8,128)(2,1)S(1)} collective-permute-done((bf16[128,4096]{1,0:T(8,128)(2,1)}, bf16[128,4096]{1,0:T(8,128)(2,1)S(1)}, u32[]{:S(2)}, u32[]{:S(2)}) %collective-permute-start) | collective-permute-done | bytes 1048608 | tf_op jit(solution)/shard_map/ppermute | solution.py:18
  25.4 1.0 copy-done.1
  26.4 0.9 constant_dynamic-slice_fusion
  27.4 0.8 reduce-window.8
  28.2 4.9 copy.47
  34.0 0.7 fusion.39
  35.3 0.7 concatenate.23
  36.0 0.7 fusion.35
  36.8 0.7 compare_select_fusion.2
  38.1 1.3 compare_and_fusion.4
  39.4 1.3 compare_and_fusion.5
  41.0 2.1 fusion.18
  43.0 2.4 copy.46
  45.4 5.6 pad_maximum_fusion
  51.0 5.1 gather_fusion.1
  56.2 3.4 broadcast_select_fusion.2
  59.6 2.1 collective-permute-start.2
  61.7 5.2 gather_fusion
  66.8 2.6 broadcast_select_fusion.3
  69.4 2.4 collective-permute-start.1
  71.9 0.7 broadcast_compare_fusion.2
  72.6 46.1 %collective-permute-done.2 = bf16[2,64,4096]{2,0,1:T(2,128)(2,1)} collective-permute-done((bf16[2,64,4096]{2,0,1:T(2,128)(2,1)}, bf16[2,64,4096]{2,0,1:T(2,128)(2,1)}, u32[]{:S(2)}, u32[]{:S(2)}) %collective-permute-start.2) | collective-permute-done | bytes 1048608 | tf_op jit(solution)/shard_map/ppermute | solution.py:24
  118.7 3.9 fusion.46
  123.2 10.9 %collective-permute-done.1 = bf16[2,64,4096]{2,0,1:T(2,128)(2,1)S(1)} collective-permute-done((bf16[2,64,4096]{2,0,1:T(2,128)(2,1)S(1)}, bf16[2,64,4096]{2,0,1:T(2,128)(2,1)S(1)}, u32[]{:S(2)}, u32[]{:S(2)}) %collective-permute-start.1) | collective-permute-done | bytes 1048608 | tf_op jit(solution)/shard_map/ppermute | solution.py:24
  134.1 2.4 fusion.45
  138.3 0.8 fusion.19
  139.2 2.7 fusion.2
  142.2 2.6 fusion.17
  144.8 0.8 fusion.16
  146.3 2.7 convolution_multiply_fusion
  149.1 1.3 compare_and_fusion.2
  150.4 238.0 %all-gather.2.cloned.1.call-done = bf16[2048,4096]{1,0:T(8,128)(2,1)} async-done(((bf16[128,4096]{1,0:T(8,128)(2,1)}), bf16[2048,4096]{1,0:T(8,128)(2,1)}) %all-gather.2.cloned.1.call-update) | async-done | bytes 16777232 | tf_op jit(solution)/shard_map/all_gather | solution.py:129
  388.4 12.0 %convolution_convert_fusion = bf16[2048,256]{1,0:T(8,128)(2,1)} fusion(bf16[2048,4096]{1,0:T(8,128)(2,1)} %all-gather.2.cloned.1.call-done, bf16[1,4096,256]{2,1,0:T(8,128)(2,1)} %param.14), kind=kOutput, calls=%fused_computation.9 | convolution fusion | flops 4295491584 | bytes 19922944 | tf_op jit(solution)/shard_map/dot_general | solution.py:128
  400.4 13.5 %all-to-all-start = ((bf16[16,128,256]{2,1,0:T(8,128)(2,1)}), bf16[16,128,256]{2,1,0:T(8,128)(2,1)}, u32[]{:S(2)}, u32[]{:S(2)}) async-start(bf16[16,128,256]{2,1,0:T(8,128)(2,1)} %bitcast.2), calls=%async_computation | async-start | bytes 2097152 | tf_op jit(solution)/shard_map/all_to_all | solution.py:133
  413.9 0.7 compare_select_fusion
  415.1 0.9 fusion.47
  416.0 1.9 collective-permute-start.4
  417.9 7.3 %collective-permute-start.3 = (bf16[64,4096]{1,0:T(8,128)(2,1)}, bf16[64,4096]{1,0:T(8,128)(2,1)S(1)}, u32[]{:S(2)}, u32[]{:S(2)}) collective-permute-start(bf16[64,4096]{1,0:T(8,128)(2,1)} %get-tuple-element.15), channel_id=1, source_target_pairs={{16,0},{32,16},{48,32},{64,48},{80,64},{96,80},{112,96},{128,112},... | collective-permute-start | bytes 1572872 | tf_op jit(solution)/shard_map/ppermute | solution.py:24
  425.8 1.5 fusion.1
  427.3 34.1 %collective-permute-done.4 = bf16[64,4096]{1,0:T(8,128)(2,1)S(1)} collective-permute-done((bf16[64,4096]{1,0:T(8,128)(2,1)S(1)}, bf16[64,4096]{1,0:T(8,128)(2,1)S(1)}, u32[]{:S(2)}, u32[]{:S(2)}) %collective-permute-start.4) | collective-permute-done | bytes 524320 | tf_op jit(solution)/shard_map/ppermute | solution.py:24
  461.4 2.2 gather_fusion.3
  463.6 1.3 collective-permute-done.3
  464.9 2.2 gather_fusion.2
  467.1 1.5 convert_bitcast_fusion
  468.8 1.0 copy-done.5
  470.4 1.6 fusion.20
  472.0 40.5 %reduce-scatter.3.cloned.1.call-done = f32[256,256]{1,0:T(8,128)} async-done(((f32[256,4096]{1,0:T(8,128)}), f32[256,256]{1,0:T(8,128)}) %reduce-scatter.3.cloned.1.call-update) | async-done | bytes 262160 | tf_op jit(solution)/shard_map/reduce_scatter | solution.py:148
  512.5 100.1 %reduce-scatter.5.cloned.1.call-done = f32[256,256]{1,0:T(8,128)} async-done(((f32[256,4096]{1,0:T(8,128)}), f32[256,256]{1,0:T(8,128)}) %reduce-scatter.5.cloned.1.call-update) | async-done | bytes 262160 | tf_op jit(solution)/shard_map/reduce_scatter | solution.py:149
  (64 shorter events, 7.9 us)
Async XLA Ops:
  7.2 33.8 %copy-start = (bf16[1,4,64,4096]{3,2,1,0:T(8,128)(2,1)S(1)}, bf16[1,4,64,4096]{3,2,1,0:T(8,128)(2,1)}, u32[]{:S(2)}) copy-start(bf16[1,4,64,4096]{3,2,1,0:T(8,128)(2,1)} %param.16) | copy-start | bytes 6291460
  7.2 381.2 %all-gather.2.cloned.1.call-start = ((), (), s32[]{:S(2)}) async-start(), calls=%async_computation.3 | async-start | bytes 17825792 | tf_op jit(solution)/shard_map/all_gather | solution.py:129
  7.2 18.1 %collective-permute-start = (bf16[128,4096]{1,0:T(8,128)(2,1)}, bf16[128,4096]{1,0:T(8,128)(2,1)S(1)}, u32[]{:S(2)}, u32[]{:S(2)}) collective-permute-start(bf16[128,4096]{1,0:T(8,128)(2,1)} %bitcast.95), channel_id=1, source_target_pairs={{0,16},{16,32},{32,48},{48,64},{64,80},{80,96},{96,112},{112,128},... | collective-permute-start | bytes 3145736 | tf_op jit(solution)/shard_map/ppermute | solution.py:18
  25.4 1.0 copy-start.1
  25.4 10.7 %copy-start.17 = (s32[1,1,4]{2,1,0:T(1,128)S(1)}, s32[1,1,4]{2,1,0:T(1,128)}, u32[]{:S(2)}) copy-start(s32[1,1,4]{2,1,0:T(1,128)} %param.12) | copy-start | bytes 52
  26.3 486.2 %reduce-scatter.3.cloned.1.call-start = ((), (), s32[]{:S(2)}) async-start(), calls=%async_computation.4 | async-start | bytes 4456448 | tf_op jit(solution)/shard_map/reduce_scatter | solution.py:148
  33.2 9.9 %copy-start.2 = (bf16[128,4096]{1,0:T(8,128)(2,1)S(1)}, bf16[128,4096]{1,0:T(8,128)(2,1)}, u32[]{:S(2)}) copy-start(bf16[128,4096]{1,0:T(8,128)(2,1)} %copy-done.1) | copy-start | bytes 3145732
  43.0 2.4 copy-start.3
  59.6 59.1 %collective-permute-start.2 = (bf16[2,64,4096]{2,0,1:T(2,128)(2,1)}, bf16[2,64,4096]{2,0,1:T(2,128)(2,1)}, u32[]{:S(2)}, u32[]{:S(2)}) collective-permute-start(bf16[2,64,4096]{2,0,1:T(2,128)(2,1)} %broadcast_select_fusion.2), channel_id=1, source_target_pairs={{16,0},{32,16},{48,32},{64,48},{80,64},{96,80},{112,96},{128,112},... | collective-permute-start | bytes 3145736 | tf_op jit(solution)/shard_map/ppermute | solution.py:24
  69.4 64.6 %collective-permute-start.1 = (bf16[2,64,4096]{2,0,1:T(2,128)(2,1)S(1)}, bf16[2,64,4096]{2,0,1:T(2,128)(2,1)S(1)}, u32[]{:S(2)}, u32[]{:S(2)}) collective-permute-start(bf16[2,64,4096]{2,0,1:T(2,128)(2,1)S(1)} %broadcast_select_fusion.3), channel_id=1, source_target_pairs={{0,16},{16,32},{32,48},{48,64},{64,80},{80,96},{96,112},{112,128},... | collective-permute-start | bytes 3145736 | tf_op jit(solution)/shard_map/ppermute | solution.py:24
  123.1 16.0 %copy-start.8 = (bf16[1,64,4096]{2,1,0:T(8,128)(2,1)}, bf16[1,64,4096]{2,1,0:T(8,128)(2,1)S(1)}, u32[]{:S(2)}) copy-start(bf16[1,64,4096]{2,1,0:T(8,128)(2,1)S(1)} %copy.59) | copy-start | bytes 1572868
  137.1 2.1 copy-start.10
  137.7 1.5 copy-start.13
  138.3 0.9 copy-start.15
  141.9 470.8 %reduce-scatter.5.cloned.1.call-start = ((), (), s32[]{:S(2)}) async-start(), calls=%async_computation.5 | async-start | bytes 4456448 | tf_op jit(solution)/shard_map/reduce_scatter | solution.py:149
  142.1 2.6 copy-start.9
  142.2 2.6 copy-start.11
  142.2 2.6 copy-start.12
  144.8 1.2 copy-start.4
  144.8 1.4 copy-start.14
  144.8 1.5 copy-start.16
  400.4 66.6 %all-to-all-start = ((bf16[16,128,256]{2,1,0:T(8,128)(2,1)}), bf16[16,128,256]{2,1,0:T(8,128)(2,1)}, u32[]{:S(2)}, u32[]{:S(2)}) async-start(bf16[16,128,256]{2,1,0:T(8,128)(2,1)} %bitcast.2), calls=%async_computation | async-start | bytes 2097152 | tf_op jit(solution)/shard_map/all_to_all | solution.py:133
  416.0 45.4 %collective-permute-start.4 = (bf16[64,4096]{1,0:T(8,128)(2,1)S(1)}, bf16[64,4096]{1,0:T(8,128)(2,1)S(1)}, u32[]{:S(2)}, u32[]{:S(2)}) collective-permute-start(bf16[64,4096]{1,0:T(8,128)(2,1)S(1)} %get-tuple-element.16), channel_id=1, source_target_pairs={{0,16},{16,32},{32,48},{48,64},{64,80},{80,96},{96,112},{112,128},... | collective-permute-start | bytes 1572872 | tf_op jit(solution)/shard_map/ppermute | solution.py:24
  417.9 47.0 %collective-permute-start.3 = (bf16[64,4096]{1,0:T(8,128)(2,1)}, bf16[64,4096]{1,0:T(8,128)(2,1)S(1)}, u32[]{:S(2)}, u32[]{:S(2)}) collective-permute-start(bf16[64,4096]{1,0:T(8,128)(2,1)} %get-tuple-element.15), channel_id=1, source_target_pairs={{16,0},{32,16},{48,32},{64,48},{80,64},{96,80},{112,96},{128,112},... | collective-permute-start | bytes 1572872 | tf_op jit(solution)/shard_map/ppermute | solution.py:24
  468.5 1.2 copy-start.5
  468.5 1.5 copy-start.6
  468.6 1.9 copy-start.7
Sparse Core Ops, SparseCore 0:
  26.5 361.8 all-gather.1
  391.5 120.9 reduce-scatter.2
  515.6 96.9 reduce-scatter.4
where the time goes:
time: 622 us; the launch traced here: 619 us
  waiting for transfers between devices  489 us (79%)
  local copies, waits for them, and re-layouts  37.5 us (6%)
  starting transfers between devices  27.6 us (4%)
  matrix products  25.7 us (4%)
  other arithmetic  24.9 us (4%)
  between operations  14.2 us (2%)
    all_gather x1, waiting for transfers between devices, on_device(): lax.all_gather(incoming, 'dp', axis=0, tiled=True)  238 us
    reduce_scatter x1, waiting for transfers between devices, on_device(): lax.psum_scatter(partial_up_output, 'dp', scatter_dimension=1, tiled=True)  100 us
    ppermute x4, waiting for transfers between devices, shifted(): return lax.ppermute(block, axis, route)  92.5 us
    reduce_scatter x1, waiting for transfers between devices, on_device(): lax.psum_scatter(part_down, 'dp', scatter_dimension=1, tiled=True)  40.5 us
    ppermute x1, waiting for transfers between devices, from_behind(): lax.ppermute(value, axis, [(i, (i + by) % length) for i in range(length)])  18 us
    ppermute x4, starting transfers between devices, shifted(): return lax.ppermute(block, axis, route)  13.7 us
    all_to_all x1, starting transfers between devices, on_device(): lax.all_to_all(columns, 'dp', split_axis=0, concat_axis=1, tiled=True)  13.5 us
  transfers between devices with their start and end apart: 9, of which 8 were waited for; matrix products, arithmetic and copies ran while one was open for 14% of the time, Pallas kernels for 0%

commit v1 on v0

v1 whole, which is shorter than its diff:
```python
import jax
import jax.numpy as jnp
from jax import lax
from jax.sharding import PartitionSpec as P

RANK = 64
JOBS = 4
SCALE = 0.5
LINES = 2
ROWS_BY_ROWS = (((0,), (0,)), ((), ()))
FEATURES = (((1,), (1,)), ((), ()))


def dot32(a, b, dims=(((1,), (0,)), ((), ()))):
    return lax.dot_general(a, b, dims, preferred_element_type=jnp.float32)


def along_z(value, by, depth):
    route = [(z * LINES + x, ((z + by) % depth) * LINES + x) for z in range(depth) for x in range(LINES)]
    return lax.ppermute(value, "dp", route)


def across_x(value, devices):
    return lax.ppermute(value, "dp", [(d, d ^ 1) for d in range(devices)])


def section_shift(value, by, sections):
    route = [(i, i + by) for i in range(sections) if 0 <= i + by < sections]
    return lax.ppermute(value, "section", route)


def hosted_slot(placement, section, code):
    plan = lax.dynamic_index_in_dim(placement, section, 0, keepdims=False)
    return jnp.sum(jnp.where(plan[:, 0] == code, plan[:, 1], 0))


def on_device(handed, lengths, placement, frozen, down, up, cotangent):
    sections = lax.axis_size("section")
    devices = lax.axis_size("dp")
    depth = devices // LINES
    s = lax.axis_index("section")
    d = lax.axis_index("dp")
    z, x = d // LINES, d % LINES
    lines = [[k * LINES + i for k in range(depth)] for i in range(LINES)]
    rows, width = handed.shape[1:]
    half = rows // 2
    cols = width // devices
    wide = width // depth

    ring = [(i, (i + 1) % sections) for i in range(sections)]
    x_a = lax.ppermute(handed[0, :half], "section", ring)
    x_b = lax.ppermute(handed[0, half:], "section", ring)

    for_below = hosted_slot(placement, jnp.maximum(s - 1, 0), 2)
    for_above = hosted_slot(placement, jnp.minimum(s + 1, sections - 1), 0)
    take = lambda w, k: lax.dynamic_index_in_dim(w[0], k, 0, keepdims=False)
    down_above = section_shift(take(down, for_below), -1, sections)
    down_below = section_shift(take(down, for_above), 1, sections)
    up_above = section_shift(take(up, for_below), -1, sections)
    up_below = section_shift(take(up, for_above), 1, sections)
    own_down = down[0].reshape(JOBS * RANK, width)
    own_up = up[0].reshape(JOBS * RANK, width)

    w_own = frozen[0]
    w_pair = across_x(w_own, devices)

    cot = cotangent[0]
    cot_line = lax.all_to_all(
        cot.reshape(rows, depth, wide).swapaxes(0, 1), "dp", 0, 0, axis_index_groups=lines, tiled=True
    ).reshape(depth * rows, wide)

    own = jnp.concatenate([x_a, x_b])
    fwd_a = fwd_b = bwd_a = bwd_b = None
    fwd, bwd = [], []
    pa, pb, qa, qb = x_a, x_b, x_a, x_b
    far = depth // 2
    for _ in range(1, far):
        pa, qa = along_z(pa, 1, depth), along_z(qa, -1, depth)
        pb, qb = along_z(pb, 1, depth), along_z(qb, -1, depth)
        fwd.append((pa, pb))
        bwd.append((qa, qb))
    last = (along_z(pa, 1, depth), along_z(qb, -1, depth))
    blocks = [(x_a, x_b)] + fwd + [last] + bwd[::-1]

    def adapter_of(counts):
        ends = jnp.cumsum(counts, axis=-1)
        job = jnp.sum((jnp.arange(rows, dtype=jnp.int32)[:, None] >= ends[..., None, :]).astype(jnp.int32), axis=-1)
        plan = lax.dynamic_index_in_dim(placement, s, 0, keepdims=False)
        which = jnp.where(plan[:, 0] == 1, plan[:, 1], jnp.where(plan[:, 0] == 2, JOBS, JOBS + 1))
        match = job[..., None] == jnp.arange(JOBS, dtype=jnp.int32)
        return jnp.sum(jnp.where(match, which, 0), axis=-1)

    adapter = adapter_of(lengths[0, 0])
    column = jnp.arange((JOBS + 2) * RANK, dtype=jnp.int32) // RANK
    chosen = adapter[:, None] == column[None, :]

    def masked(own_part, above_part, below_part):
        return jnp.where(chosen, jnp.concatenate([own_part, above_part, below_part], axis=1), 0.0)

    codes = masked(
        dot32(own, own_down, FEATURES), dot32(own, down_above, FEATURES), dot32(own, down_below, FEATURES)
    ).astype(jnp.bfloat16)
    signals = (
        SCALE * masked(dot32(cot, own_up, FEATURES), dot32(cot, up_above, FEATURES), dot32(cot, up_below, FEATURES))
    ).astype(jnp.bfloat16)
    n = JOBS * RANK
    adapted = (
        SCALE
        * (
            dot32(codes[:, :n], own_up)
            + dot32(codes[:, n : n + RANK], up_above)
            + dot32(codes[:, n + RANK :], up_below)
        )
    ).astype(jnp.bfloat16)

    def narrow(v):
        return jnp.sum(v.astype(jnp.float32).reshape(rows, JOBS + 2, RANK), axis=1).astype(jnp.bfloat16)

    tail = jnp.zeros((16, 2 * RANK), jnp.bfloat16).at[0, :JOBS].set(lengths[0, 0].astype(jnp.bfloat16))
    sent = jnp.concatenate([jnp.concatenate([narrow(codes), narrow(signals)], axis=1), tail])
    line = lax.all_gather(sent, "dp", axis_index_groups=lines)
    line_adapter = adapter_of(line[:, rows, :JOBS].astype(jnp.int32))
    line_chosen = line_adapter[:, :, None] == column
    line_codes = jnp.where(line_chosen, jnp.tile(line[:, :rows, :RANK], (1, 1, JOBS + 2)), 0)
    line_signals = jnp.where(line_chosen, jnp.tile(line[:, :rows, RANK:], (1, 1, JOBS + 2)), 0)

    part_up = SCALE * dot32(line_codes.reshape(depth * rows, -1), cot_line, ROWS_BY_ROWS)

    pieces = [None] * depth
    part_down = None
    for k in sorted(range(depth), key=lambda k: min(k, depth - k)):
        block = own if k == 0 else jnp.concatenate(blocks[k])
        piece = jnp.concatenate([dot32(block, w_own), dot32(block, w_pair)], axis=1).astype(jnp.bfloat16)
        pieces[k] = piece if k == 0 else along_z(piece, -k, depth)
        block_signals = lax.dynamic_index_in_dim(line_signals, (z - k) % depth, 0, keepdims=False)
        term = dot32(block_signals, lax.dynamic_slice_in_dim(block, z * wide, wide, 1), ROWS_BY_ROWS)
        part_down = term if part_down is None else part_down + term

    passed = jnp.zeros((rows, width), jnp.bfloat16)
    for k in sorted(range(depth), key=lambda k: min(k, depth - k)):
        for side, piece in ((x, pieces[k][:, :cols]), (1 - x, pieces[k][:, cols:])):
            at = ((z + k) % depth) * wide + side * cols
            added = piece.astype(jnp.float32) + lax.dynamic_slice_in_dim(adapted, at, cols, 1).astype(jnp.float32)
            passed = lax.dynamic_update_slice_in_dim(passed, added.astype(jnp.bfloat16), at, 1)

    slot_below = hosted_slot(placement, jnp.maximum(s - 1, 0), 2)
    slot_above = hosted_slot(placement, jnp.minimum(s + 1, sections - 1), 0)
    slots = jnp.arange(JOBS, dtype=jnp.int32)[:, None, None]

    def gradient(part):
        mine = lax.dynamic_slice_in_dim(part, x * cols, cols, 1)
        theirs = lax.dynamic_slice_in_dim(part, (1 - x) * cols, cols, 1)
        total = (mine + across_x(theirs, devices)).reshape(JOBS + 2, RANK, cols)
        from_below = section_shift(total[JOBS], 1, sections)
        from_above = section_shift(total[JOBS + 1], -1, sections)
        return (
            total[:JOBS]
            + jnp.where(slots == slot_below, from_below[None], 0.0)
            + jnp.where(slots == slot_above, from_above[None], 0.0)
        )[None]

    return passed[None], gradient(part_down), gradient(part_up)


def solution(mesh):
    in_specs = (
        P("section", "dp", None),
        P("section", "dp", None),
        P(),
        P("section", None, "dp"),
        P("section", None, None, None),
        P("section", None, None, None),
        P("section", "dp", None),
    )
    out_specs = (
        P("section", "dp", None),
        P("section", None, None, "dp"),
        P("section", None, None, "dp"),
    )
    return jax.shard_map(on_device, mesh=mesh, in_specs=in_specs, out_specs=out_specs, check_vma=False)
```

time: 622 us -> 257 us (0.41)
  waiting for transfers between devices: 489 us -> 62.7 us
  starting transfers between devices: 27.6 us -> 80.6 us
  blocking collectives: 0 us -> 26.3 us
  matrix products: 25.7 us -> 43.8 us
  other arithmetic: 24.9 us -> 7.82 us
  local copies, waits for them, and re-layouts: 37.5 us -> 25.3 us
  between operations: 14.2 us -> 6.12 us
    all_gather x1 -> x0, waiting for transfers between devices: 238 us -> none  [on_device(): lax.all_gather(incoming, 'dp', axis=0, tiled=True)]
    reduce_scatter x2 -> x0, waiting for transfers between devices: 141 us -> none  [the longest x1 100 us: on_device(): lax.psum_scatter(partial_up_output, 'dp', scatter_dimension=1, tiled=True)]
    ppermute x5 -> x34, starting transfers between devices: 13.8 us -> 72.1 us  [the longest x8 38.5 us: section_shift(): return lax.ppermute(value, 'section', route)]
    ppermute x5 -> x34, waiting for transfers between devices: 110 us -> 62.7 us  [the longest x21 57.7 us: along_z(): return lax.ppermute(value, 'dp', route)]
    all_gather x0 -> x1, blocking collectives: none -> 26.3 us  [on_device(): line = lax.all_gather(sent, 'dp', axis_index_groups=lines)]
    dot_general x9 -> x34, matrix products: 25.7 us -> 43.8 us  [dot32(): return lax.dot_general(a, b, dims, preferred_element_type=jnp.float32)]
    gather x4 -> x0, local copies, waits for them, and re-layouts: 14.7 us -> none  [the longest x2 10.3 us: pick_rows(): jnp.take(both_rows, jnp.clip(first_row + steps_in, 0, row_count - 1), axi...]
    select_n x7 -> x4, other arithmetic: 8.61 us -> 0.27 us  [the longest x1 0.25 us: on_device(): jnp.where(line_chosen, jnp.tile(line[:, :rows, RANK:], (1, 1, JOBS + 2)), 0)]
  transfers between devices with their start and end apart: 9 -> 35, of which waited for: 8 -> 11; matrix products, arithmetic and copies ran while one was open for 14% -> 28% of each run, Pallas kernels for 0% -> 0%
where the time goes in v1:
time: 257 us; the launch traced here: 253 us
  starting transfers between devices  80.6 us (31%)
  waiting for transfers between devices  62.7 us (24%)
  matrix products  43.8 us (17%)
  blocking collectives  26.3 us (10%)
  local copies, waits for them, and re-layouts  25.3 us (10%)
  other arithmetic  7.82 us (3%)
  between operations  6.12 us (2%)
    ppermute x21, waiting for transfers between devices, along_z(): return lax.ppermute(value, 'dp', route)  57.7 us
    dot_general x34, matrix products, dot32(): return lax.dot_general(a, b, dims, preferred_element_type=jnp.float32)  43.8 us
    ppermute x8, starting transfers between devices, section_shift(): return lax.ppermute(value, 'section', route)  38.5 us
    ppermute x21, starting transfers between devices, along_z(): return lax.ppermute(value, 'dp', route)  33.4 us
    all_gather x1, blocking collectives, on_device(): line = lax.all_gather(sent, 'dp', axis_index_groups=lines)  26.3 us
    all_to_all x1, starting transfers between devices, on_device(): lax.all_to_all(cot.reshape(rows, depth, wide).swapaxes(0, 1), 'dp', 0, 0,...  8.47 us
    unnamed x66, local copies, waits for them, and re-layouts  8.07 us
    concatenate x7, local copies, waits for them, and re-layouts, on_device(): block = own if k == 0 else jnp.concatenate(blocks[k])  5.45 us
  transfers between devices with their start and end apart: 35, of which 11 were waited for; matrix products, arithmetic and copies ran while one was open for 28% of the time, Pallas kernels for 0%

profile of v1, /device:TPU:6, one launch (start us, length us, event | category | flops | bytes accessed | tf_op | source)
XLA Modules:
  0.0 252.6 jit_solution(16338869864332433511)
XLA Ops:
  6.3 2.5 dynamic-slice_bitcast_fusion.3
  8.8 5.3 %collective-permute-start.2 = (bf16[64,4096]{1,0:T(8,128)(2,1)}, bf16[64,4096]{1,0:T(8,128)(2,1)}, u32[]{:S(2)}, u32[]{:S(2)}) collective-permute-start(bf16[64,4096]{1,0:T(8,128)(2,1)} %get-tuple-element.21), channel_id=1, source_target_pairs={{16,0},{32,16},{48,32},{64,48},{80,64},{96,80},{112,96},{128,112},... | collective-permute-start | bytes 1572872 | tf_op jit(solution)/shard_map/ppermute | solution.py:29
  15.1 1.9 collective-permute-start.3
  18.2 2.0 collective-permute-start.5
  22.2 8.5 %all-to-all-start = ((bf16[8,128,512]{2,1,0:T(8,128)(2,1)}), bf16[8,128,512]{2,1,0:T(8,128)(2,1)}, u32[]{:S(2)}, u32[]{:S(2)}) async-start(bf16[8,128,512]{2,1,0:T(8,128)(2,1)} %bitcast.51), calls=%async_computation | async-start | bytes 2097152 | tf_op jit(solution)/shard_map/all_to_all | solution.py:68
  32.9 2.6 %fusion.17 = f32[128,256]{1,0:T(8,128)S(1)} fusion(bf16[256,4096]{1,0:T(8,128)(2,1)} %bitcast.194, bf16[1,128,4096]{2,1,0:T(8,128)(2,1)S(1)} %copy-done.1), kind=kOutput, calls=%fused_computation.45 | convolution fusion | flops 268435456 | bytes 3276800 | tf_op jit(solution)/shard_map/dot_general | solution.py:15
  36.6 6.9 %collective-permute-start.4 = (bf16[64,4096]{1,0:T(8,128)(2,1)}, bf16[64,4096]{1,0:T(8,128)(2,1)}, u32[]{:S(2)}, u32[]{:S(2)}) collective-permute-start(bf16[64,4096]{1,0:T(8,128)(2,1)} %get-tuple-element.20), channel_id=1, source_target_pairs={{16,0},{32,16},{48,32},{64,48},{80,64},{96,80},{112,96},{128,112},... | collective-permute-start | bytes 1572872 | tf_op jit(solution)/shard_map/ppermute | solution.py:29
  46.8 1.5 fusion.116
  51.2 1.8 convolution_bitcast_fusion.1
  53.0 3.2 %collective-permute-done.4 = bf16[64,4096]{1,0:T(8,128)(2,1)} collective-permute-done((bf16[64,4096]{1,0:T(8,128)(2,1)}, bf16[64,4096]{1,0:T(8,128)(2,1)}, u32[]{:S(2)}, u32[]{:S(2)}) %collective-permute-start.4) | collective-permute-done | bytes 524320 | tf_op jit(solution)/shard_map/ppermute | solution.py:29
  56.2 1.8 convolution_bitcast_fusion.2
  59.4 26.3 %all-gather = bf16[1152,128]{1,0:T(8,128)(2,1)S(1)} all-gather(bf16[144,128]{1,0:T(8,128)(2,1)S(1)} %copy.95), channel_id=2, replica_groups={{0,2,4,6,8,10,12,14},{1,3,5,7,9,11,13,15},{16,18,20,22,24,26,28,30},{17..., dimensions={0}, use_global_device_ids=true | all-gather | bytes 331776 | tf_op jit(solution)/shard_map/all_gather | solution.py:121
  88.6 2.1 fusion.84
  91.7 2.2 collective-permute-start.8
  95.4 1.5 fusion.1
  102.9 6.6 %collective-permute-done.8 = bf16[64,4096]{1,0:T(8,128)(2,1)} collective-permute-done((bf16[64,4096]{1,0:T(8,128)(2,1)}, bf16[64,4096]{1,0:T(8,128)(2,1)}, u32[]{:S(2)}, u32[]{:S(2)}) %collective-permute-start.8) | collective-permute-done | bytes 524320 | tf_op jit(solution)/shard_map/ppermute | solution.py:20
  111.1 10.8 %collective-permute-done.11 = bf16[64,4096]{1,0:T(8,128)(2,1)S(1)} collective-permute-done((bf16[64,4096]{1,0:T(8,128)(2,1)}, bf16[64,4096]{1,0:T(8,128)(2,1)S(1)}, u32[]{:S(2)}, u32[]{:S(2)}) %collective-permute-start.11) | collective-permute-done | bytes 524320 | tf_op jit(solution)/shard_map/ppermute | solution.py:20
  122.4 1.6 collective-permute-start.13
  124.0 3.7 %collective-permute-start.14 = (bf16[64,4096]{1,0:T(8,128)(2,1)}, bf16[64,4096]{1,0:T(8,128)(2,1)}, u32[]{:S(2)}, u32[]{:S(2)}) collective-permute-start(bf16[64,4096]{1,0:T(8,128)(2,1)} %collective-permute-done.8), channel_id=1, source_target_pairs={{0,2},{1,3},{2,4},{3,5},{4,6},{5,7},{6,8},{7,9},{8,10},{9,11},{10,... | collective-permute-start | bytes 1572872 | tf_op jit(solution)/shard_map/ppermute | solution.py:20
  128.4 4.8 %collective-permute-done.13 = bf16[64,4096]{1,0:T(8,128)(2,1)} collective-permute-done((bf16[64,4096]{1,0:T(8,128)(2,1)}, bf16[64,4096]{1,0:T(8,128)(2,1)}, u32[]{:S(2)}, u32[]{:S(2)}) %collective-permute-start.13) | collective-permute-done | bytes 524320 | tf_op jit(solution)/shard_map/ppermute | solution.py:20
  134.3 8.4 %collective-permute-done.14 = bf16[64,4096]{1,0:T(8,128)(2,1)} collective-permute-done((bf16[64,4096]{1,0:T(8,128)(2,1)}, bf16[64,4096]{1,0:T(8,128)(2,1)}, u32[]{:S(2)}, u32[]{:S(2)}) %collective-permute-start.14) | collective-permute-done | bytes 524320 | tf_op jit(solution)/shard_map/ppermute | solution.py:20
  145.3 7.7 %collective-permute-done.17 = bf16[64,4096]{1,0:T(8,128)(2,1)} collective-permute-done((bf16[64,4096]{1,0:T(8,128)(2,1)S(1)}, bf16[64,4096]{1,0:T(8,128)(2,1)}, u32[]{:S(2)}, u32[]{:S(2)}) %collective-permute-start.17) | collective-permute-done | bytes 524320 | tf_op jit(solution)/shard_map/ppermute | solution.py:20
  155.1 1.8 collective-permute-start.22
  158.1 2.0 collective-permute-start.19
  160.5 1.9 fusion.2
  162.4 3.6 %collective-permute-done.22 = bf16[64,4096]{1,0:T(8,128)(2,1)} collective-permute-done((bf16[64,4096]{1,0:T(8,128)(2,1)}, bf16[64,4096]{1,0:T(8,128)(2,1)}, u32[]{:S(2)}, u32[]{:S(2)}) %collective-permute-start.22) | collective-permute-done | bytes 524320 | tf_op jit(solution)/shard_map/ppermute | solution.py:20
  167.0 6.7 %collective-permute-done.23 = bf16[64,4096]{1,0:T(8,128)(2,1)} collective-permute-done((bf16[64,4096]{1,0:T(8,128)(2,1)}, bf16[64,4096]{1,0:T(8,128)(2,1)}, u32[]{:S(2)}, u32[]{:S(2)}) %collective-permute-start.23) | collective-permute-done | bytes 524320 | tf_op jit(solution)/shard_map/ppermute | solution.py:20
  176.6 2.1 convolution_convert_fusion.12
  178.7 3.7 %collective-permute-start.9 = (bf16[128,512]{1,0:T(8,128)(2,1)S(1)}, bf16[128,512]{1,0:T(8,128)(2,1)S(1)}, u32[]{:S(2)}, u32[]{:S(2)}) collective-permute-start(bf16[128,512]{1,0:T(8,128)(2,1)S(1)} %pad_maximum_fusion.2), channel_id=1, source_target_pairs={{0,14},{1,15},{2,0},{3,1},{4,2},{5,3},{6,4},{7,5},{8,6},{9,7},{10,... | collective-permute-start | bytes 393224 | tf_op jit(solution)/shard_map/ppermute | solution.py:20
  182.4 2.0 convolution_convert_fusion.10
  184.8 2.0 convolution_convert_fusion.8
  186.9 2.0 convolution_convert_fusion.6
  189.0 1.6 collective-permute-start.15
  191.7 1.5 collective-permute-start.18
  194.7 2.1 convolution_convert_fusion.4
  198.0 2.2 convolution_convert_fusion.2
  200.2 2.0 fusion.12
  202.3 2.7 %collective-permute-start.21 = (bf16[128,512]{1,0:T(8,128)(2,1)S(1)}, bf16[128,512]{1,0:T(8,128)(2,1)S(1)}, u32[]{:S(2)}, u32[]{:S(2)}) collective-permute-start(bf16[128,512]{1,0:T(8,128)(2,1)S(1)} %pad_maximum_fusion.6), channel_id=1, source_target_pairs={{0,10},{1,11},{2,12},{3,13},{4,14},{5,15},{6,0},{7,1},{8,2},{9,3},... | collective-permute-start | bytes 393224 | tf_op jit(solution)/shard_map/ppermute | solution.py:20
  206.4 3.1 %collective-permute-start.25 = (bf16[64,4096]{1,0:T(8,128)(2,1)}, bf16[64,4096]{1,0:T(8,128)(2,1)S(1)}, u32[]{:S(2)}, u32[]{:S(2)}) collective-permute-start(bf16[64,4096]{1,0:T(8,128)(2,1)} %collective-permute-done.19), channel_id=1, source_target_pairs={{0,2},{1,3},{2,4},{3,5},{4,6},{5,7},{6,8},{7,9},{8,10},{9,11},{10,... | collective-permute-start | bytes 1572872 | tf_op jit(solution)/shard_map/ppermute | solution.py:20
  209.6 2.8 %collective-permute-start.26 = (bf16[64,4096]{1,0:T(8,128)(2,1)}, bf16[64,4096]{1,0:T(8,128)(2,1)S(1)}, u32[]{:S(2)}, u32[]{:S(2)}) collective-permute-start(bf16[64,4096]{1,0:T(8,128)(2,1)} %collective-permute-done.23), channel_id=1, source_target_pairs={{0,14},{1,15},{2,0},{3,1},{4,2},{5,3},{6,4},{7,5},{8,6},{9,7},{10,... | collective-permute-start | bytes 1572872 | tf_op jit(solution)/shard_map/ppermute | solution.py:20
  212.4 1.9 collective-permute-start.32
  214.4 7.3 %collective-permute-start.33 = (f32[64,256]{1,0:T(8,128)S(1)}, f32[64,256]{1,0:T(8,128)S(1)}, u32[]{:S(2)}, u32[]{:S(2)}) collective-permute-start(f32[64,256]{1,0:T(8,128)S(1)} %get-tuple-element.26), channel_id=1, source_target_pairs={{16,0},{32,16},{48,32},{64,48},{80,64},{96,80},{112,96},{128,112},... | collective-permute-start | bytes 196616 | tf_op jit(solution)/shard_map/ppermute | solution.py:29
  224.0 2.0 convolution_convert_fusion
  226.1 1.6 collective-permute-start.27
  227.7 8.7 %collective-permute-done.27 = bf16[128,512]{1,0:T(8,128)(2,1)S(1)} collective-permute-done((bf16[128,512]{1,0:T(8,128)(2,1)S(1)}, bf16[128,512]{1,0:T(8,128)(2,1)S(1)}, u32[]{:S(2)}, u32[]{:S(2)}) %collective-permute-start.27) | collective-permute-done | bytes 131104 | tf_op jit(solution)/shard_map/ppermute | solution.py:20
  236.6 1.9 collective-permute-start.29
  238.5 11.2 %collective-permute-start.30 = (f32[64,256]{1,0:T(8,128)S(1)}, f32[64,256]{1,0:T(8,128)S(1)}, u32[]{:S(2)}, u32[]{:S(2)}) collective-permute-start(f32[64,256]{1,0:T(8,128)S(1)} %get-tuple-element.28), channel_id=1, source_target_pairs={{16,0},{32,16},{48,32},{64,48},{80,64},{96,80},{112,96},{128,112},... | collective-permute-start | bytes 196616 | tf_op jit(solution)/shard_map/ppermute | solution.py:29
  249.9 1.8 collective-permute-done.30
  (199 shorter events, 50.5 us)
Async XLA Ops:
  0.6 13.5 %copy-start.19 = (bf16[1,128,4096]{2,1,0:T(8,128)(2,1)S(1)}, bf16[1,128,4096]{2,1,0:T(8,128)(2,1)}, u32[]{:S(2)}) copy-start(bf16[1,128,4096]{2,1,0:T(8,128)(2,1)} %param.9) | copy-start | bytes 3145732
  6.3 10.8 %copy-start.2 = (bf16[1,4,64,4096]{3,2,1,0:T(8,128)(2,1)S(1)}, bf16[1,4,64,4096]{3,2,1,0:T(8,128)(2,1)}, u32[]{:S(2)}) copy-start(bf16[1,4,64,4096]{3,2,1,0:T(8,128)(2,1)} %param.14) | copy-start | bytes 6291460
  8.8 11.5 %copy-start.1 = (bf16[1,128,4096]{2,1,0:T(8,128)(2,1)S(1)}, bf16[1,128,4096]{2,1,0:T(8,128)(2,1)}, u32[]{:S(2)}) copy-start(bf16[1,128,4096]{2,1,0:T(8,128)(2,1)} %param.15) | copy-start | bytes 3145732
  8.8 38.0 %collective-permute-start.2 = (bf16[64,4096]{1,0:T(8,128)(2,1)}, bf16[64,4096]{1,0:T(8,128)(2,1)}, u32[]{:S(2)}, u32[]{:S(2)}) collective-permute-start(bf16[64,4096]{1,0:T(8,128)(2,1)} %get-tuple-element.21), channel_id=1, source_target_pairs={{16,0},{32,16},{48,32},{64,48},{80,64},{96,80},{112,96},{128,112},... | collective-permute-start | bytes 1572872 | tf_op jit(solution)/shard_map/ppermute | solution.py:29
  15.1 21.5 %collective-permute-start = (bf16[64,4096]{1,0:T(8,128)(2,1)}, bf16[64,4096]{1,0:T(8,128)(2,1)}, u32[]{:S(2)}, u32[]{:S(2)}) collective-permute-start(bf16[64,4096]{1,0:T(8,128)(2,1)} %get-tuple-element.24), channel_id=1, source_target_pairs={{0,16},{16,32},{32,48},{48,64},{64,80},{80,96},{96,112},{112,128},... | collective-permute-start | bytes 1572872 | tf_op jit(solution)/shard_map/ppermute | solution.py:51
  15.1 29.5 %collective-permute-start.1 = (bf16[64,4096]{1,0:T(8,128)(2,1)}, bf16[64,4096]{1,0:T(8,128)(2,1)}, u32[]{:S(2)}, u32[]{:S(2)}) collective-permute-start(bf16[64,4096]{1,0:T(8,128)(2,1)} %get-tuple-element.23), channel_id=1, source_target_pairs={{0,16},{16,32},{32,48},{48,64},{64,80},{80,96},{96,112},{112,128},... | collective-permute-start | bytes 1572872 | tf_op jit(solution)/shard_map/ppermute | solution.py:52
  15.1 33.1 %collective-permute-start.3 = (bf16[64,4096]{1,0:T(8,128)(2,1)}, bf16[64,4096]{1,0:T(8,128)(2,1)}, u32[]{:S(2)}, u32[]{:S(2)}) collective-permute-start(bf16[64,4096]{1,0:T(8,128)(2,1)} %get-tuple-element.22), channel_id=1, source_target_pairs={{0,16},{16,32},{32,48},{48,64},{64,80},{80,96},{96,112},{112,128},... | collective-permute-start | bytes 1572872 | tf_op jit(solution)/shard_map/ppermute | solution.py:29
  18.2 33.0 %collective-permute-start.5 = (bf16[64,4096]{1,0:T(8,128)(2,1)}, bf16[64,4096]{1,0:T(8,128)(2,1)}, u32[]{:S(2)}, u32[]{:S(2)}) collective-permute-start(bf16[64,4096]{1,0:T(8,128)(2,1)} %get-tuple-element.19), channel_id=1, source_target_pairs={{0,16},{16,32},{32,48},{48,64},{64,80},{80,96},{96,112},{112,128},... | collective-permute-start | bytes 1572872 | tf_op jit(solution)/shard_map/ppermute | solution.py:29
  22.2 138.1 %all-to-all-start = ((bf16[8,128,512]{2,1,0:T(8,128)(2,1)}), bf16[8,128,512]{2,1,0:T(8,128)(2,1)}, u32[]{:S(2)}, u32[]{:S(2)}) async-start(bf16[8,128,512]{2,1,0:T(8,128)(2,1)} %bitcast.51), calls=%async_computation | async-start | bytes 2097152 | tf_op jit(solution)/shard_map/all_to_all | solution.py:68
  32.9 11.8 %copy-start = (bf16[1,4096,256]{2,1,0:T(8,128)(2,1)S(1)}, bf16[1,4096,256]{2,1,0:T(8,128)(2,1)}, u32[]{:S(2)}) copy-start(bf16[1,4096,256]{2,1,0:T(8,128)(2,1)} %param.12) | copy-start | bytes 6291460
  32.9 12.9 %copy-start.11 = (bf16[1,4,64,4096]{3,2,1,0:T(8,128)(2,1)S(1)}, bf16[1,4,64,4096]{3,2,1,0:T(8,128)(2,1)}, u32[]{:S(2)}) copy-start(bf16[1,4,64,4096]{3,2,1,0:T(8,128)(2,1)} %param.13) | copy-start | bytes 6291460
  36.6 19.6 %collective-permute-start.4 = (bf16[64,4096]{1,0:T(8,128)(2,1)}, bf16[64,4096]{1,0:T(8,128)(2,1)}, u32[]{:S(2)}, u32[]{:S(2)}) collective-permute-start(bf16[64,4096]{1,0:T(8,128)(2,1)} %get-tuple-element.20), channel_id=1, source_target_pairs={{16,0},{32,16},{48,32},{64,48},{80,64},{96,80},{112,96},{128,112},... | collective-permute-start | bytes 1572872 | tf_op jit(solution)/shard_map/ppermute | solution.py:29
  44.7 131.9 %collective-permute-start.6 = (bf16[4096,256]{1,0:T(8,128)(2,1)S(1)}, bf16[4096,256]{1,0:T(8,128)(2,1)}, u32[]{:S(2)}, u32[]{:S(2)}) collective-permute-start(bf16[4096,256]{1,0:T(8,128)(2,1)S(1)} %bitcast.193), channel_id=1, source_target_pairs={{0,1},{1,0},{2,3},{3,2},{4,5},{5,4},{6,7},{7,6},{8,9},{9,8},{10,11... | collective-permute-start | bytes 6291464 | tf_op jit(solution)/shard_map/ppermute | solution.py:24
  91.0 10.9 %collective-permute-start.7 = (bf16[64,4096]{1,0:T(8,128)(2,1)}, bf16[64,4096]{1,0:T(8,128)(2,1)}, u32[]{:S(2)}, u32[]{:S(2)}) collective-permute-start(bf16[64,4096]{1,0:T(8,128)(2,1)} %collective-permute-done), channel_id=1, source_target_pairs={{0,2},{1,3},{2,4},{3,5},{4,6},{5,7},{6,8},{7,9},{8,10},{9,11},{10,... | collective-permute-start | bytes 1572872 | tf_op jit(solution)/shard_map/ppermute | solution.py:20
  91.7 17.8 %collective-permute-start.8 = (bf16[64,4096]{1,0:T(8,128)(2,1)}, bf16[64,4096]{1,0:T(8,128)(2,1)}, u32[]{:S(2)}, u32[]{:S(2)}) collective-permute-start(bf16[64,4096]{1,0:T(8,128)(2,1)} %collective-permute-done.1), channel_id=1, source_target_pairs={{0,2},{1,3},{2,4},{3,5},{4,6},{5,7},{6,8},{7,9},{8,10},{9,11},{10,... | collective-permute-start | bytes 1572872 | tf_op jit(solution)/shard_map/ppermute | solution.py:20
  99.3 11.7 %collective-permute-start.10 = (bf16[64,4096]{1,0:T(8,128)(2,1)}, bf16[64,4096]{1,0:T(8,128)(2,1)S(1)}, u32[]{:S(2)}, u32[]{:S(2)}) collective-permute-start(bf16[64,4096]{1,0:T(8,128)(2,1)} %collective-permute-done), channel_id=1, source_target_pairs={{0,14},{1,15},{2,0},{3,1},{4,2},{5,3},{6,4},{7,5},{8,6},{9,7},{10,... | collective-permute-start | bytes 1572872 | tf_op jit(solution)/shard_map/ppermute | solution.py:20
  100.4 21.5 %collective-permute-start.11 = (bf16[64,4096]{1,0:T(8,128)(2,1)}, bf16[64,4096]{1,0:T(8,128)(2,1)S(1)}, u32[]{:S(2)}, u32[]{:S(2)}) collective-permute-start(bf16[64,4096]{1,0:T(8,128)(2,1)} %collective-permute-done.1), channel_id=1, source_target_pairs={{0,14},{1,15},{2,0},{3,1},{4,2},{5,3},{6,4},{7,5},{8,6},{9,7},{10,... | collective-permute-start | bytes 1572872 | tf_op jit(solution)/shard_map/ppermute | solution.py:20
  110.6 17.1 %copy-start.9 = (bf16[128,4096]{1,0:T(8,128)(2,1)}, bf16[128,4096]{1,0:T(8,128)(2,1)S(1)}, u32[]{:S(2)}) copy-start(bf16[128,4096]{1,0:T(8,128)(2,1)S(1)} %constant_dynamic-update-slice_fusion.2) | copy-start | bytes 3145732
  111.1 16.6 %copy-start.15 = (bf16[8,128,384]{1,2,0:T(8,128)(2,1)S(1)}, bf16[8,128,384]{1,2,0:T(8,128)(2,1)}, u32[]{:S(2)}) copy-start(bf16[8,128,384]{1,2,0:T(8,128)(2,1)} %copy-done.14) | copy-start | bytes 2359300
  111.1 16.5 %copy-start.16 = (f32[384,512]{1,0:T(8,128)S(1)}, f32[384,512]{1,0:T(8,128)}, u32[]{:S(2)}) copy-start(f32[384,512]{1,0:T(8,128)} %fusion.34) | copy-start | bytes 2359300
  122.4 10.8 %collective-permute-start.13 = (bf16[64,4096]{1,0:T(8,128)(2,1)}, bf16[64,4096]{1,0:T(8,128)(2,1)}, u32[]{:S(2)}, u32[]{:S(2)}) collective-permute-start(bf16[64,4096]{1,0:T(8,128)(2,1)} %collective-permute-done.7), channel_id=1, source_target_pairs={{0,2},{1,3},{2,4},{3,5},{4,6},{5,7},{6,8},{7,9},{8,10},{9,11},{10,... | collective-permute-start | bytes 1572872 | tf_op jit(solution)/shard_map/ppermute | solution.py:20
  124.0 18.7 %collective-permute-start.14 = (bf16[64,4096]{1,0:T(8,128)(2,1)}, bf16[64,4096]{1,0:T(8,128)(2,1)}, u32[]{:S(2)}, u32[]{:S(2)}) collective-permute-start(bf16[64,4096]{1,0:T(8,128)(2,1)} %collective-permute-done.8), channel_id=1, source_target_pairs={{0,2},{1,3},{2,4},{3,5},{4,6},{5,7},{6,8},{7,9},{8,10},{9,11},{10,... | collective-permute-start | bytes 1572872 | tf_op jit(solution)/shard_map/ppermute | solution.py:20
  128.2 16.1 %collective-permute-start.16 = (bf16[64,4096]{1,0:T(8,128)(2,1)S(1)}, bf16[64,4096]{1,0:T(8,128)(2,1)}, u32[]{:S(2)}, u32[]{:S(2)}) collective-permute-start(bf16[64,4096]{1,0:T(8,128)(2,1)S(1)} %collective-permute-done.10), channel_id=1, source_target_pairs={{0,14},{1,15},{2,0},{3,1},{4,2},{5,3},{6,4},{7,5},{8,6},{9,7},{10,... | collective-permute-start | bytes 1572872 | tf_op jit(solution)/shard_map/ppermute | solution.py:20
  128.3 24.7 %collective-permute-start.17 = (bf16[64,4096]{1,0:T(8,128)(2,1)S(1)}, bf16[64,4096]{1,0:T(8,128)(2,1)}, u32[]{:S(2)}, u32[]{:S(2)}) collective-permute-start(bf16[64,4096]{1,0:T(8,128)(2,1)S(1)} %collective-permute-done.11), channel_id=1, source_target_pairs={{0,14},{1,15},{2,0},{3,1},{4,2},{5,3},{6,4},{7,5},{8,6},{9,7},{10,... | collective-permute-start | bytes 1572872 | tf_op jit(solution)/shard_map/ppermute | solution.py:20
  143.8 13.1 %copy-start.5 = (bf16[128,4096]{1,0:T(8,128)(2,1)}, bf16[128,4096]{1,0:T(8,128)(2,1)S(1)}, u32[]{:S(2)}) copy-start(bf16[128,4096]{1,0:T(8,128)(2,1)S(1)} %constant_dynamic-update-slice_fusion.6) | copy-start | bytes 3145732
  155.1 10.9 %collective-permute-start.22 = (bf16[64,4096]{1,0:T(8,128)(2,1)}, bf16[64,4096]{1,0:T(8,128)(2,1)}, u32[]{:S(2)}, u32[]{:S(2)}) collective-permute-start(bf16[64,4096]{1,0:T(8,128)(2,1)} %collective-permute-done.16), channel_id=1, source_target_pairs={{0,14},{1,15},{2,0},{3,1},{4,2},{5,3},{6,4},{7,5},{8,6},{9,7},{10,... | collective-permute-start | bytes 1572872 | tf_op jit(solution)/shard_map/ppermute | solution.py:20
  158.0 15.7 %collective-permute-start.23 = (bf16[64,4096]{1,0:T(8,128)(2,1)}, bf16[64,4096]{1,0:T(8,128)(2,1)}, u32[]{:S(2)}, u32[]{:S(2)}) collective-permute-start(bf16[64,4096]{1,0:T(8,128)(2,1)} %collective-permute-done.17), channel_id=1, source_target_pairs={{0,14},{1,15},{2,0},{3,1},{4,2},{5,3},{6,4},{7,5},{8,6},{9,7},{10,... | collective-permute-start | bytes 1572872 | tf_op jit(solution)/shard_map/ppermute | solution.py:20
  158.1 30.9 %collective-permute-start.19 = (bf16[64,4096]{1,0:T(8,128)(2,1)}, bf16[64,4096]{1,0:T(8,128)(2,1)}, u32[]{:S(2)}, u32[]{:S(2)}) collective-permute-start(bf16[64,4096]{1,0:T(8,128)(2,1)} %collective-permute-done.13), channel_id=1, source_target_pairs={{0,2},{1,3},{2,4},{3,5},{4,6},{5,7},{6,8},{7,9},{8,10},{9,11},{10,... | collective-permute-start | bytes 1572872 | tf_op jit(solution)/shard_map/ppermute | solution.py:20
  160.1 31.6 %collective-permute-start.20 = (bf16[64,4096]{1,0:T(8,128)(2,1)}, bf16[64,4096]{1,0:T(8,128)(2,1)}, u32[]{:S(2)}, u32[]{:S(2)}) collective-permute-start(bf16[64,4096]{1,0:T(8,128)(2,1)} %collective-permute-done.14), channel_id=1, source_target_pairs={{0,2},{1,3},{2,4},{3,5},{4,6},{5,7},{6,8},{7,9},{8,10},{9,11},{10,... | collective-permute-start | bytes 1572872 | tf_op jit(solution)/shard_map/ppermute | solution.py:20
  166.0 36.3 %collective-permute-start.31 = (f32[384,256]{1,0:T(8,128)S(1)}, f32[384,256]{1,0:T(8,128)S(1)}, u32[]{:S(2)}, u32[]{:S(2)}) collective-permute-start(f32[384,256]{1,0:T(8,128)S(1)} %constant_dynamic-slice_fusion), channel_id=1, source_target_pairs={{0,1},{1,0},{2,3},{3,2},{4,5},{5,4},{6,7},{7,6},{8,9},{9,8},{10,11... | collective-permute-start | bytes 1179656 | tf_op jit(solution)/shard_map/ppermute | solution.py:24
  178.7 26.4 %collective-permute-start.9 = (bf16[128,512]{1,0:T(8,128)(2,1)S(1)}, bf16[128,512]{1,0:T(8,128)(2,1)S(1)}, u32[]{:S(2)}, u32[]{:S(2)}) collective-permute-start(bf16[128,512]{1,0:T(8,128)(2,1)S(1)} %pad_maximum_fusion.2), channel_id=1, source_target_pairs={{0,14},{1,15},{2,0},{3,1},{4,2},{5,3},{6,4},{7,5},{8,6},{9,7},{10,... | collective-permute-start | bytes 393224 | tf_op jit(solution)/shard_map/ppermute | solution.py:20
  184.5 21.9 %collective-permute-start.12 = (bf16[128,512]{1,0:T(8,128)(2,1)S(1)}, bf16[128,512]{1,0:T(8,128)(2,1)S(1)}, u32[]{:S(2)}, u32[]{:S(2)}) collective-permute-start(bf16[128,512]{1,0:T(8,128)(2,1)S(1)} %pad_maximum_fusion.3), channel_id=1, source_target_pairs={{0,2},{1,3},{2,4},{3,5},{4,6},{5,7},{6,8},{7,9},{8,10},{9,11},{10,... | collective-permute-start | bytes 393224 | tf_op jit(solution)/shard_map/ppermute | solution.py:20
  189.0 20.6 %collective-permute-start.15 = (bf16[128,512]{1,0:T(8,128)(2,1)S(1)}, bf16[128,512]{1,0:T(8,128)(2,1)S(1)}, u32[]{:S(2)}, u32[]{:S(2)}) collective-permute-start(bf16[128,512]{1,0:T(8,128)(2,1)S(1)} %pad_maximum_fusion.4), channel_id=1, source_target_pairs={{0,12},{1,13},{2,14},{3,15},{4,0},{5,1},{6,2},{7,3},{8,4},{9,5},{1... | collective-permute-start | bytes 393224 | tf_op jit(solution)/shard_map/ppermute | solution.py:20
  191.7 20.7 %collective-permute-start.18 = (bf16[128,512]{1,0:T(8,128)(2,1)S(1)}, bf16[128,512]{1,0:T(8,128)(2,1)S(1)}, u32[]{:S(2)}, u32[]{:S(2)}) collective-permute-start(bf16[128,512]{1,0:T(8,128)(2,1)S(1)} %pad_maximum_fusion.5), channel_id=1, source_target_pairs={{0,4},{1,5},{2,6},{3,7},{4,8},{5,9},{6,10},{7,11},{8,12},{9,13},{1... | collective-permute-start | bytes 393224 | tf_op jit(solution)/shard_map/ppermute | solution.py:20
  202.3 12.1 %collective-permute-start.21 = (bf16[128,512]{1,0:T(8,128)(2,1)S(1)}, bf16[128,512]{1,0:T(8,128)(2,1)S(1)}, u32[]{:S(2)}, u32[]{:S(2)}) collective-permute-start(bf16[128,512]{1,0:T(8,128)(2,1)S(1)} %pad_maximum_fusion.6), channel_id=1, source_target_pairs={{0,10},{1,11},{2,12},{3,13},{4,14},{5,15},{6,0},{7,1},{8,2},{9,3},... | collective-permute-start | bytes 393224 | tf_op jit(solution)/shard_map/ppermute | solution.py:20
  205.1 17.1 %copy-start.18 = (f32[384,256]{1,0:T(8,128)}, f32[384,256]{1,0:T(8,128)S(1)}, u32[]{:S(2)}) copy-start(f32[384,256]{1,0:T(8,128)S(1)} %dynamic-slice_add_fusion) | copy-start | bytes 1179652
  205.1 16.6 %collective-permute-start.24 = (bf16[128,512]{1,0:T(8,128)(2,1)S(1)}, bf16[128,512]{1,0:T(8,128)(2,1)S(1)}, u32[]{:S(2)}, u32[]{:S(2)}) collective-permute-start(bf16[128,512]{1,0:T(8,128)(2,1)S(1)} %pad_maximum_fusion.7), channel_id=1, source_target_pairs={{0,6},{1,7},{2,8},{3,9},{4,10},{5,11},{6,12},{7,13},{8,14},{9,15},... | collective-permute-start | bytes 393224 | tf_op jit(solution)/shard_map/ppermute | solution.py:20
  206.4 15.7 %collective-permute-start.25 = (bf16[64,4096]{1,0:T(8,128)(2,1)}, bf16[64,4096]{1,0:T(8,128)(2,1)S(1)}, u32[]{:S(2)}, u32[]{:S(2)}) collective-permute-start(bf16[64,4096]{1,0:T(8,128)(2,1)} %collective-permute-done.19), channel_id=1, source_target_pairs={{0,2},{1,3},{2,4},{3,5},{4,6},{5,7},{6,8},{7,9},{8,10},{9,11},{10,... | collective-permute-start | bytes 1572872 | tf_op jit(solution)/shard_map/ppermute | solution.py:20
  209.6 12.6 %collective-permute-start.26 = (bf16[64,4096]{1,0:T(8,128)(2,1)}, bf16[64,4096]{1,0:T(8,128)(2,1)S(1)}, u32[]{:S(2)}, u32[]{:S(2)}) collective-permute-start(bf16[64,4096]{1,0:T(8,128)(2,1)} %collective-permute-done.23), channel_id=1, source_target_pairs={{0,14},{1,15},{2,0},{3,1},{4,2},{5,3},{6,4},{7,5},{8,6},{9,7},{10,... | collective-permute-start | bytes 1572872 | tf_op jit(solution)/shard_map/ppermute | solution.py:20
  212.4 37.5 %collective-permute-start.32 = (f32[64,256]{1,0:T(8,128)S(1)}, f32[64,256]{1,0:T(8,128)S(1)}, u32[]{:S(2)}, u32[]{:S(2)}) collective-permute-start(f32[64,256]{1,0:T(8,128)S(1)} %get-tuple-element.25), channel_id=1, source_target_pairs={{0,16},{16,32},{32,48},{48,64},{64,80},{80,96},{96,112},{112,128},... | collective-permute-start | bytes 196616 | tf_op jit(solution)/shard_map/ppermute | solution.py:29
  214.4 35.5 %collective-permute-start.33 = (f32[64,256]{1,0:T(8,128)S(1)}, f32[64,256]{1,0:T(8,128)S(1)}, u32[]{:S(2)}, u32[]{:S(2)}) collective-permute-start(f32[64,256]{1,0:T(8,128)S(1)} %get-tuple-element.26), channel_id=1, source_target_pairs={{16,0},{32,16},{48,32},{64,48},{80,64},{96,80},{112,96},{128,112},... | collective-permute-start | bytes 196616 | tf_op jit(solution)/shard_map/ppermute | solution.py:29
  223.9 12.6 %collective-permute-start.28 = (f32[384,256]{1,0:T(8,128)S(1)}, f32[384,256]{1,0:T(8,128)S(1)}, u32[]{:S(2)}, u32[]{:S(2)}) collective-permute-start(f32[384,256]{1,0:T(8,128)S(1)} %constant_dynamic-slice_fusion.1), channel_id=1, source_target_pairs={{0,1},{1,0},{2,3},{3,2},{4,5},{5,4},{6,7},{7,6},{8,9},{9,8},{10,11... | collective-permute-start | bytes 1179656 | tf_op jit(solution)/shard_map/ppermute | solution.py:24
  226.0 25.6 %slice-start = ((f32[384,256]{1,0:T(8,128)}), f32[256,256]{1,0:T(8,128)S(1)}, s32[]{:S(2)}) async-start(f32[384,256]{1,0:T(8,128)} %copy-done.18), calls=%async_computation.1 | async-start | bytes 524288 | tf_op jit(solution)/shard_map/slice | solution.py:157
  226.0 25.6 %copy-start.24 = (pred[4]{0:T(512)(128)(4,1)S(1)}, pred[4]{0:T(512)(128)(4,1)}, u32[]{:S(2)}) copy-start(pred[4]{0:T(512)(128)(4,1)} %iota_compare_fusion.5) | copy-start | bytes 16
  226.1 25.6 %copy-start.25 = (pred[4]{0:T(512)(128)(4,1)S(1)}, pred[4]{0:T(512)(128)(4,1)}, u32[]{:S(2)}) copy-start(pred[4]{0:T(512)(128)(4,1)} %iota_compare_fusion.6) | copy-start | bytes 16
  226.1 10.4 %collective-permute-start.27 = (bf16[128,512]{1,0:T(8,128)(2,1)S(1)}, bf16[128,512]{1,0:T(8,128)(2,1)S(1)}, u32[]{:S(2)}, u32[]{:S(2)}) collective-permute-start(bf16[128,512]{1,0:T(8,128)(2,1)S(1)} %pad_maximum_fusion.8), channel_id=1, source_target_pairs={{0,8},{1,9},{2,10},{3,11},{4,12},{5,13},{6,14},{7,15},{8,0},{9,1},... | collective-permute-start | bytes 393224 | tf_op jit(solution)/shard_map/ppermute | solution.py:20
  236.6 13.3 %collective-permute-start.29 = (f32[64,256]{1,0:T(8,128)S(1)}, f32[64,256]{1,0:T(8,128)S(1)}, u32[]{:S(2)}, u32[]{:S(2)}) collective-permute-start(f32[64,256]{1,0:T(8,128)S(1)} %get-tuple-element.27), channel_id=1, source_target_pairs={{0,16},{16,32},{32,48},{48,64},{64,80},{80,96},{96,112},{112,128},... | collective-permute-start | bytes 196616 | tf_op jit(solution)/shard_map/ppermute | solution.py:29
  238.5 13.1 %collective-permute-start.30 = (f32[64,256]{1,0:T(8,128)S(1)}, f32[64,256]{1,0:T(8,128)S(1)}, u32[]{:S(2)}, u32[]{:S(2)}) collective-permute-start(f32[64,256]{1,0:T(8,128)S(1)} %get-tuple-element.28), channel_id=1, source_target_pairs={{16,0},{32,16},{48,32},{64,48},{80,64},{96,80},{112,96},{128,112},... | collective-permute-start | bytes 196616 | tf_op jit(solution)/shard_map/ppermute | solution.py:29
  (16 other events, 58.6 us)

commit v2 on v1

v2 whole, which is shorter than its diff:
```python
import functools

import jax
import jax.numpy as jnp
from jax import lax
from jax.experimental import pallas as pl
from jax.experimental.pallas import tpu as pltpu
from jax.sharding import PartitionSpec as P

RANK = 64
JOBS = 4
SIX = (JOBS + 2) * RANK
SCALE = 0.5
LINES = 2
PAD = 16
FEATURES = (((1,), (1,)), ((), ()))
BF16, F32, I32 = jnp.bfloat16, jnp.float32, jnp.int32


def dot32(a, b):
    return jnp.dot(a, b, preferred_element_type=F32)


def dot_features(a, b):
    return lax.dot_general(a, b, FEATURES, preferred_element_type=F32)


def along_z(value, by, depth):
    route = [(z * LINES + x, ((z + by) % depth) * LINES + x) for z in range(depth) for x in range(LINES)]
    return lax.ppermute(value, "dp", route)


def across_x(value, devices):
    return lax.ppermute(value, "dp", [(d, d ^ 1) for d in range(devices)])


def section_shift(value, by, sections):
    route = [(i, i + by) for i in range(sections) if 0 <= i + by < sections]
    return lax.ppermute(value, "section", route)


def hosted_slot(placement, section, code):
    plan = lax.dynamic_index_in_dim(placement, section, 0, keepdims=False)
    return jnp.sum(jnp.where(plan[:, 0] == code, plan[:, 1], 0))


def in_order(values, *others):
    return lax.optimization_barrier((tuple(values), others))[0]


def kernel_call(kernel, outs, scalars, arrays):
    vmem, smem = pl.BlockSpec(memory_space=pltpu.VMEM), pl.BlockSpec(memory_space=pltpu.SMEM)
    return pl.pallas_call(
        kernel,
        out_shape=tuple(jax.ShapeDtypeStruct(shape, dtype) for shape, dtype in outs),
        in_specs=[smem] * len(scalars) + [vmem] * len(arrays),
        out_specs=tuple(vmem for _ in outs),
        compiler_params=pltpu.CompilerParams(vmem_limit_bytes=40 * 2**20),
        cost_estimate=pl.CostEstimate(flops=1024, bytes_accessed=1024, transcendentals=0),
    )(*scalars, *arrays)


def split_kernel(cot_ref, out_ref):
    wide = out_ref.shape[2]
    for k in range(out_ref.shape[0]):
        out_ref[k] = cot_ref[:, k * wide : (k + 1) * wide]


def iota(shape, dim):
    return lax.broadcasted_iota(I32, shape, dim)


def rows_kernel(place, lengths, plan, xa, xb, cot, own_down, own_up, above, below, adapted, sent):
    rows, width = cot.shape
    first = place[2] * (2 * JOBS)
    which = []
    for j in range(JOBS):
        offset, slot = plan[first + 2 * j], plan[first + 2 * j + 1]
        which.append(jnp.where(offset == 1, slot, jnp.where(offset == 2, JOBS, JOBS + 1)))

    def adapter_of(position):
        found, end = jnp.full(position.shape, which[0], I32), 0
        for j in range(1, JOBS):
            end = end + lengths[j - 1]
            found = jnp.where(position >= end, which[j], found)
        return found

    chosen = adapter_of(iota((rows, SIX), 0)) == lax.shift_right_logical(iota((rows, SIX), 1), 6)
    x = jnp.concatenate([xa[...], xb[...]], axis=0)
    guest_down = jnp.concatenate([above[:RANK], below[:RANK]], axis=0)
    guest_up = jnp.concatenate([above[RANK:], below[RANK:]], axis=0)

    def all_six(v, own, guest):
        return jnp.concatenate([dot_features(v, own[...]), dot_features(v, guest)], axis=1)

    codes = jnp.where(chosen, all_six(x, own_down, guest_down), 0.0).astype(BF16)
    signals = jnp.where(chosen, SCALE * all_six(cot[...], own_up, guest_up), 0.0).astype(BF16)
    own = JOBS * RANK
    tile = width // 8
    for t in range(8):
        at = slice(t * tile, (t + 1) * tile)
        total = dot32(codes[:, :own], own_up[:, at]) + dot32(codes[:, own:], guest_up[:, at])
        adapted[:, at] = (SCALE * total).astype(BF16)
    rank, lane = iota((SIX, 2 * RANK), 0) & (RANK - 1), iota((SIX, 2 * RANK), 1)
    to_codes = (rank == lane).astype(F32).astype(BF16)
    to_signals = (rank + RANK == lane).astype(F32).astype(BF16)
    narrow = (dot32(codes, to_codes) + dot32(signals, to_signals)).astype(BF16)
    ids = adapter_of(iota((PAD, rows), 1)).astype(F32).astype(BF16)
    for k in range(sent.shape[0]):
        sent[k, :rows] = narrow
        sent[k, rows:] = ids


def base_kernel(groups, with_columns, place, *refs):
    blocks, (w_own, w_pair), outs = refs[: 2 * groups], refs[2 * groups : 2 * groups + 2], refs[2 * groups + 2 :]
    half, _ = blocks[0].shape
    rows, cols = 2 * half, w_own.shape[1]
    wide = LINES * cols
    lhs = jnp.concatenate([b[...] for b in blocks], axis=0)
    for w, first in ((w_own, 0), (w_pair, cols)):
        result = dot32(lhs, w[...]).astype(BF16)
        for i in range(groups):
            outs[i][:, first : first + cols] = result[i * rows : (i + 1) * rows]
    if with_columns:
        at = pl.multiple_of(place[0] * wide, wide)
        for i, b in enumerate(blocks):
            outs[groups][i // 2, (i % 2) * half : (i % 2 + 1) * half] = b[:, pl.ds(at, wide)]


def base(place, halves, w_own, w_pair, with_columns=True):
    groups = len(halves) // 2
    half, wide = halves[0].shape[0], LINES * w_own.shape[1]
    outs = [((2 * half, wide), BF16)] * groups
    if with_columns:
        outs = outs + [((groups, 2 * half, wide), BF16)]
    return kernel_call(
        functools.partial(base_kernel, groups, with_columns), outs, [place], [*halves, w_own, w_pair]
    )


def gradient_kernel(of_signals, order, place, line, *refs):
    blocks, (mine, theirs) = refs[:-2], refs[-2:]
    depth, rows = line.shape[0], line.shape[1] - PAD
    cols = mine.shape[1]
    pick = iota((SIX, 2 * RANK), 0) & (RANK - 1)
    pick = (pick + (RANK if of_signals else 0) == iota((SIX, 2 * RANK), 1)).astype(F32).astype(BF16)
    slot = lax.shift_right_logical(iota((SIX, rows), 0), 6)
    lhs = []
    for k in order:
        at = lax.rem(place[0] + (depth - k), depth) if of_signals else k
        spread = dot_features(pick, line[at, :rows])
        ids = line[at, rows : rows + PAD][:1].astype(F32).astype(I32)
        lhs.append(jnp.where(slot == ids, spread, 0.0).astype(BF16))
    values = jnp.concatenate([b[...].reshape(-1, b.shape[-1]) for b in blocks], axis=0)
    total = dot32(jnp.concatenate(lhs, axis=1), values)
    if not of_signals:
        total = SCALE * total
    first = place[1] == 0
    mine[...] = jnp.where(first, total[:, :cols], total[:, cols:])
    theirs[...] = jnp.where(first, total[:, cols:], total[:, :cols]).astype(BF16)


def gradient(of_signals, order, place, line, blocks):
    cols = blocks[0].shape[-1] // LINES
    return kernel_call(
        functools.partial(gradient_kernel, of_signals, order),
        [((SIX, cols), F32), ((SIX, cols), BF16)],
        [place],
        [line, *blocks],
    )


def finish_kernel(depth, cols, place, adapted, *refs):
    pieces, out = refs[:depth], refs[depth]
    z, x = place[0], place[1]
    for k in range(depth):
        for side, first in ((x, 0), (1 - x, cols)):
            at = pl.multiple_of((lax.rem(z + k, depth) * LINES + side) * cols, cols)
            total = pieces[k][:, first : first + cols].astype(F32) + adapted[:, pl.ds(at, cols)].astype(F32)
            out[:, pl.ds(at, cols)] = total.astype(BF16)


def on_device(handed, lengths, placement, frozen, down, up, cotangent):
    sections = lax.axis_size("section")
    devices = lax.axis_size("dp")
    depth = devices // LINES
    far = depth // 2
    s = lax.axis_index("section")
    d = lax.axis_index("dp")
    z, x = d // LINES, d % LINES
    place = jnp.stack([z, x, s]).astype(I32)
    lines = [[k * LINES + i for k in range(depth)] for i in range(LINES)]
    rows, width = handed.shape[1:]
    half = rows // 2
    cols = width // devices
    wide = width // depth
    cot = cotangent[0]

    behind = [(i, (i + 1) % sections) for i in range(sections)]
    xa = lax.ppermute(handed[0, :half], "section", behind)
    xb = lax.ppermute(handed[0, half:], "section", behind)

    def to_line(value):
        return lax.all_to_all(value, "dp", 0, 0, axis_index_groups=lines, tiled=True)

    cot_line = to_line(kernel_call(split_kernel, [((depth, rows, wide), BF16)], [], [cot])[0])

    slot_below = hosted_slot(placement, jnp.maximum(s - 1, 0), 2)
    slot_above = hosted_slot(placement, jnp.minimum(s + 1, sections - 1), 0)
    maps = lambda k: jnp.concatenate([lax.dynamic_index_in_dim(w[0], k, 0, keepdims=False) for w in (down, up)])
    from_above = section_shift(maps(slot_below), -1, sections)
    from_below = section_shift(maps(slot_above), 1, sections)
    own_down = down[0].reshape(JOBS * RANK, width)
    own_up = up[0].reshape(JOBS * RANK, width)

    w_own = frozen[0]
    w_pair = across_x(w_own, devices)

    step = lambda pair: (along_z(pair[0], 1, depth), along_z(pair[1], -1, depth))
    a1 = step((xa, xa))
    b1 = step((xb, xb))
    (xa_,) = in_order((xa,), *a1, cot_line)
    adapted, sent = kernel_call(
        rows_kernel,
        [((rows, width), BF16), ((depth, rows + PAD, 2 * RANK), BF16)],
        [place, lengths.reshape(-1), placement.reshape(-1)],
        [xa_, xb, cot, own_down, own_up, from_above, from_below],
    )
    line = to_line(sent)
    a2 = step(a1)
    b2 = step(b1)
    far_columns = along_z(
        lax.dynamic_slice_in_dim(jnp.concatenate([xa, xb]), ((z + far) % depth) * wide, wide, 1), far, depth
    )
    a3 = step(a2)
    (line_,) = in_order((line,), *b2)
    up_mine, up_theirs = gradient(False, tuple(range(depth)), place, line_, [cot_line])
    up_theirs = across_x(up_theirs, devices)
    b3 = step(b2)

    pieces = [None] * depth
    (xa_,) = in_order((xa,), *a3)
    pieces[0], near_f, near_b, near_columns = base(
        place, (xa_, xb, a1[0], b1[0], a1[1], b1[1]), w_own, w_pair
    )
    pieces[1], pieces[depth - 1] = along_z(near_f, -1, depth), along_z(near_b, 1, depth)
    last_a, last_b = along_z(a3[0], 1, depth), along_z(b3[1], -1, depth)

    f2, r2, f3, r3, next_columns = base(
        place, (a2[0], b2[0], a2[1], b2[1], a3[0], b3[0], a3[1], b3[1]), w_own, w_pair
    )
    pieces[2], pieces[depth - 2] = along_z(f2, -2, depth), along_z(r2, 2, depth)
    pieces[3], pieces[depth - 3] = along_z(f3, -3, depth), along_z(r3, 3, depth)
    order = (0, 1, depth - 1, 2, depth - 2, 3, depth - 3, far)
    down_mine, down_theirs = gradient(True, order, place, line, [near_columns, next_columns, far_columns])
    down_theirs = across_x(down_theirs, devices)

    last_a, last_b = in_order((last_a, last_b), down_mine, up_mine, near_columns, next_columns)
    (last,) = base(place, (last_a, last_b), w_own, w_pair, with_columns=False)
    pieces[far] = along_z(last, far, depth)

    def over_pair(mine, theirs):
        return (mine + theirs.astype(F32)).reshape(JOBS + 2, RANK, cols)

    up_total, down_total = over_pair(up_mine, up_theirs), over_pair(down_mine, down_theirs)
    guests = lambda job: jnp.stack([down_total[job], up_total[job]]).astype(BF16)
    of_below = section_shift(guests(JOBS), 1, sections).astype(F32)
    of_above = section_shift(guests(JOBS + 1), -1, sections).astype(F32)
    slots = jnp.arange(JOBS, dtype=I32)[:, None, None]

    def gathered(total, i):
        return (
            total[:JOBS]
            + jnp.where(slots == slot_below, of_below[i][None], 0.0)
            + jnp.where(slots == slot_above, of_above[i][None], 0.0)
        )[None]

    (passed,) = kernel_call(
        functools.partial(finish_kernel, depth, cols), [((rows, width), BF16)], [place], [adapted, *pieces]
    )
    return passed[None], gathered(down_total, 0), gathered(up_total, 1)


def solution(mesh):
    in_specs = (
        P("section", "dp", None),
        P("section", "dp", None),
        P(),
        P("section", None, "dp"),
        P("section", None, None, None),
        P("section", None, None, None),
        P("section", "dp", None),
    )
    out_specs = (
        P("section", "dp", None),
        P("section", None, None, "dp"),
        P("section", None, None, "dp"),
    )
    return jax.shard_map(on_device, mesh=mesh, in_specs=in_specs, out_specs=out_specs, check_vma=False)
```

time: 257 us -> 191 us (0.74); the launches traced: 253 us -> 190 us
  matrix products: 43.8 us -> 0 us
  blocking collectives: 26.3 us -> 0 us
  Pallas kernels: 0 us -> 19.9 us
  waiting for transfers between devices: 62.7 us -> 79.4 us
  starting transfers between devices: 80.6 us -> 67 us
  local copies, waits for them, and re-layouts: 25.3 us -> 15.9 us
  other arithmetic: 7.82 us -> 3.08 us
    dot_general x34 -> x0, matrix products: 43.8 us -> none  [dot32(): return lax.dot_general(a, b, dims, preferred_element_type=jnp.float32)]
    all_gather x1 -> x0, blocking collectives: 26.3 us -> none  [on_device(): line = lax.all_gather(sent, 'dp', axis_index_groups=lines)]
    ppermute x8 -> x4, starting transfers between devices: 38.5 us -> 12.2 us  [section_shift(): return lax.ppermute(value, 'section', route)]
    pallas_call x0 -> x8, Pallas kernels: none -> 19.9 us  [kernel_call(): pl.pallas_call(kernel, out_shape=tuple((jax.ShapeDtypeStruct(shape, dtype...]
    all_to_all x1 -> x2, waiting for transfers between devices: 0.01 us -> 7.57 us  [to_line(): lax.all_to_all(value, 'dp', 0, 0, axis_index_groups=lines, tiled=True)]
    concatenate x11 -> x0, local copies, waits for them, and re-layouts: 7.5 us -> none  [the longest x7 5.45 us: on_device(): block = own if k == 0 else jnp.concatenate(blocks[k])]
    ppermute x3, waiting for transfers between devices: 0.01 us -> 4.78 us  [across_x(): return lax.ppermute(value, 'dp', [(d, d ^ 1) for d in range(devices)])]
    ppermute x21 -> x22, waiting for transfers between devices: 57.7 us -> 62.4 us  [along_z(): return lax.ppermute(value, 'dp', route)]
  transfers between devices with their start and end apart: 35 -> 33, of which waited for: 11 -> 12; matrix products, arithmetic and copies ran while one was open for 28% -> 3% of each run, Pallas kernels for 0% -> 10%
where the time goes in v2:
time: 191 us; the launch traced here: 190 us
  waiting for transfers between devices  79.4 us (42%)
  starting transfers between devices  67 us (35%)
  Pallas kernels  19.9 us (10%)
  local copies, waits for them, and re-layouts  15.9 us (8%)
  between operations  4.35 us (2%)
  other arithmetic  3.08 us (2%)
    ppermute x22, waiting for transfers between devices, along_z(): return lax.ppermute(value, 'dp', route)  62.4 us
    ppermute x22, starting transfers between devices, along_z(): return lax.ppermute(value, 'dp', route)  37.6 us
    pallas_call x8, Pallas kernels, kernel_call(): pl.pallas_call(kernel, out_shape=tuple((jax.ShapeDtypeStruct(shape, dtype...  19.9 us
    all_to_all x2, starting transfers between devices, to_line(): lax.all_to_all(value, 'dp', 0, 0, axis_index_groups=lines, tiled=True)  13.1 us
    ppermute x4, starting transfers between devices, section_shift(): return lax.ppermute(value, 'section', route)  12.2 us
    unnamed x33, local copies, waits for them, and re-layouts  11.6 us
    all_to_all x2, waiting for transfers between devices, to_line(): lax.all_to_all(value, 'dp', 0, 0, axis_index_groups=lines, tiled=True)  7.57 us
    ppermute x3, waiting for transfers between devices, across_x(): return lax.ppermute(value, 'dp', [(d, d ^ 1) for d in range(devices)])  4.78 us
  transfers between devices with their start and end apart: 33, of which 12 were waited for; matrix products, arithmetic and copies ran while one was open for 3% of the time, Pallas kernels for 10%

profile of v2, /device:TPU:6, one launch (start us, length us, event | category | flops | bytes accessed | tf_op | source)
XLA Modules:
  0.0 189.7 jit_solution(13722673730210720767)
XLA Ops:
  0.6 2.4 %slice_bitcast_fusion = (bf16[64,4096]{1,0:T(8,128)(2,1)}, bf16[64,4096]{1,0:T(8,128)(2,1)}) fusion(bf16[1,128,4096]{2,1,0:T(8,128)(2,1)} %param.7), kind=kLoop, calls=%fused_computation.8 | loop fusion | bytes 2097152 | tf_op jit(solution)/shard_map/squeeze | solution.py:201
  4.1 8.6 %all-to-all-start = ((bf16[8,128,512]{2,1,0:T(8,128)(2,1)}), bf16[8,128,512]{2,1,0:T(8,128)(2,1)}, u32[]{:S(2)}, u32[]{:S(2)}) async-start(bf16[8,128,512]{2,1,0:T(8,128)(2,1)} %copy-done.6), calls=%async_computation | async-start | bytes 2097152 | tf_op jit(solution)/shard_map/all_to_all | solution.py:204
  12.7 1.4 collective-permute-start.3
  18.3 1.3 dynamic-slice_bitcast_fusion
  19.8 6.0 %collective-permute-start.4 = (bf16[128,4096]{1,0:T(8,128)(2,1)S(1)}, bf16[128,4096]{1,0:T(8,128)(2,1)S(1)}, u32[]{:S(2)}, u32[]{:S(2)}) collective-permute-start(bf16[128,4096]{1,0:T(8,128)(2,1)S(1)} %pad_maximum_fusion), channel_id=1, source_target_pairs={{16,0},{32,16},{48,32},{64,48},{80,64},{96,80},{112,96},{128,112},... | collective-permute-start | bytes 3145736 | tf_op jit(solution)/shard_map/ppermute | solution.py:39
  25.9 1.9 %collective-permute-start.5 = (bf16[128,4096]{1,0:T(8,128)(2,1)S(1)}, bf16[128,4096]{1,0:T(8,128)(2,1)S(1)}, u32[]{:S(2)}, u32[]{:S(2)}) collective-permute-start(bf16[128,4096]{1,0:T(8,128)(2,1)S(1)} %pad_maximum_fusion.1), channel_id=1, source_target_pairs={{0,16},{16,32},{32,48},{48,64},{64,80},{80,96},{96,112},{112,128},... | collective-permute-start | bytes 3145736 | tf_op jit(solution)/shard_map/ppermute | solution.py:39
  27.9 2.1 %collective-permute-start.1 = (bf16[64,4096]{1,0:T(8,128)(2,1)S(1)}, bf16[64,4096]{1,0:T(8,128)(2,1)}, u32[]{:S(2)}, u32[]{:S(2)}) collective-permute-start(bf16[64,4096]{1,0:T(8,128)(2,1)S(1)} %collective-permute-done.xa.refs_0_), channel_id=1, source_target_pairs={{0,2},{1,3},{2,4},{3,5},{4,6},{5,7},{6,8},{7,9},{8,10},{9,11},{10,... | collective-permute-start | bytes 1572872 | tf_op jit(solution)/shard_map/ppermute | solution.py:30
  30.8 1.3 collective-permute-start.2
  32.1 19.0 %collective-permute-done.1.refs_2_ = bf16[64,4096]{1,0:T(8,128)(2,1)} collective-permute-done((bf16[64,4096]{1,0:T(8,128)(2,1)S(1)}, bf16[64,4096]{1,0:T(8,128)(2,1)}, u32[]{:S(2)}, u32[]{:S(2)}) %collective-permute-start.1) | collective-permute-done | bytes 524320 | tf_op jit(solution)/shard_map/ppermute | solution.py:30
  51.1 1.6 collective-permute-start.11
  54.1 2.8 %collective-permute-done.5.below = bf16[128,4096]{1,0:T(8,128)(2,1)S(1)} collective-permute-done((bf16[128,4096]{1,0:T(8,128)(2,1)S(1)}, bf16[128,4096]{1,0:T(8,128)(2,1)S(1)}, u32[]{:S(2)}, u32[]{:S(2)}) %collective-permute-start.5) | collective-permute-done | bytes 1048608 | tf_op jit(solution)/shard_map/ppermute | solution.py:39
  57.9 3.3 %collective-permute-start.8 = (bf16[64,4096]{1,0:T(8,128)(2,1)}, bf16[64,4096]{1,0:T(8,128)(2,1)}, u32[]{:S(2)}, u32[]{:S(2)}) collective-permute-start(bf16[64,4096]{1,0:T(8,128)(2,1)} %collective-permute-done.2.refs_4_), channel_id=1, source_target_pairs={{0,14},{1,15},{2,0},{3,1},{4,2},{5,3},{6,4},{7,5},{8,6},{9,7},{10,... | collective-permute-start | bytes 1572872 | tf_op jit(solution)/shard_map/ppermute | solution.py:30
  61.2 4.8 %collective-permute-done.11.refs_5_ = bf16[64,4096]{1,0:T(8,128)(2,1)} collective-permute-done((bf16[64,4096]{1,0:T(8,128)(2,1)S(1)}, bf16[64,4096]{1,0:T(8,128)(2,1)}, u32[]{:S(2)}, u32[]{:S(2)}) %collective-permute-start.11) | collective-permute-done | bytes 524320 | tf_op jit(solution)/shard_map/ppermute | solution.py:30
  66.0 2.8 %collective-permute-start.15 = (bf16[64,4096]{1,0:T(8,128)(2,1)}, bf16[64,4096]{1,0:T(8,128)(2,1)}, u32[]{:S(2)}, u32[]{:S(2)}) collective-permute-start(bf16[64,4096]{1,0:T(8,128)(2,1)} %collective-permute-done.11.refs_5_), channel_id=1, source_target_pairs={{0,14},{1,15},{2,0},{3,1},{4,2},{5,3},{6,4},{7,5},{8,6},{9,7},{10,... | collective-permute-start | bytes 1572872 | tf_op jit(solution)/shard_map/ppermute | solution.py:30
  68.8 11.2 %collective-permute-done.6.refs_0_ = bf16[64,4096]{1,0:T(8,128)(2,1)} collective-permute-done((bf16[64,4096]{1,0:T(8,128)(2,1)}, bf16[64,4096]{1,0:T(8,128)(2,1)}, u32[]{:S(2)}, u32[]{:S(2)}) %collective-permute-start.6) | collective-permute-done | bytes 524320 | tf_op jit(solution)/shard_map/ppermute | solution.py:30
  80.4 1.6 copy-done.2
  82.0 1.6 copy-done.3
  83.6 1.2 copy-done.5
  84.8 1.2 copy-done.8
  86.0 1.2 copy-done.10
  87.2 3.1 %shard_map.95 = (bf16[128,4096]{1,0:T(8,128)(2,1)S(1)}, bf16[8,144,128]{2,1,0:T(8,128)(2,1)S(1)}) custom-call(s32[3]{0:T(128)S(1)} %pad_add_fusion.place, s32[4]{0:T(128)S(1)} %bitcast.49, s32[128]{0:T(128)S(1)} %reshape.89.plan, bf16[64,4096]{1,0:T(8,128)(2,1)S(1)} %collective-permute-done.xa.refs_0_, ...), custom_call_target="tpu_custom_call" | custom-call | flops 1024 | bytes 1024 | tf_op jit(solution)/shard_map/pallas_call | solution.py:53
  92.0 4.5 %all-to-all-start.1 = ((bf16[8,144,128]{2,1,0:T(8,128)(2,1)}), bf16[8,144,128]{2,1,0:T(8,128)(2,1)S(1)}, u32[]{:S(2)}, u32[]{:S(2)}) async-start(bf16[8,144,128]{2,1,0:T(8,128)(2,1)} %copy-done.13), calls=%async_computation.1 | async-start | bytes 589824 | tf_op jit(solution)/shard_map/all_to_all | solution.py:204
  96.6 3.2 %collective-permute-start.9 = (bf16[64,4096]{1,0:T(8,128)(2,1)}, bf16[64,4096]{1,0:T(8,128)(2,1)}, u32[]{:S(2)}, u32[]{:S(2)}) collective-permute-start(bf16[64,4096]{1,0:T(8,128)(2,1)} %collective-permute-done.8.refs_2_), channel_id=1, source_target_pairs={{0,14},{1,15},{2,0},{3,1},{4,2},{5,3},{6,4},{7,5},{8,6},{9,7},{10,... | collective-permute-start | bytes 1572872 | tf_op jit(solution)/shard_map/ppermute | solution.py:30
  99.8 1.5 collective-permute-start.17
  101.8 7.6 %all-to-all-done.1.line = bf16[8,144,128]{2,1,0:T(8,128)(2,1)S(1)} async-done(((bf16[8,144,128]{2,1,0:T(8,128)(2,1)}), bf16[8,144,128]{2,1,0:T(8,128)(2,1)S(1)}, u32[]{:S(2)}, u32[]{:S(2)}) %all-to-all-start.1) | async-done | bytes 294944 | tf_op jit(solution)/shard_map/all_to_all | solution.py:204
  109.4 2.0 %shard_map.99 = (f32[384,256]{1,0:T(8,128)S(1)}, bf16[384,256]{1,0:T(8,128)(2,1)S(1)}) custom-call(s32[3]{0:T(128)S(1)} %pad_add_fusion.place, bf16[8,144,128]{2,1,0:T(8,128)(2,1)S(1)} %all-to-all-done.1.line, bf16[8,128,512]{2,1,0:T(8,128)(2,1)} %all-to-all-done.refs_0_), custom_call_target="tpu_custom_call" | custom-call | flops 1024 | bytes 1024 | tf_op jit(solution)/shard_map/pallas_call | solution.py:53
  112.4 4.5 %collective-permute-done.9.refs_6_ = bf16[64,4096]{1,0:T(8,128)(2,1)} collective-permute-done((bf16[64,4096]{1,0:T(8,128)(2,1)}, bf16[64,4096]{1,0:T(8,128)(2,1)}, u32[]{:S(2)}, u32[]{:S(2)}) %collective-permute-start.9) | collective-permute-done | bytes 524320 | tf_op jit(solution)/shard_map/ppermute | solution.py:30
  116.9 4.1 %collective-permute-start.22 = (bf16[128,512]{1,0:T(8,128)(2,1)S(1)}, bf16[128,512]{1,0:T(8,128)(2,1)S(1)}, u32[]{:S(2)}, u32[]{:S(2)}) collective-permute-start(bf16[128,512]{1,0:T(8,128)(2,1)S(1)} %fusion), channel_id=1, source_target_pairs={{0,8},{1,9},{2,10},{3,11},{4,12},{5,13},{6,14},{7,15},{8,0},{9,1},... | collective-permute-start | bytes 393224 | tf_op jit(solution)/shard_map/ppermute | solution.py:30
  121.9 7.6 %collective-permute-done.17.refs_7_ = bf16[64,4096]{1,0:T(8,128)(2,1)} collective-permute-done((bf16[64,4096]{1,0:T(8,128)(2,1)}, bf16[64,4096]{1,0:T(8,128)(2,1)}, u32[]{:S(2)}, u32[]{:S(2)}) %collective-permute-start.17) | collective-permute-done | bytes 524320 | tf_op jit(solution)/shard_map/ppermute | solution.py:30
  129.5 1.3 collective-permute-start.21
  130.8 4.0 %shard_map.96 = (bf16[128,512]{1,0:T(8,128)(2,1)S(1)}, bf16[128,512]{1,0:T(8,128)(2,1)S(1)}, bf16[128,512]{1,0:T(8,128)(2,1)S(1)}, bf16[3,128,512]{2,1,0:T(8,128)(2,1)S(1)}) custom-call(s32[3]{0:T(128)S(1)} %pad_add_fusion.place, bf16[64,4096]{1,0:T(8,128)(2,1)S(1)} %collective-permute-done.xa.refs_0_, ...), custom_call_target="tpu_custom_call" | custom-call | flops 1024 | bytes 1024 | tf_op jit(solution)/shard_map/pallas_call | solution.py:53
  134.9 5.2 %shard_map.97 = (bf16[128,512]{1,0:T(8,128)(2,1)S(1)}, bf16[128,512]{1,0:T(8,128)(2,1)S(1)}, bf16[128,512]{1,0:T(8,128)(2,1)S(1)}, bf16[128,512]{1,0:T(8,128)(2,1)S(1)}, bf16[4,128,512]{2,1,0:T(8,128)(2,1)S(1)}) custom-call(s32[3]{0:T(128)S(1)} %pad_add_fusion.place, bf16[64,4096]{1,0:T(8,128)(2,1)} %collective-permute-done.6.refs_0_, ...), custom_call_target="tpu_custom_call" | custom-call | flops 1024 | bytes 1024 | tf_op jit(solution)/shard_map/pallas_call | solution.py:53
  140.1 1.3 shard_map.98
  142.4 4.8 %collective-permute-done.27 = bf16[384,256]{1,0:T(8,128)(2,1)S(1)} collective-permute-done((bf16[384,256]{1,0:T(8,128)(2,1)S(1)}, bf16[384,256]{1,0:T(8,128)(2,1)S(1)}, u32[]{:S(2)}, u32[]{:S(2)}) %collective-permute-start.27) | collective-permute-done | bytes 196640 | tf_op jit(solution)/shard_map/ppermute | solution.py:34
  147.3 1.9 %collective-permute-start.30 = (bf16[2,64,256]{2,1,0:T(8,128)(2,1)S(1)}, bf16[2,64,256]{2,1,0:T(8,128)(2,1)S(1)}, u32[]{:S(2)}, u32[]{:S(2)}) collective-permute-start(bf16[2,64,256]{2,1,0:T(8,128)(2,1)S(1)} %pad_maximum_fusion.3), channel_id=1, source_target_pairs={{16,0},{32,16},{48,32},{64,48},{80,64},{96,80},{112,96},{128,112},... | collective-permute-start | bytes 196616 | tf_op jit(solution)/shard_map/ppermute | solution.py:39
  149.2 2.4 %collective-permute-start.29 = (bf16[2,64,256]{2,1,0:T(8,128)(2,1)S(1)}, bf16[2,64,256]{2,1,0:T(8,128)(2,1)S(1)}, u32[]{:S(2)}, u32[]{:S(2)}) collective-permute-start(bf16[2,64,256]{2,1,0:T(8,128)(2,1)S(1)} %pad_maximum_fusion.2), channel_id=1, source_target_pairs={{0,16},{16,32},{32,48},{48,64},{64,80},{80,96},{96,112},{112,128},... | collective-permute-start | bytes 196616 | tf_op jit(solution)/shard_map/ppermute | solution.py:39
  152.2 2.0 %collective-permute-start.13 = (bf16[128,512]{1,0:T(8,128)(2,1)S(1)}, bf16[128,512]{1,0:T(8,128)(2,1)S(1)}, u32[]{:S(2)}, u32[]{:S(2)}) collective-permute-start(bf16[128,512]{1,0:T(8,128)(2,1)S(1)} %get-tuple-element.27), channel_id=1, source_target_pairs={{0,14},{1,15},{2,0},{3,1},{4,2},{5,3},{6,4},{7,5},{8,6},{9,7},{10,... | collective-permute-start | bytes 393224 | tf_op jit(solution)/shard_map/ppermute | solution.py:30
  154.3 2.3 %collective-permute-start.18 = (bf16[128,512]{1,0:T(8,128)(2,1)S(1)}, bf16[128,512]{1,0:T(8,128)(2,1)S(1)}, u32[]{:S(2)}, u32[]{:S(2)}) collective-permute-start(bf16[128,512]{1,0:T(8,128)(2,1)S(1)} %get-tuple-element.28), channel_id=1, source_target_pairs={{0,12},{1,13},{2,14},{3,15},{4,0},{5,1},{6,2},{7,3},{8,4},{9,5},{1... | collective-permute-start | bytes 393224 | tf_op jit(solution)/shard_map/ppermute | solution.py:30
  156.6 1.9 collective-permute-done.29
  158.4 3.3 %collective-permute-start.19 = (bf16[128,512]{1,0:T(8,128)(2,1)S(1)}, bf16[128,512]{1,0:T(8,128)(2,1)S(1)}, u32[]{:S(2)}, u32[]{:S(2)}) collective-permute-start(bf16[128,512]{1,0:T(8,128)(2,1)S(1)} %get-tuple-element.29), channel_id=1, source_target_pairs={{0,10},{1,11},{2,12},{3,13},{4,14},{5,15},{6,0},{7,1},{8,2},{9,3},... | collective-permute-start | bytes 393224 | tf_op jit(solution)/shard_map/ppermute | solution.py:30
  162.4 1.2 collective-permute-start.25
  163.6 2.3 %shard_map.100 = bf16[128,512]{1,0:T(8,128)(2,1)S(1)} custom-call(s32[3]{0:T(128)S(1)} %pad_add_fusion.place, bf16[64,4096]{1,0:T(8,128)(2,1)S(1)} %collective-permute-done.20.refs_0_, bf16[64,4096]{1,0:T(8,128)(2,1)S(1)} %collective-permute-done.21.refs_1_, bf16[4096,256]{1,0:T(8,128)(2,1)S(1)} %bitcast.44, ...), custom_call_target="tpu_custom_call" | custom-call | flops 1024 | bytes 1024 | tf_op jit(solution)/shard_map/pallas_call | solution.py:53
  166.0 3.1 %collective-permute-start.26 = (bf16[128,512]{1,0:T(8,128)(2,1)S(1)}, bf16[128,512]{1,0:T(8,128)(2,1)S(1)}, u32[]{:S(2)}, u32[]{:S(2)}) collective-permute-start(bf16[128,512]{1,0:T(8,128)(2,1)S(1)} %get-tuple-element.40), channel_id=1, source_target_pairs={{0,2},{1,3},{2,4},{3,5},{4,6},{5,7},{6,8},{7,9},{8,10},{9,11},{10,... | collective-permute-start | bytes 393224 | tf_op jit(solution)/shard_map/ppermute | solution.py:30
  169.1 2.5 %collective-permute-start.23 = (bf16[128,512]{1,0:T(8,128)(2,1)S(1)}, bf16[128,512]{1,0:T(8,128)(2,1)S(1)}, u32[]{:S(2)}, u32[]{:S(2)}) collective-permute-start(bf16[128,512]{1,0:T(8,128)(2,1)S(1)} %shard_map.100), channel_id=1, source_target_pairs={{0,8},{1,9},{2,10},{3,11},{4,12},{5,13},{6,14},{7,15},{8,0},{9,1},... | collective-permute-start | bytes 393224 | tf_op jit(solution)/shard_map/ppermute | solution.py:30
  172.5 1.1 collective-permute-done.24.refs_5_
  173.6 7.3 %collective-permute-done.25.refs_6_ = bf16[128,512]{1,0:T(8,128)(2,1)S(1)} collective-permute-done((bf16[128,512]{1,0:T(8,128)(2,1)S(1)}, bf16[128,512]{1,0:T(8,128)(2,1)S(1)}, u32[]{:S(2)}, u32[]{:S(2)}) %collective-permute-start.25) | collective-permute-done | bytes 131104 | tf_op jit(solution)/shard_map/ppermute | solution.py:30
  180.9 6.9 %collective-permute-done.26.refs_7_ = bf16[128,512]{1,0:T(8,128)(2,1)S(1)} collective-permute-done((bf16[128,512]{1,0:T(8,128)(2,1)S(1)}, bf16[128,512]{1,0:T(8,128)(2,1)S(1)}, u32[]{:S(2)}, u32[]{:S(2)}) %collective-permute-start.26) | collective-permute-done | bytes 131104 | tf_op jit(solution)/shard_map/ppermute | solution.py:30
  187.8 1.9 shard_map.101
  (86 shorter events, 13.3 us)
Async XLA Ops:
  0.6 2.4 %copy-start.4 = (bf16[1,128,4096]{2,1,0:T(8,128)(2,1)S(1)}, bf16[1,128,4096]{2,1,0:T(8,128)(2,1)}, u32[]{:S(2)}) copy-start(bf16[1,128,4096]{2,1,0:T(8,128)(2,1)} %param.13) | copy-start | bytes 3145732
  3.0 24.9 %collective-permute-start = (bf16[64,4096]{1,0:T(8,128)(2,1)}, bf16[64,4096]{1,0:T(8,128)(2,1)S(1)}, u32[]{:S(2)}, u32[]{:S(2)}) collective-permute-start(bf16[64,4096]{1,0:T(8,128)(2,1)} %get-tuple-element.52), channel_id=1, source_target_pairs={{0,16},{16,32},{32,48},{48,64},{64,80},{80,96},{96,112},{112,128},... | collective-permute-start | bytes 1572872 | tf_op jit(solution)/shard_map/ppermute | solution.py:200
  3.0 11.1 %copy-start.15 = (s32[16,4,2]{0,2,1:T(2,128)S(1)}, s32[16,4,2]{0,2,1:T(2,128)}, u32[]{:S(2)}) copy-start(s32[16,4,2]{0,2,1:T(2,128)} %param.9) | copy-start | bytes 1540
  3.1 1.0 copy-start.6
  4.1 15.5 %copy-start.1 = (bf16[1,4,64,4096]{3,2,1,0:T(8,128)(2,1)S(1)}, bf16[1,4,64,4096]{3,2,1,0:T(8,128)(2,1)}, u32[]{:S(2)}) copy-start(bf16[1,4,64,4096]{3,2,1,0:T(8,128)(2,1)} %param.11) | copy-start | bytes 6291460
  4.1 76.3 %all-to-all-start = ((bf16[8,128,512]{2,1,0:T(8,128)(2,1)}), bf16[8,128,512]{2,1,0:T(8,128)(2,1)}, u32[]{:S(2)}, u32[]{:S(2)}) async-start(bf16[8,128,512]{2,1,0:T(8,128)(2,1)} %copy-done.6), calls=%async_computation | async-start | bytes 2097152 | tf_op jit(solution)/shard_map/all_to_all | solution.py:204
  12.7 18.1 %collective-permute-start.3 = (bf16[64,4096]{1,0:T(8,128)(2,1)}, bf16[64,4096]{1,0:T(8,128)(2,1)S(1)}, u32[]{:S(2)}, u32[]{:S(2)}) collective-permute-start(bf16[64,4096]{1,0:T(8,128)(2,1)} %get-tuple-element.51), channel_id=1, source_target_pairs={{0,16},{16,32},{32,48},{48,64},{64,80},{80,96},{96,112},{112,128},... | collective-permute-start | bytes 1572872 | tf_op jit(solution)/shard_map/ppermute | solution.py:201
  19.7 10.3 %copy-start = (bf16[1,4096,256]{2,1,0:T(8,128)(2,1)S(1)}, bf16[1,4096,256]{2,1,0:T(8,128)(2,1)}, u32[]{:S(2)}) copy-start(bf16[1,4096,256]{2,1,0:T(8,128)(2,1)} %param.10) | copy-start | bytes 6291460
  19.7 60.6 %copy-start.14 = (s32[1,1,4]{2,1,0:T(1,128)S(1)}, s32[1,1,4]{2,1,0:T(1,128)}, u32[]{:S(2)}) copy-start(s32[1,1,4]{2,1,0:T(1,128)} %param.8) | copy-start | bytes 52
  19.8 33.3 %collective-permute-start.4 = (bf16[128,4096]{1,0:T(8,128)(2,1)S(1)}, bf16[128,4096]{1,0:T(8,128)(2,1)S(1)}, u32[]{:S(2)}, u32[]{:S(2)}) collective-permute-start(bf16[128,4096]{1,0:T(8,128)(2,1)S(1)} %pad_maximum_fusion), channel_id=1, source_target_pairs={{16,0},{32,16},{48,32},{64,48},{80,64},{96,80},{112,96},{128,112},... | collective-permute-start | bytes 3145736 | tf_op jit(solution)/shard_map/ppermute | solution.py:39
  25.9 31.0 %collective-permute-start.5 = (bf16[128,4096]{1,0:T(8,128)(2,1)S(1)}, bf16[128,4096]{1,0:T(8,128)(2,1)S(1)}, u32[]{:S(2)}, u32[]{:S(2)}) collective-permute-start(bf16[128,4096]{1,0:T(8,128)(2,1)S(1)} %pad_maximum_fusion.1), channel_id=1, source_target_pairs={{0,16},{16,32},{32,48},{48,64},{64,80},{80,96},{96,112},{112,128},... | collective-permute-start | bytes 3145736 | tf_op jit(solution)/shard_map/ppermute | solution.py:39
  27.9 23.2 %collective-permute-start.1 = (bf16[64,4096]{1,0:T(8,128)(2,1)S(1)}, bf16[64,4096]{1,0:T(8,128)(2,1)}, u32[]{:S(2)}, u32[]{:S(2)}) collective-permute-start(bf16[64,4096]{1,0:T(8,128)(2,1)S(1)} %collective-permute-done.xa.refs_0_), channel_id=1, source_target_pairs={{0,2},{1,3},{2,4},{3,5},{4,6},{5,7},{6,8},{7,9},{8,10},{9,11},{10,... | collective-permute-start | bytes 1572872 | tf_op jit(solution)/shard_map/ppermute | solution.py:30
  30.0 91.5 %collective-permute-start.12 = (bf16[4096,256]{1,0:T(8,128)(2,1)S(1)}, bf16[4096,256]{1,0:T(8,128)(2,1)}, u32[]{:S(2)}, u32[]{:S(2)}) collective-permute-start(bf16[4096,256]{1,0:T(8,128)(2,1)S(1)} %bitcast.41), channel_id=1, source_target_pairs={{0,1},{1,0},{2,3},{3,2},{4,5},{5,4},{6,7},{7,6},{8,9},{9,8},{10,11... | collective-permute-start | bytes 6291464 | tf_op jit(solution)/shard_map/ppermute | solution.py:34
  30.8 21.9 %collective-permute-start.2 = (bf16[64,4096]{1,0:T(8,128)(2,1)S(1)}, bf16[64,4096]{1,0:T(8,128)(2,1)}, u32[]{:S(2)}, u32[]{:S(2)}) collective-permute-start(bf16[64,4096]{1,0:T(8,128)(2,1)S(1)} %collective-permute-done.xa.refs_0_), channel_id=1, source_target_pairs={{0,14},{1,15},{2,0},{3,1},{4,2},{5,3},{6,4},{7,5},{8,6},{9,7},{10,... | collective-permute-start | bytes 1572872 | tf_op jit(solution)/shard_map/ppermute | solution.py:30
  51.1 14.9 %collective-permute-start.11 = (bf16[64,4096]{1,0:T(8,128)(2,1)S(1)}, bf16[64,4096]{1,0:T(8,128)(2,1)}, u32[]{:S(2)}, u32[]{:S(2)}) collective-permute-start(bf16[64,4096]{1,0:T(8,128)(2,1)S(1)} %collective-permute-done.3.xb.refs_1_), channel_id=1, source_target_pairs={{0,14},{1,15},{2,0},{3,1},{4,2},{5,3},{6,4},{7,5},{8,6},{9,7},{10,... | collective-permute-start | bytes 1572872 | tf_op jit(solution)/shard_map/ppermute | solution.py:30
  52.7 16.1 %collective-permute-start.10 = (bf16[64,4096]{1,0:T(8,128)(2,1)S(1)}, bf16[64,4096]{1,0:T(8,128)(2,1)}, u32[]{:S(2)}, u32[]{:S(2)}) collective-permute-start(bf16[64,4096]{1,0:T(8,128)(2,1)S(1)} %collective-permute-done.3.xb.refs_1_), channel_id=1, source_target_pairs={{0,2},{1,3},{2,4},{3,5},{4,6},{5,7},{6,8},{7,9},{8,10},{9,11},{10,... | collective-permute-start | bytes 1572872 | tf_op jit(solution)/shard_map/ppermute | solution.py:30
  53.2 1.0 copy-start.7
  54.1 25.9 %collective-permute-start.6 = (bf16[64,4096]{1,0:T(8,128)(2,1)}, bf16[64,4096]{1,0:T(8,128)(2,1)}, u32[]{:S(2)}, u32[]{:S(2)}) collective-permute-start(bf16[64,4096]{1,0:T(8,128)(2,1)} %collective-permute-done.1.refs_2_), channel_id=1, source_target_pairs={{0,2},{1,3},{2,4},{3,5},{4,6},{5,7},{6,8},{7,9},{8,10},{9,11},{10,... | collective-permute-start | bytes 1572872 | tf_op jit(solution)/shard_map/ppermute | solution.py:30
  56.9 1.0 copy-start.9
  57.9 38.7 %collective-permute-start.8 = (bf16[64,4096]{1,0:T(8,128)(2,1)}, bf16[64,4096]{1,0:T(8,128)(2,1)}, u32[]{:S(2)}, u32[]{:S(2)}) collective-permute-start(bf16[64,4096]{1,0:T(8,128)(2,1)} %collective-permute-done.2.refs_4_), channel_id=1, source_target_pairs={{0,14},{1,15},{2,0},{3,1},{4,2},{5,3},{6,4},{7,5},{8,6},{9,7},{10,... | collective-permute-start | bytes 1572872 | tf_op jit(solution)/shard_map/ppermute | solution.py:30
  66.0 33.8 %collective-permute-start.15 = (bf16[64,4096]{1,0:T(8,128)(2,1)}, bf16[64,4096]{1,0:T(8,128)(2,1)}, u32[]{:S(2)}, u32[]{:S(2)}) collective-permute-start(bf16[64,4096]{1,0:T(8,128)(2,1)} %collective-permute-done.11.refs_5_), channel_id=1, source_target_pairs={{0,14},{1,15},{2,0},{3,1},{4,2},{5,3},{6,4},{7,5},{8,6},{9,7},{10,... | collective-permute-start | bytes 1572872 | tf_op jit(solution)/shard_map/ppermute | solution.py:30
  68.8 32.5 %collective-permute-start.14 = (bf16[64,4096]{1,0:T(8,128)(2,1)}, bf16[64,4096]{1,0:T(8,128)(2,1)}, u32[]{:S(2)}, u32[]{:S(2)}) collective-permute-start(bf16[64,4096]{1,0:T(8,128)(2,1)} %collective-permute-done.10.refs_3_), channel_id=1, source_target_pairs={{0,2},{1,3},{2,4},{3,5},{4,6},{5,7},{6,8},{7,9},{8,10},{9,11},{10,... | collective-permute-start | bytes 1572872 | tf_op jit(solution)/shard_map/ppermute | solution.py:30
  80.0 31.4 %collective-permute-start.7 = (bf16[64,4096]{1,0:T(8,128)(2,1)}, bf16[64,4096]{1,0:T(8,128)(2,1)}, u32[]{:S(2)}, u32[]{:S(2)}) collective-permute-start(bf16[64,4096]{1,0:T(8,128)(2,1)} %collective-permute-done.6.refs_0_), channel_id=1, source_target_pairs={{0,2},{1,3},{2,4},{3,5},{4,6},{5,7},{6,8},{7,9},{8,10},{9,11},{10,... | collective-permute-start | bytes 1572872 | tf_op jit(solution)/shard_map/ppermute | solution.py:30
  80.4 1.6 copy-start.2
  82.0 1.6 copy-start.3
  83.6 1.2 copy-start.5
  84.8 1.2 copy-start.8
  86.0 1.2 copy-start.10
  90.3 1.0 copy-start.11
  92.0 17.4 %all-to-all-start.1 = ((bf16[8,144,128]{2,1,0:T(8,128)(2,1)}), bf16[8,144,128]{2,1,0:T(8,128)(2,1)S(1)}, u32[]{:S(2)}, u32[]{:S(2)}) async-start(bf16[8,144,128]{2,1,0:T(8,128)(2,1)} %copy-done.13), calls=%async_computation.1 | async-start | bytes 589824 | tf_op jit(solution)/shard_map/all_to_all | solution.py:204
  96.6 20.3 %collective-permute-start.9 = (bf16[64,4096]{1,0:T(8,128)(2,1)}, bf16[64,4096]{1,0:T(8,128)(2,1)}, u32[]{:S(2)}, u32[]{:S(2)}) collective-permute-start(bf16[64,4096]{1,0:T(8,128)(2,1)} %collective-permute-done.8.refs_2_), channel_id=1, source_target_pairs={{0,14},{1,15},{2,0},{3,1},{4,2},{5,3},{6,4},{7,5},{8,6},{9,7},{10,... | collective-permute-start | bytes 1572872 | tf_op jit(solution)/shard_map/ppermute | solution.py:30
  99.8 29.7 %collective-permute-start.17 = (bf16[64,4096]{1,0:T(8,128)(2,1)}, bf16[64,4096]{1,0:T(8,128)(2,1)}, u32[]{:S(2)}, u32[]{:S(2)}) collective-permute-start(bf16[64,4096]{1,0:T(8,128)(2,1)} %collective-permute-done.15.refs_3_), channel_id=1, source_target_pairs={{0,14},{1,15},{2,0},{3,1},{4,2},{5,3},{6,4},{7,5},{8,6},{9,7},{10,... | collective-permute-start | bytes 1572872 | tf_op jit(solution)/shard_map/ppermute | solution.py:30
  101.3 33.6 %collective-permute-start.16 = (bf16[64,4096]{1,0:T(8,128)(2,1)}, bf16[64,4096]{1,0:T(8,128)(2,1)}, u32[]{:S(2)}, u32[]{:S(2)}) collective-permute-start(bf16[64,4096]{1,0:T(8,128)(2,1)} %collective-permute-done.14.refs_1_), channel_id=1, source_target_pairs={{0,2},{1,3},{2,4},{3,5},{4,6},{5,7},{6,8},{7,9},{8,10},{9,11},{10,... | collective-permute-start | bytes 1572872 | tf_op jit(solution)/shard_map/ppermute | solution.py:30
  111.4 30.9 %collective-permute-start.28 = (bf16[384,256]{1,0:T(8,128)(2,1)S(1)}, bf16[384,256]{1,0:T(8,128)(2,1)S(1)}, u32[]{:S(2)}, u32[]{:S(2)}) collective-permute-start(bf16[384,256]{1,0:T(8,128)(2,1)S(1)} %get-tuple-element.42), channel_id=1, source_target_pairs={{0,1},{1,0},{2,3},{3,2},{4,5},{5,4},{6,7},{7,6},{8,9},{9,8},{10,11... | collective-permute-start | bytes 589832 | tf_op jit(solution)/shard_map/ppermute | solution.py:34
  116.9 23.2 %collective-permute-start.22 = (bf16[128,512]{1,0:T(8,128)(2,1)S(1)}, bf16[128,512]{1,0:T(8,128)(2,1)S(1)}, u32[]{:S(2)}, u32[]{:S(2)}) collective-permute-start(bf16[128,512]{1,0:T(8,128)(2,1)S(1)} %fusion), channel_id=1, source_target_pairs={{0,8},{1,9},{2,10},{3,11},{4,12},{5,13},{6,14},{7,15},{8,0},{9,1},... | collective-permute-start | bytes 393224 | tf_op jit(solution)/shard_map/ppermute | solution.py:30
  121.5 40.3 %collective-permute-start.20 = (bf16[64,4096]{1,0:T(8,128)(2,1)}, bf16[64,4096]{1,0:T(8,128)(2,1)S(1)}, u32[]{:S(2)}, u32[]{:S(2)}) collective-permute-start(bf16[64,4096]{1,0:T(8,128)(2,1)} %collective-permute-done.7.refs_4_), channel_id=1, source_target_pairs={{0,2},{1,3},{2,4},{3,5},{4,6},{5,7},{6,8},{7,9},{8,10},{9,11},{10,... | collective-permute-start | bytes 1572872 | tf_op jit(solution)/shard_map/ppermute | solution.py:30
  129.5 32.9 %collective-permute-start.21 = (bf16[64,4096]{1,0:T(8,128)(2,1)}, bf16[64,4096]{1,0:T(8,128)(2,1)S(1)}, u32[]{:S(2)}, u32[]{:S(2)}) collective-permute-start(bf16[64,4096]{1,0:T(8,128)(2,1)} %collective-permute-done.17.refs_7_), channel_id=1, source_target_pairs={{0,14},{1,15},{2,0},{3,1},{4,2},{5,3},{6,4},{7,5},{8,6},{9,7},{10,... | collective-permute-start | bytes 1572872 | tf_op jit(solution)/shard_map/ppermute | solution.py:30
  141.4 5.8 %collective-permute-start.27 = (bf16[384,256]{1,0:T(8,128)(2,1)S(1)}, bf16[384,256]{1,0:T(8,128)(2,1)S(1)}, u32[]{:S(2)}, u32[]{:S(2)}) collective-permute-start(bf16[384,256]{1,0:T(8,128)(2,1)S(1)} %get-tuple-element.41), channel_id=1, source_target_pairs={{0,1},{1,0},{2,3},{3,2},{4,5},{5,4},{6,7},{7,6},{8,9},{9,8},{10,11... | collective-permute-start | bytes 589832 | tf_op jit(solution)/shard_map/ppermute | solution.py:34
  147.3 7.0 %collective-permute-start.30 = (bf16[2,64,256]{2,1,0:T(8,128)(2,1)S(1)}, bf16[2,64,256]{2,1,0:T(8,128)(2,1)S(1)}, u32[]{:S(2)}, u32[]{:S(2)}) collective-permute-start(bf16[2,64,256]{2,1,0:T(8,128)(2,1)S(1)} %pad_maximum_fusion.3), channel_id=1, source_target_pairs={{16,0},{32,16},{48,32},{64,48},{80,64},{96,80},{112,96},{128,112},... | collective-permute-start | bytes 196616 | tf_op jit(solution)/shard_map/ppermute | solution.py:39
  149.2 9.2 %collective-permute-start.29 = (bf16[2,64,256]{2,1,0:T(8,128)(2,1)S(1)}, bf16[2,64,256]{2,1,0:T(8,128)(2,1)S(1)}, u32[]{:S(2)}, u32[]{:S(2)}) collective-permute-start(bf16[2,64,256]{2,1,0:T(8,128)(2,1)S(1)} %pad_maximum_fusion.2), channel_id=1, source_target_pairs={{0,16},{16,32},{32,48},{48,64},{64,80},{80,96},{96,112},{112,128},... | collective-permute-start | bytes 196616 | tf_op jit(solution)/shard_map/ppermute | solution.py:39
  152.2 13.7 %collective-permute-start.13 = (bf16[128,512]{1,0:T(8,128)(2,1)S(1)}, bf16[128,512]{1,0:T(8,128)(2,1)S(1)}, u32[]{:S(2)}, u32[]{:S(2)}) collective-permute-start(bf16[128,512]{1,0:T(8,128)(2,1)S(1)} %get-tuple-element.27), channel_id=1, source_target_pairs={{0,14},{1,15},{2,0},{3,1},{4,2},{5,3},{6,4},{7,5},{8,6},{9,7},{10,... | collective-permute-start | bytes 393224 | tf_op jit(solution)/shard_map/ppermute | solution.py:30
  154.3 14.8 %collective-permute-start.18 = (bf16[128,512]{1,0:T(8,128)(2,1)S(1)}, bf16[128,512]{1,0:T(8,128)(2,1)S(1)}, u32[]{:S(2)}, u32[]{:S(2)}) collective-permute-start(bf16[128,512]{1,0:T(8,128)(2,1)S(1)} %get-tuple-element.28), channel_id=1, source_target_pairs={{0,12},{1,13},{2,14},{3,15},{4,0},{5,1},{6,2},{7,3},{8,4},{9,5},{1... | collective-permute-start | bytes 393224 | tf_op jit(solution)/shard_map/ppermute | solution.py:30
  158.4 14.1 %collective-permute-start.19 = (bf16[128,512]{1,0:T(8,128)(2,1)S(1)}, bf16[128,512]{1,0:T(8,128)(2,1)S(1)}, u32[]{:S(2)}, u32[]{:S(2)}) collective-permute-start(bf16[128,512]{1,0:T(8,128)(2,1)S(1)} %get-tuple-element.29), channel_id=1, source_target_pairs={{0,10},{1,11},{2,12},{3,13},{4,14},{5,15},{6,0},{7,1},{8,2},{9,3},... | collective-permute-start | bytes 393224 | tf_op jit(solution)/shard_map/ppermute | solution.py:30
  161.8 11.8 %collective-permute-start.24 = (bf16[128,512]{1,0:T(8,128)(2,1)S(1)}, bf16[128,512]{1,0:T(8,128)(2,1)S(1)}, u32[]{:S(2)}, u32[]{:S(2)}) collective-permute-start(bf16[128,512]{1,0:T(8,128)(2,1)S(1)} %get-tuple-element.38), channel_id=1, source_target_pairs={{0,6},{1,7},{2,8},{3,9},{4,10},{5,11},{6,12},{7,13},{8,14},{9,15},... | collective-permute-start | bytes 393224 | tf_op jit(solution)/shard_map/ppermute | solution.py:30
  162.4 25.4 %copy-start.12 = (bf16[128,4096]{1,0:T(8,128)(2,1)S(1)}, bf16[128,4096]{1,0:T(8,128)(2,1)}, u32[]{:S(2)}) copy-start(bf16[128,4096]{1,0:T(8,128)(2,1)} %copy-done.11) | copy-start | bytes 3145732
  162.4 18.5 %collective-permute-start.25 = (bf16[128,512]{1,0:T(8,128)(2,1)S(1)}, bf16[128,512]{1,0:T(8,128)(2,1)S(1)}, u32[]{:S(2)}, u32[]{:S(2)}) collective-permute-start(bf16[128,512]{1,0:T(8,128)(2,1)S(1)} %get-tuple-element.39), channel_id=1, source_target_pairs={{0,4},{1,5},{2,6},{3,7},{4,8},{5,9},{6,10},{7,11},{8,12},{9,13},{1... | collective-permute-start | bytes 393224 | tf_op jit(solution)/shard_map/ppermute | solution.py:30
  166.0 21.8 %collective-permute-start.26 = (bf16[128,512]{1,0:T(8,128)(2,1)S(1)}, bf16[128,512]{1,0:T(8,128)(2,1)S(1)}, u32[]{:S(2)}, u32[]{:S(2)}) collective-permute-start(bf16[128,512]{1,0:T(8,128)(2,1)S(1)} %get-tuple-element.40), channel_id=1, source_target_pairs={{0,2},{1,3},{2,4},{3,5},{4,6},{5,7},{6,8},{7,9},{8,10},{9,11},{10,... | collective-permute-start | bytes 393224 | tf_op jit(solution)/shard_map/ppermute | solution.py:30
  169.1 18.7 %collective-permute-start.23 = (bf16[128,512]{1,0:T(8,128)(2,1)S(1)}, bf16[128,512]{1,0:T(8,128)(2,1)S(1)}, u32[]{:S(2)}, u32[]{:S(2)}) collective-permute-start(bf16[128,512]{1,0:T(8,128)(2,1)S(1)} %shard_map.100), channel_id=1, source_target_pairs={{0,8},{1,9},{2,10},{3,11},{4,12},{5,13},{6,14},{7,15},{8,0},{9,1},... | collective-permute-start | bytes 393224 | tf_op jit(solution)/shard_map/ppermute | solution.py:30
  (1 other events, 0.7 us)

commit v3 on v2

--- a/solution.py
+++ b/solution.py
@@ -70,7 +70,7 @@
     return lax.broadcasted_iota(I32, shape, dim)
 
 
-def rows_kernel(place, lengths, plan, xa, xb, cot, own_down, own_up, above, below, adapted, sent):
+def rows_kernel(place, lengths, plan, own_x, cot, own_down, own_up, above, below, adapted, sent):
     rows, width = cot.shape
     first = place[2] * (2 * JOBS)
     which = []
@@ -86,7 +86,7 @@
         return found
 
     chosen = adapter_of(iota((rows, SIX), 0)) == lax.shift_right_logical(iota((rows, SIX), 1), 6)
-    x = jnp.concatenate([xa[...], xb[...]], axis=0)
+    x = own_x[...]
     guest_down = jnp.concatenate([above[:RANK], below[:RANK]], axis=0)
     guest_up = jnp.concatenate([above[RANK:], below[RANK:]], axis=0)
 
@@ -111,31 +111,66 @@
         sent[k, rows:] = ids
 
 
-def base_kernel(groups, with_columns, place, *refs):
-    blocks, (w_own, w_pair), outs = refs[: 2 * groups], refs[2 * groups : 2 * groups + 2], refs[2 * groups + 2 :]
-    half, _ = blocks[0].shape
-    rows, cols = 2 * half, w_own.shape[1]
+def base_kernel(count, place, *refs):
+    blocks, (w_own, w_pair, out, columns) = refs[:count], refs[count:]
+    rows, cols = blocks[0].shape[0], w_own.shape[1]
     wide = LINES * cols
     lhs = jnp.concatenate([b[...] for b in blocks], axis=0)
     for w, first in ((w_own, 0), (w_pair, cols)):
         result = dot32(lhs, w[...]).astype(BF16)
-        for i in range(groups):
-            outs[i][:, first : first + cols] = result[i * rows : (i + 1) * rows]
-    if with_columns:
-        at = pl.multiple_of(place[0] * wide, wide)
-        for i, b in enumerate(blocks):
-            outs[groups][i // 2, (i % 2) * half : (i % 2 + 1) * half] = b[:, pl.ds(at, wide)]
-
-
-def base(place, halves, w_own, w_pair, with_columns=True):
-    groups = len(halves) // 2
-    half, wide = halves[0].shape[0], LINES * w_own.shape[1]
-    outs = [((2 * half, wide), BF16)] * groups
-    if with_columns:
-        outs = outs + [((groups, 2 * half, wide), BF16)]
-    return kernel_call(
-        functools.partial(base_kernel, groups, with_columns), outs, [place], [*halves, w_own, w_pair]
-    )
+        for i in range(count):
+            out[i, :, first : first + cols] = result[i * rows : (i + 1) * rows]
+    at = pl.multiple_of(place[0] * wide, wide)
+    for i, b in enumerate(blocks):
+        columns[i] = b[:, pl.ds(at, wide)]
+
+
+def owners_kernel(order, places, place, done, f3, r3, w_own, w_pair, out, columns):
+    rows, cols = f3.shape[0], w_own.shape[1]
+    wide = LINES * cols
+    owner = lambda k: lax.rem(place[0] + (places - k), places)
+    for i, k in enumerate(order[: done.shape[0]]):
+        out[owner(k)] = done[i]
+    lhs = jnp.concatenate([f3[...], r3[...]], axis=0)
+    for w, first in ((w_own, 0), (w_pair, cols)):
+        result = dot32(lhs, w[...]).astype(BF16)
+        for i, k in enumerate(order[done.shape[0] :]):
+            out[owner(k), :, first : first + cols] = result[i * rows : (i + 1) * rows]
+    out[owner(places // 2)] = jnp.zeros((rows, wide), BF16)
+    at = pl.multiple_of(place[0] * wide, wide)
+    for i, b in enumerate((f3, r3)):
+        columns[i] = b[:, pl.ds(at, wide)]
+
+
+def halves_kernel(f3, r3, first, second):
+    first[...] = f3[...]
+    second[...] = r3[...]
+
+
+def halves(f3, r3):
+    half, width = f3.shape[0] // 2, f3.shape[1]
+    tile = width // 4
+    shape = jax.ShapeDtypeStruct((half, width), f3.dtype)
+    at = lambda i: pl.BlockSpec((half, tile), lambda j: (i, j))
+    return pl.pallas_call(
+        halves_kernel,
+        grid=(width // tile,),
+        out_shape=(shape, shape),
+        in_specs=[at(0), at(1)],
+        out_specs=(at(0), at(0)),
+        cost_estimate=pl.CostEstimate(flops=1024, bytes_accessed=1024, transcendentals=0),
+    )(f3, r3)
+
+
+def last_kernel(place, first_half, second_half, w_own, w_pair, out, columns):
+    lhs = jnp.concatenate([first_half[...], second_half[...]], axis=0)
+    cols = w_own.shape[1]
+    for w, first in ((w_own, 0), (w_pair, cols)):
+        out[:, first : first + cols] = dot32(lhs, w[...]).astype(BF16)
+    at = pl.multiple_of(place[0] * (LINES * cols), LINES * cols)
+    half = first_half.shape[0]
+    columns[:half] = first_half[:, pl.ds(at, LINES * cols)]
+    columns[half:] = second_half[:, pl.ds(at, LINES * cols)]
 
 
 def gradient_kernel(of_signals, order, place, line, *refs):
@@ -170,14 +205,19 @@
     )
 
 
-def finish_kernel(depth, cols, place, adapted, *refs):
-    pieces, out = refs[:depth], refs[depth]
+def finish_kernel(place, adapted, results, last, out):
     z, x = place[0], place[1]
+    depth, cols = results.shape[0], results.shape[2] // LINES
+
+    def add(at_z, piece):
+        for side, first in ((x, 0), (1 - x, cols)):
+            at = pl.multiple_of((at_z * LINES + side) * cols, cols)
+            total = piece[:, first : first + cols].astype(F32) + adapted[:, pl.ds(at, cols)].astype(F32)
+            out[:, pl.ds(at, cols)] = total.astype(BF16)
+
     for k in range(depth):
-        for side, first in ((x, 0), (1 - x, cols)):
-            at = pl.multiple_of((lax.rem(z + k, depth) * LINES + side) * cols, cols)
-            total = pieces[k][:, first : first + cols].astype(F32) + adapted[:, pl.ds(at, cols)].astype(F32)
-            out[:, pl.ds(at, cols)] = total.astype(BF16)
+        add(k, results[k])
+    add(lax.rem(z + depth // 2, depth), last[...])
 
 
 def on_device(handed, lengths, placement, frozen, down, up, cotangent):
@@ -196,89 +236,97 @@
     wide = width // depth
     cot = cotangent[0]
 
-    behind = [(i, (i + 1) % sections) for i in range(sections)]
-    xa = lax.ppermute(handed[0, :half], "section", behind)
-    xb = lax.ppermute(handed[0, half:], "section", behind)
+    own = lax.ppermute(handed[0], "section", [(i, (i + 1) % sections) for i in range(sections)])
 
     def to_line(value):
         return lax.all_to_all(value, "dp", 0, 0, axis_index_groups=lines, tiled=True)
 
     cot_line = to_line(kernel_call(split_kernel, [((depth, rows, wide), BF16)], [], [cot])[0])
+
+    step = lambda pair: (along_z(pair[0], 1, depth), along_z(pair[1], -1, depth))
+    ring_1 = step((own, own))
 
     slot_below = hosted_slot(placement, jnp.maximum(s - 1, 0), 2)
     slot_above = hosted_slot(placement, jnp.minimum(s + 1, sections - 1), 0)
     maps = lambda k: jnp.concatenate([lax.dynamic_index_in_dim(w[0], k, 0, keepdims=False) for w in (down, up)])
-    from_above = section_shift(maps(slot_below), -1, sections)
-    from_below = section_shift(maps(slot_above), 1, sections)
+    to_below, to_above = in_order((maps(slot_below), maps(slot_above)), own)
+    from_above = section_shift(to_below, -1, sections)
+    from_below = section_shift(to_above, 1, sections)
     own_down = down[0].reshape(JOBS * RANK, width)
     own_up = up[0].reshape(JOBS * RANK, width)
 
     w_own = frozen[0]
-    w_pair = across_x(w_own, devices)
-
-    step = lambda pair: (along_z(pair[0], 1, depth), along_z(pair[1], -1, depth))
-    a1 = step((xa, xa))
-    b1 = step((xb, xb))
-    (xa_,) = in_order((xa,), *a1, cot_line)
+    w_pair = across_x(in_order((w_own,), own)[0], devices)
+
+    ring_2 = step(ring_1)
+    (own_,) = in_order((own,), ring_1, cot_line, w_pair)
     adapted, sent = kernel_call(
         rows_kernel,
         [((rows, width), BF16), ((depth, rows + PAD, 2 * RANK), BF16)],
         [place, lengths.reshape(-1), placement.reshape(-1)],
-        [xa_, xb, cot, own_down, own_up, from_above, from_below],
+        [own_, cot, own_down, own_up, from_above, from_below],
     )
     line = to_line(sent)
-    a2 = step(a1)
-    b2 = step(b1)
-    far_columns = along_z(
-        lax.dynamic_slice_in_dim(jnp.concatenate([xa, xb]), ((z + far) % depth) * wide, wide, 1), far, depth
-    )
-    a3 = step(a2)
-    (line_,) = in_order((line,), *b2)
-    up_mine, up_theirs = gradient(False, tuple(range(depth)), place, line_, [cot_line])
-    up_theirs = across_x(up_theirs, devices)
-    b3 = step(b2)
-
-    pieces = [None] * depth
-    (xa_,) = in_order((xa,), *a3)
-    pieces[0], near_f, near_b, near_columns = base(
-        place, (xa_, xb, a1[0], b1[0], a1[1], b1[1]), w_own, w_pair
-    )
-    pieces[1], pieces[depth - 1] = along_z(near_f, -1, depth), along_z(near_b, 1, depth)
-    last_a, last_b = along_z(a3[0], 1, depth), along_z(b3[1], -1, depth)
-
-    f2, r2, f3, r3, next_columns = base(
-        place, (a2[0], b2[0], a2[1], b2[1], a3[0], b3[0], a3[1], b3[1]), w_own, w_pair
-    )
-    pieces[2], pieces[depth - 2] = along_z(f2, -2, depth), along_z(r2, 2, depth)
-    pieces[3], pieces[depth - 3] = along_z(f3, -3, depth), along_z(r3, 3, depth)
-    order = (0, 1, depth - 1, 2, depth - 2, 3, depth - 3, far)
-    down_mine, down_theirs = gradient(True, order, place, line, [near_columns, next_columns, far_columns])
-    down_theirs = across_x(down_theirs, devices)
-
-    last_a, last_b = in_order((last_a, last_b), down_mine, up_mine, near_columns, next_columns)
-    (last,) = base(place, (last_a, last_b), w_own, w_pair, with_columns=False)
-    pieces[far] = along_z(last, far, depth)
-
-    def over_pair(mine, theirs):
-        return (mine + theirs.astype(F32)).reshape(JOBS + 2, RANK, cols)
-
-    up_total, down_total = over_pair(up_mine, up_theirs), over_pair(down_mine, down_theirs)
-    guests = lambda job: jnp.stack([down_total[job], up_total[job]]).astype(BF16)
-    of_below = section_shift(guests(JOBS), 1, sections).astype(F32)
-    of_above = section_shift(guests(JOBS + 1), -1, sections).astype(F32)
+
+    ring_2 = in_order(ring_2, sent)
+    ring_3 = step(ring_2)
+    order = (0, 1, depth - 1, 2, depth - 2, 3, depth - 3)
+    done, near_columns = kernel_call(
+        functools.partial(base_kernel, 5),
+        [((5, rows, wide), BF16)] * 2,
+        [place],
+        [own, *ring_1, *ring_2, w_own, w_pair],
+    )
+
+    ring_3 = in_order(ring_3, near_columns)
+    half_f, half_r = halves(*ring_3)
+    last = along_z(half_f, 1, depth), along_z(half_r, -1, depth)
+    ring_3 = in_order(ring_3, half_f)
+    results, next_columns = kernel_call(
+        functools.partial(owners_kernel, order, depth),
+        [((depth, rows, wide), BF16), ((2, rows, wide), BF16)],
+        [place],
+        [done, *ring_3, w_own, w_pair],
+    )
+    (line_,) = in_order((line,), results)
+    results = to_line(results)
+    up_parts = gradient(False, tuple(range(depth)), place, line_, [cot_line])
+    last = in_order(last, up_parts)
+    last, far_columns = kernel_call(last_kernel, [((rows, wide), BF16)] * 2, [place], [*last, w_own, w_pair])
+    result_last = along_z(last, far, depth)
+    down_parts = gradient(
+        True, order + (far,), place, line, [near_columns, next_columns, far_columns]
+    )
+
+    (down_mine, down_theirs), (up_mine, up_theirs) = down_parts, up_parts
+    own_rows = JOBS * RANK
+    both = lambda v, w, first, last: jnp.stack([v[first:last], w[first:last]]).astype(BF16)
+    from_pair = across_x(both(down_theirs, up_theirs, 0, own_rows), devices)
+
+    def to_host(first, by):
+        here = both(down_mine, up_mine, first, first + RANK)
+        there = both(down_theirs, up_theirs, first, first + RANK)
+        moves = [(i, i + by) for i in range(sections) if 0 <= i + by < sections]
+        route = [(i * devices + k, j * devices + (k ^ 1)) for i, j in moves for k in range(devices)]
+        return section_shift(here, by, sections).astype(F32) + lax.ppermute(
+            there, ("section", "dp"), route
+        ).astype(F32)
+
+    of_below = to_host(own_rows, 1)
+    of_above = to_host(own_rows + RANK, -1)
     slots = jnp.arange(JOBS, dtype=I32)[:, None, None]
 
-    def gathered(total, i):
+    def gathered(mine, i):
         return (
-            total[:JOBS]
+            (mine[:own_rows] + from_pair[i].astype(F32)).reshape(JOBS, RANK, cols)
             + jnp.where(slots == slot_below, of_below[i][None], 0.0)
             + jnp.where(slots == slot_above, of_above[i][None], 0.0)
         )[None]
 
     (passed,) = kernel_call(
-        functools.partial(finish_kernel, depth, cols), [((rows, width), BF16)], [place], [adapted, *pieces]
-    )
-    return passed[None], gathered(down_total, 0), gathered(up_total, 1)
+        finish_kernel, [((rows, width), BF16)], [place], [adapted, results, result_last]
+    )
+    return passed[None], gathered(down_mine, 0), gathered(up_mine, 1)
 
 
 def solution(mesh):

time: 191 us -> 176 us (0.921); the launches traced: 190 us -> 173 us
  waiting for transfers between devices: 79.4 us -> 65.1 us
  starting transfers between devices: 67 us -> 57 us
  Pallas kernels: 19.9 us -> 24.8 us
  other arithmetic: 3.08 us -> 5.11 us
    ppermute x22 -> x9, waiting for transfers between devices: 62.4 us -> 42.2 us  [along_z(): return lax.ppermute(value, 'dp', route)]
    ppermute x22 -> x9, starting transfers between devices: 37.6 us -> 17.6 us  [along_z(): return lax.ppermute(value, 'dp', route)]
    ppermute x4, waiting for transfers between devices: 4.64 us -> 15.4 us  [section_shift(): return lax.ppermute(value, 'section', route)]
    ppermute x2 -> x3, starting transfers between devices: 1.4 us -> 9.02 us  [the longest x2 8.94 us: to_host(): lax.ppermute(there, ('section', 'dp'), route).astype(F32)]
    all_to_all x2 -> x3, waiting for transfers between devices: 7.57 us -> 0.01 us  [to_line(): lax.all_to_all(value, 'dp', 0, 0, axis_index_groups=lines, tiled=True)]
    all_to_all x2 -> x3, starting transfers between devices: 13.1 us -> 19.4 us  [to_line(): lax.all_to_all(value, 'dp', 0, 0, axis_index_groups=lines, tiled=True)]
    ppermute x2 -> x3, waiting for transfers between devices: 0.01 us -> 5.72 us  [the longest x2 4.52 us: to_host(): lax.ppermute(there, ('section', 'dp'), route).astype(F32)]
    pallas_call x0 -> x1, Pallas kernels: none -> 3.46 us  [halves(): pl.pallas_call(halves_kernel, grid=(width // tile,), out_shape=(shape, sh...]
  transfers between devices with their start and end apart: 33 -> 21, of which waited for: 12 -> 10; matrix products, arithmetic and copies ran while one was open for 3% -> 4% of each run, Pallas kernels for 10% -> 13%
where the time goes in v3:
time: 176 us; the launch traced here: 173 us
  waiting for transfers between devices  65.1 us (37%)
  starting transfers between devices  57 us (32%)
  Pallas kernels  24.8 us (14%)
  local copies, waits for them, and re-layouts  16.2 us (9%)
  other arithmetic  5.11 us (3%)
  between operations  4.57 us (3%)
    ppermute x9, waiting for transfers between devices, along_z(): return lax.ppermute(value, 'dp', route)  42.2 us
    pallas_call x8, Pallas kernels, kernel_call(): pl.pallas_call(kernel, out_shape=tuple((jax.ShapeDtypeStruct(shape, dtype...  21.3 us
    all_to_all x3, starting transfers between devices, to_line(): lax.all_to_all(value, 'dp', 0, 0, axis_index_groups=lines, tiled=True)  19.4 us
    ppermute x9, starting transfers between devices, along_z(): return lax.ppermute(value, 'dp', route)  17.6 us
    ppermute x4, waiting for transfers between devices, section_shift(): return lax.ppermute(value, 'section', route)  15.4 us
    unnamed x39, local copies, waits for them, and re-layouts  14.2 us
    ppermute x4, starting transfers between devices, section_shift(): return lax.ppermute(value, 'section', route)  9.26 us
    ppermute x2, starting transfers between devices, to_host(): lax.ppermute(there, ('section', 'dp'), route).astype(F32)  8.94 us
  transfers between devices with their start and end apart: 21, of which 10 were waited for; matrix products, arithmetic and copies ran while one was open for 4% of the time, Pallas kernels for 13%

profile of v3, /device:TPU:6, one launch (start us, length us, event | category | flops | bytes accessed | tf_op | source)
XLA Modules:
  0.0 172.8 jit_solution(1299541629360703538)
XLA Ops:
  0.7 1.2 copy-done.4
  2.0 1.0 copy-done.6
  3.1 8.6 %all-to-all-start = ((bf16[8,128,512]{2,1,0:T(8,128)(2,1)}), bf16[8,128,512]{2,1,0:T(8,128)(2,1)}, u32[]{:S(2)}, u32[]{:S(2)}) async-start(bf16[8,128,512]{2,1,0:T(8,128)(2,1)} %copy-done.6), calls=%async_computation | async-start | bytes 2097152 | tf_op jit(solution)/shard_map/all_to_all | solution.py:242
  16.1 1.4 dynamic-slice_bitcast_fusion
  17.6 1.2 collective-permute-done.own_x.refs_0_
  19.6 1.9 %collective-permute-start.1 = (bf16[128,4096]{1,0:T(8,128)(2,1)S(1)}, bf16[128,4096]{1,0:T(8,128)(2,1)}, u32[]{:S(2)}, u32[]{:S(2)}) collective-permute-start(bf16[128,4096]{1,0:T(8,128)(2,1)S(1)} %collective-permute-done.own_x.refs_0_), channel_id=1, source_target_pairs={{0,2},{1,3},{2,4},{3,5},{4,6},{5,7},{6,8},{7,9},{8,10},{9,11},{10,... | collective-permute-start | bytes 3145736 | tf_op jit(solution)/shard_map/ppermute | solution.py:30
  21.5 3.9 %collective-permute-start.2 = (bf16[128,4096]{1,0:T(8,128)(2,1)S(1)}, bf16[128,4096]{1,0:T(8,128)(2,1)}, u32[]{:S(2)}, u32[]{:S(2)}) collective-permute-start(bf16[128,4096]{1,0:T(8,128)(2,1)S(1)} %collective-permute-done.own_x.refs_0_), channel_id=1, source_target_pairs={{0,14},{1,15},{2,0},{3,1},{4,2},{5,3},{6,4},{7,5},{8,6},{9,7},{10,... | collective-permute-start | bytes 3145736 | tf_op jit(solution)/shard_map/ppermute | solution.py:30
  25.6 1.0 pad_maximum_fusion
  26.6 1.0 pad_maximum_fusion.1
  27.6 3.0 %collective-permute-start.4 = (bf16[128,4096]{1,0:T(8,128)(2,1)}, bf16[128,4096]{1,0:T(8,128)(2,1)}, u32[]{:S(2)}, u32[]{:S(2)}) collective-permute-start(bf16[128,4096]{1,0:T(8,128)(2,1)} %pad_maximum_fusion), channel_id=1, source_target_pairs={{16,0},{32,16},{48,32},{64,48},{80,64},{96,80},{112,96},{128,112},... | collective-permute-start | bytes 3145736 | tf_op jit(solution)/shard_map/ppermute | solution.py:39
  30.7 1.9 %collective-permute-start.5 = (bf16[128,4096]{1,0:T(8,128)(2,1)}, bf16[128,4096]{1,0:T(8,128)(2,1)}, u32[]{:S(2)}, u32[]{:S(2)}) collective-permute-start(bf16[128,4096]{1,0:T(8,128)(2,1)} %pad_maximum_fusion.1), channel_id=1, source_target_pairs={{0,16},{16,32},{32,48},{48,64},{64,80},{80,96},{96,112},{112,128},... | collective-permute-start | bytes 3145736 | tf_op jit(solution)/shard_map/ppermute | solution.py:39
  32.6 28.8 %collective-permute-done.1.refs_1_ = bf16[128,4096]{1,0:T(8,128)(2,1)} collective-permute-done((bf16[128,4096]{1,0:T(8,128)(2,1)S(1)}, bf16[128,4096]{1,0:T(8,128)(2,1)}, u32[]{:S(2)}, u32[]{:S(2)}) %collective-permute-start.1) | collective-permute-done | bytes 1048608 | tf_op jit(solution)/shard_map/ppermute | solution.py:30
  61.4 3.2 %collective-permute-start.7 = (bf16[128,4096]{1,0:T(8,128)(2,1)}, bf16[128,4096]{1,0:T(8,128)(2,1)}, u32[]{:S(2)}, u32[]{:S(2)}) collective-permute-start(bf16[128,4096]{1,0:T(8,128)(2,1)} %collective-permute-done.2.refs_2_), channel_id=1, source_target_pairs={{0,14},{1,15},{2,0},{3,1},{4,2},{5,3},{6,4},{7,5},{8,6},{9,7},{10,... | collective-permute-start | bytes 3145736 | tf_op jit(solution)/shard_map/ppermute | solution.py:30
  65.0 1.7 %collective-permute-done.3.refs_6_.w_pair = bf16[4096,256]{1,0:T(8,128)(2,1)} collective-permute-done((bf16[4096,256]{1,0:T(8,128)(2,1)S(1)}, bf16[4096,256]{1,0:T(8,128)(2,1)}, u32[]{:S(2)}, u32[]{:S(2)}) %collective-permute-start.3) | collective-permute-done | bytes 2097184 | tf_op jit(solution)/shard_map/ppermute | solution.py:34
  66.7 9.6 %collective-permute-done.4.above = bf16[128,4096]{1,0:T(8,128)(2,1)} collective-permute-done((bf16[128,4096]{1,0:T(8,128)(2,1)}, bf16[128,4096]{1,0:T(8,128)(2,1)}, u32[]{:S(2)}, u32[]{:S(2)}) %collective-permute-start.4) | collective-permute-done | bytes 1048608 | tf_op jit(solution)/shard_map/ppermute | solution.py:39
  76.3 3.6 %collective-permute-done.5.below = bf16[128,4096]{1,0:T(8,128)(2,1)} collective-permute-done((bf16[128,4096]{1,0:T(8,128)(2,1)}, bf16[128,4096]{1,0:T(8,128)(2,1)}, u32[]{:S(2)}, u32[]{:S(2)}) %collective-permute-start.5) | collective-permute-done | bytes 1048608 | tf_op jit(solution)/shard_map/ppermute | solution.py:39
  79.9 1.6 copy-done.2
  81.5 1.6 copy-done.3
  83.1 1.2 copy-done.5
  84.3 4.1 %shard_map.95 = (bf16[128,4096]{1,0:T(8,128)(2,1)S(1)}, bf16[8,144,128]{2,1,0:T(8,128)(2,1)S(1)}) custom-call(s32[3]{0:T(128)S(1)} %pad_add_fusion.place, s32[4]{0:T(128)S(1)} %bitcast.68, s32[128]{0:T(128)S(1)} %reshape.87.plan, bf16[128,4096]{1,0:T(8,128)(2,1)S(1)} %collective-permute-done.own_x.refs_0_, bf16[128,4096]{1,0:T(8,128)(2,1)S(1)} %bitcast.67, ...), custom_call_target="tpu_custom_call" | custom-call | flops 1024 | bytes 1024 | tf_op jit(solution)/shard_map/pallas_call | solution.py:53
  88.4 1.0 copy-done.7
  90.1 2.0 %collective-permute-start.8 = (bf16[128,4096]{1,0:T(8,128)(2,1)}, bf16[128,4096]{1,0:T(8,128)(2,1)}, u32[]{:S(2)}, u32[]{:S(2)}) collective-permute-start(bf16[128,4096]{1,0:T(8,128)(2,1)} %collective-permute-done.6.refs_3_), channel_id=1, source_target_pairs={{0,2},{1,3},{2,4},{3,5},{4,6},{5,7},{6,8},{7,9},{8,10},{9,11},{10,... | collective-permute-start | bytes 3145736 | tf_op jit(solution)/shard_map/ppermute | solution.py:30
  92.1 1.4 collective-permute-start.9
  93.5 7.0 %all-to-all-start.2 = ((bf16[8,144,128]{2,1,0:T(8,128)(2,1)}), bf16[8,144,128]{2,1,0:T(8,128)(2,1)S(1)}, u32[]{:S(2)}, u32[]{:S(2)}) async-start(bf16[8,144,128]{2,1,0:T(8,128)(2,1)} %copy-done.14), calls=%async_computation.2 | async-start | bytes 589824 | tf_op jit(solution)/shard_map/all_to_all | solution.py:242
  101.7 5.8 %shard_map.96 = (bf16[5,128,512]{2,1,0:T(8,128)(2,1)S(1)}, bf16[5,128,512]{2,1,0:T(8,128)(2,1)S(1)}) custom-call(s32[3]{0:T(128)S(1)} %pad_add_fusion.place, bf16[128,4096]{1,0:T(8,128)(2,1)S(1)} %collective-permute-done.own_x.refs_0_, bf16[128,4096]{1,0:T(8,128)(2,1)} %collective-permute-done.1.refs_1_, bf16[128,4096]{1,0:T(8,128)(2,1)} %collective-permute-done.2.refs_2_, ...), custom_call_target="tpu_custom_call" | custom-call | flops 1024 | bytes 1024 | tf_op jit(solution)/shard_map/pallas_call | solution.py:53
  107.5 0.8 copy-done.10
  109.2 8.4 %collective-permute-done.8.f3 = bf16[128,4096]{1,0:T(8,128)(2,1)} collective-permute-done((bf16[128,4096]{1,0:T(8,128)(2,1)}, bf16[128,4096]{1,0:T(8,128)(2,1)}, u32[]{:S(2)}, u32[]{:S(2)}) %collective-permute-start.8) | collective-permute-done | bytes 1048608 | tf_op jit(solution)/shard_map/ppermute | solution.py:30
  117.7 3.5 %shard_map.97 = (bf16[64,4096]{1,0:T(8,128)(2,1)}, bf16[64,4096]{1,0:T(8,128)(2,1)}) custom-call(bf16[128,4096]{1,0:T(8,128)(2,1)} %collective-permute-done.8.f3, bf16[128,4096]{1,0:T(8,128)(2,1)} %collective-permute-done.9.r3), custom_call_target="tpu_custom_call" | custom-call | flops 1024 | bytes 1024 | tf_op jit(solution)/shard_map/pallas_call | solution.py:155
  121.8 3.3 %collective-permute-start.11 = (bf16[64,4096]{1,0:T(8,128)(2,1)}, bf16[64,4096]{1,0:T(8,128)(2,1)}, u32[]{:S(2)}, u32[]{:S(2)}) collective-permute-start(bf16[64,4096]{1,0:T(8,128)(2,1)} %get-tuple-element.46), channel_id=1, source_target_pairs={{0,14},{1,15},{2,0},{3,1},{4,2},{5,3},{6,4},{7,5},{8,6},{9,7},{10,... | collective-permute-start | bytes 1572872 | tf_op jit(solution)/shard_map/ppermute | solution.py:30
  125.1 1.1 copy-done.13
  126.1 3.5 %shard_map.98 = (bf16[8,128,512]{2,1,0:T(8,128)(2,1)S(1)}, bf16[2,128,512]{2,1,0:T(8,128)(2,1)S(1)}) custom-call(s32[3]{0:T(128)S(1)} %pad_add_fusion.place, bf16[5,128,512]{2,1,0:T(8,128)(2,1)S(1)} %copy-done.13, bf16[128,4096]{1,0:T(8,128)(2,1)} %collective-permute-done.8.f3, bf16[128,4096]{1,0:T(8,128)(2,1)} %collective-permute-done.9.r3, ...), custom_call_target="tpu_custom_call" | custom-call | flops 1024 | bytes 1024 | tf_op jit(solution)/shard_map/pallas_call | solution.py:53
  129.7 1.0 copy-done.9
  131.3 3.8 %all-to-all-start.1 = ((bf16[8,128,512]{2,1,0:T(8,128)(2,1)}), bf16[8,128,512]{2,1,0:T(8,128)(2,1)S(1)}, u32[]{:S(2)}, u32[]{:S(2)}) async-start(bf16[8,128,512]{2,1,0:T(8,128)(2,1)} %copy-done.9), calls=%async_computation.1 | async-start | bytes 2097152 | tf_op jit(solution)/shard_map/all_to_all | solution.py:242
  135.2 2.0 %shard_map.99 = (f32[384,256]{1,0:T(8,128)S(1)}, bf16[384,256]{1,0:T(8,128)(2,1)S(1)}) custom-call(s32[3]{0:T(128)S(1)} %pad_add_fusion.place, bf16[8,144,128]{2,1,0:T(8,128)(2,1)S(1)} %all-to-all-done.2.line, bf16[8,128,512]{2,1,0:T(8,128)(2,1)} %all-to-all-done.refs_0_), custom_call_target="tpu_custom_call" | custom-call | flops 1024 | bytes 1024 | tf_op jit(solution)/shard_map/pallas_call | solution.py:53
  137.3 4.9 %collective-permute-done.11.second_half = bf16[64,4096]{1,0:T(8,128)(2,1)} collective-permute-done((bf16[64,4096]{1,0:T(8,128)(2,1)}, bf16[64,4096]{1,0:T(8,128)(2,1)}, u32[]{:S(2)}, u32[]{:S(2)}) %collective-permute-start.11) | collective-permute-done | bytes 524320 | tf_op jit(solution)/shard_map/ppermute | solution.py:30
  142.2 2.6 %shard_map.100 = (bf16[128,512]{1,0:T(8,128)(2,1)S(1)}, bf16[128,512]{1,0:T(8,128)(2,1)S(1)}) custom-call(s32[3]{0:T(128)S(1)} %pad_add_fusion.place, bf16[64,4096]{1,0:T(8,128)(2,1)} %collective-permute-done.10.first_half, bf16[64,4096]{1,0:T(8,128)(2,1)} %collective-permute-done.11.second_half, bf16[4096,256]{1,0:T(8,128)(2,1)S(1)} %bitcast.63, ...), custom_call_target="tpu_custom_call" | custom-call | flops 1024 | bytes 1024 | tf_op jit(solution)/shard_map/pallas_call | solution.py:53
  144.9 1.3 shard_map.102
  146.2 1.2 collective-permute-start.12
  147.4 0.9 collective-permute-start.13
  148.3 7.0 %collective-permute-start.17 = (bf16[2,64,256]{2,1,0:T(8,128)(2,1)S(1)}, bf16[2,64,256]{2,1,0:T(8,128)(2,1)S(1)}, u32[]{:S(2)}, u32[]{:S(2)}) collective-permute-start(bf16[2,64,256]{2,1,0:T(8,128)(2,1)S(1)} %pad_maximum_fusion.6), channel_id=1, source_target_pairs={{16,1},{17,0},{18,3},{19,2},{20,5},{21,4},{22,7},{23,6},{24,9},{25... | collective-permute-start | bytes 196616 | tf_op jit(solution)/shard_map/ppermute | solution.py:311
  155.4 1.9 %collective-permute-start.16 = (bf16[2,64,256]{2,1,0:T(8,128)(2,1)S(1)}, bf16[2,64,256]{2,1,0:T(8,128)(2,1)S(1)}, u32[]{:S(2)}, u32[]{:S(2)}) collective-permute-start(bf16[2,64,256]{2,1,0:T(8,128)(2,1)S(1)} %pad_maximum_fusion.5), channel_id=1, source_target_pairs={{16,0},{32,16},{48,32},{64,48},{80,64},{96,80},{112,96},{128,112},... | collective-permute-start | bytes 196616 | tf_op jit(solution)/shard_map/ppermute | solution.py:39
  157.4 1.9 %collective-permute-start.15 = (bf16[2,64,256]{2,1,0:T(8,128)(2,1)S(1)}, bf16[2,64,256]{2,1,0:T(8,128)(2,1)S(1)}, u32[]{:S(2)}, u32[]{:S(2)}) collective-permute-start(bf16[2,64,256]{2,1,0:T(8,128)(2,1)S(1)} %pad_maximum_fusion.4), channel_id=1, source_target_pairs={{0,17},{1,16},{2,19},{3,18},{4,21},{5,20},{6,23},{7,22},{8,25},{9,... | collective-permute-start | bytes 196616 | tf_op jit(solution)/shard_map/ppermute | solution.py:311
  159.4 2.4 %collective-permute-start.14 = (bf16[2,64,256]{2,1,0:T(8,128)(2,1)S(1)}, bf16[2,64,256]{2,1,0:T(8,128)(2,1)S(1)}, u32[]{:S(2)}, u32[]{:S(2)}) collective-permute-start(bf16[2,64,256]{2,1,0:T(8,128)(2,1)S(1)} %pad_maximum_fusion.3), channel_id=1, source_target_pairs={{0,16},{16,32},{32,48},{48,64},{64,80},{80,96},{96,112},{112,128},... | collective-permute-start | bytes 196616 | tf_op jit(solution)/shard_map/ppermute | solution.py:39
  161.8 4.5 %collective-permute-done.15 = bf16[2,64,256]{2,1,0:T(8,128)(2,1)S(1)} collective-permute-done((bf16[2,64,256]{2,1,0:T(8,128)(2,1)S(1)}, bf16[2,64,256]{2,1,0:T(8,128)(2,1)S(1)}, u32[]{:S(2)}, u32[]{:S(2)}) %collective-permute-start.15) | collective-permute-done | bytes 65568 | tf_op jit(solution)/shard_map/ppermute | solution.py:311
  166.3 2.2 %collective-permute-done.14 = bf16[2,64,256]{2,1,0:T(8,128)(2,1)S(1)} collective-permute-done((bf16[2,64,256]{2,1,0:T(8,128)(2,1)S(1)}, bf16[2,64,256]{2,1,0:T(8,128)(2,1)S(1)}, u32[]{:S(2)}, u32[]{:S(2)}) %collective-permute-start.14) | collective-permute-done | bytes 65568 | tf_op jit(solution)/shard_map/ppermute | solution.py:39
  168.7 0.9 select_add_fusion
  169.6 1.2 copy-done.8
  170.8 1.9 %shard_map.101 = bf16[128,4096]{1,0:T(8,128)(2,1)} custom-call(s32[3]{0:T(128)S(1)} %pad_add_fusion.place, bf16[128,4096]{1,0:T(8,128)(2,1)S(1)} %copy-done.8, bf16[8,128,512]{2,1,0:T(8,128)(2,1)S(1)} %all-to-all-done.1.results, bf16[128,512]{1,0:T(8,128)(2,1)S(1)} %collective-permute-done.12.last), custom_call_target="tpu_custom_call" | custom-call | flops 1024 | bytes 1024 | tf_op jit(solution)/shard_map/pallas_call | solution.py:53
  (73 shorter events, 6.8 us)
Async XLA Ops:
  0.6 18.1 %collective-permute-start = (bf16[128,4096]{1,0:T(8,128)(2,1)}, bf16[128,4096]{1,0:T(8,128)(2,1)S(1)}, u32[]{:S(2)}, u32[]{:S(2)}) collective-permute-start(bf16[128,4096]{1,0:T(8,128)(2,1)} %bitcast.74), channel_id=1, source_target_pairs={{0,16},{16,32},{32,48},{48,64},{64,80},{80,96},{96,112},{112,128},... | collective-permute-start | bytes 3145736 | tf_op jit(solution)/shard_map/ppermute | solution.py:239
  0.7 1.2 copy-start.4
  1.9 9.7 %copy-start.18 = (s32[16,4,2]{0,2,1:T(2,128)S(1)}, s32[16,4,2]{0,2,1:T(2,128)}, u32[]{:S(2)}) copy-start(s32[16,4,2]{0,2,1:T(2,128)} %param.9) | copy-start | bytes 1540
  2.0 1.1 copy-start.6
  3.1 15.7 %copy-start = (bf16[1,4096,256]{2,1,0:T(8,128)(2,1)S(1)}, bf16[1,4096,256]{2,1,0:T(8,128)(2,1)}, u32[]{:S(2)}) copy-start(bf16[1,4096,256]{2,1,0:T(8,128)(2,1)} %param.10) | copy-start | bytes 6291460
  3.1 61.9 %all-to-all-start = ((bf16[8,128,512]{2,1,0:T(8,128)(2,1)}), bf16[8,128,512]{2,1,0:T(8,128)(2,1)}, u32[]{:S(2)}, u32[]{:S(2)}) async-start(bf16[8,128,512]{2,1,0:T(8,128)(2,1)} %copy-done.6), calls=%async_computation | async-start | bytes 2097152 | tf_op jit(solution)/shard_map/all_to_all | solution.py:242
  16.1 9.3 %copy-start.1 = (bf16[1,4,64,4096]{3,2,1,0:T(8,128)(2,1)S(1)}, bf16[1,4,64,4096]{3,2,1,0:T(8,128)(2,1)}, u32[]{:S(2)}) copy-start(bf16[1,4,64,4096]{3,2,1,0:T(8,128)(2,1)} %param.11) | copy-start | bytes 6291460
  18.8 47.9 %collective-permute-start.3 = (bf16[4096,256]{1,0:T(8,128)(2,1)S(1)}, bf16[4096,256]{1,0:T(8,128)(2,1)}, u32[]{:S(2)}, u32[]{:S(2)}) collective-permute-start(bf16[4096,256]{1,0:T(8,128)(2,1)S(1)} %bitcast.60), channel_id=1, source_target_pairs={{0,1},{1,0},{2,3},{3,2},{4,5},{5,4},{6,7},{7,6},{8,9},{9,8},{10,11... | collective-permute-start | bytes 6291464 | tf_op jit(solution)/shard_map/ppermute | solution.py:34
  19.6 41.8 %collective-permute-start.1 = (bf16[128,4096]{1,0:T(8,128)(2,1)S(1)}, bf16[128,4096]{1,0:T(8,128)(2,1)}, u32[]{:S(2)}, u32[]{:S(2)}) collective-permute-start(bf16[128,4096]{1,0:T(8,128)(2,1)S(1)} %collective-permute-done.own_x.refs_0_), channel_id=1, source_target_pairs={{0,2},{1,3},{2,4},{3,5},{4,6},{5,7},{6,8},{7,9},{8,10},{9,11},{10,... | collective-permute-start | bytes 3145736 | tf_op jit(solution)/shard_map/ppermute | solution.py:30
  21.5 39.9 %collective-permute-start.2 = (bf16[128,4096]{1,0:T(8,128)(2,1)S(1)}, bf16[128,4096]{1,0:T(8,128)(2,1)}, u32[]{:S(2)}, u32[]{:S(2)}) collective-permute-start(bf16[128,4096]{1,0:T(8,128)(2,1)S(1)} %collective-permute-done.own_x.refs_0_), channel_id=1, source_target_pairs={{0,14},{1,15},{2,0},{3,1},{4,2},{5,3},{6,4},{7,5},{8,6},{9,7},{10,... | collective-permute-start | bytes 3145736 | tf_op jit(solution)/shard_map/ppermute | solution.py:30
  25.5 54.3 %copy-start.17 = (s32[1,1,4]{2,1,0:T(1,128)S(1)}, s32[1,1,4]{2,1,0:T(1,128)}, u32[]{:S(2)}) copy-start(s32[1,1,4]{2,1,0:T(1,128)} %param.8) | copy-start | bytes 52
  27.6 48.6 %collective-permute-start.4 = (bf16[128,4096]{1,0:T(8,128)(2,1)}, bf16[128,4096]{1,0:T(8,128)(2,1)}, u32[]{:S(2)}, u32[]{:S(2)}) collective-permute-start(bf16[128,4096]{1,0:T(8,128)(2,1)} %pad_maximum_fusion), channel_id=1, source_target_pairs={{16,0},{32,16},{48,32},{64,48},{80,64},{96,80},{112,96},{128,112},... | collective-permute-start | bytes 3145736 | tf_op jit(solution)/shard_map/ppermute | solution.py:39
  30.7 49.2 %collective-permute-start.5 = (bf16[128,4096]{1,0:T(8,128)(2,1)}, bf16[128,4096]{1,0:T(8,128)(2,1)}, u32[]{:S(2)}, u32[]{:S(2)}) collective-permute-start(bf16[128,4096]{1,0:T(8,128)(2,1)} %pad_maximum_fusion.1), channel_id=1, source_target_pairs={{0,16},{16,32},{32,48},{48,64},{64,80},{80,96},{96,112},{112,128},... | collective-permute-start | bytes 3145736 | tf_op jit(solution)/shard_map/ppermute | solution.py:39
  61.4 28.8 %collective-permute-start.6 = (bf16[128,4096]{1,0:T(8,128)(2,1)}, bf16[128,4096]{1,0:T(8,128)(2,1)}, u32[]{:S(2)}, u32[]{:S(2)}) collective-permute-start(bf16[128,4096]{1,0:T(8,128)(2,1)} %collective-permute-done.1.refs_1_), channel_id=1, source_target_pairs={{0,2},{1,3},{2,4},{3,5},{4,6},{5,7},{6,8},{7,9},{8,10},{9,11},{10,... | collective-permute-start | bytes 3145736 | tf_op jit(solution)/shard_map/ppermute | solution.py:30
  61.4 28.8 %collective-permute-start.7 = (bf16[128,4096]{1,0:T(8,128)(2,1)}, bf16[128,4096]{1,0:T(8,128)(2,1)}, u32[]{:S(2)}, u32[]{:S(2)}) collective-permute-start(bf16[128,4096]{1,0:T(8,128)(2,1)} %collective-permute-done.2.refs_2_), channel_id=1, source_target_pairs={{0,14},{1,15},{2,0},{3,1},{4,2},{5,3},{6,4},{7,5},{8,6},{9,7},{10,... | collective-permute-start | bytes 3145736 | tf_op jit(solution)/shard_map/ppermute | solution.py:30
  79.9 1.6 copy-start.2
  81.5 1.6 copy-start.3
  83.1 1.2 copy-start.5
  88.4 1.0 copy-start.7
  89.4 0.7 copy-start.14
  90.1 27.5 %collective-permute-start.8 = (bf16[128,4096]{1,0:T(8,128)(2,1)}, bf16[128,4096]{1,0:T(8,128)(2,1)}, u32[]{:S(2)}, u32[]{:S(2)}) collective-permute-start(bf16[128,4096]{1,0:T(8,128)(2,1)} %collective-permute-done.6.refs_3_), channel_id=1, source_target_pairs={{0,2},{1,3},{2,4},{3,5},{4,6},{5,7},{6,8},{7,9},{8,10},{9,11},{10,... | collective-permute-start | bytes 3145736 | tf_op jit(solution)/shard_map/ppermute | solution.py:30
  92.1 25.6 %collective-permute-start.9 = (bf16[128,4096]{1,0:T(8,128)(2,1)}, bf16[128,4096]{1,0:T(8,128)(2,1)}, u32[]{:S(2)}, u32[]{:S(2)}) collective-permute-start(bf16[128,4096]{1,0:T(8,128)(2,1)} %collective-permute-done.7.refs_4_), channel_id=1, source_target_pairs={{0,14},{1,15},{2,0},{3,1},{4,2},{5,3},{6,4},{7,5},{8,6},{9,7},{10,... | collective-permute-start | bytes 3145736 | tf_op jit(solution)/shard_map/ppermute | solution.py:30
  93.5 37.8 %all-to-all-start.2 = ((bf16[8,144,128]{2,1,0:T(8,128)(2,1)}), bf16[8,144,128]{2,1,0:T(8,128)(2,1)S(1)}, u32[]{:S(2)}, u32[]{:S(2)}) async-start(bf16[8,144,128]{2,1,0:T(8,128)(2,1)} %copy-done.14), calls=%async_computation.2 | async-start | bytes 589824 | tf_op jit(solution)/shard_map/all_to_all | solution.py:242
  107.5 0.9 copy-start.10
  108.4 0.8 copy-start.12
  121.2 16.1 %collective-permute-start.10 = (bf16[64,4096]{1,0:T(8,128)(2,1)}, bf16[64,4096]{1,0:T(8,128)(2,1)}, u32[]{:S(2)}, u32[]{:S(2)}) collective-permute-start(bf16[64,4096]{1,0:T(8,128)(2,1)} %get-tuple-element.42), channel_id=1, source_target_pairs={{0,2},{1,3},{2,4},{3,5},{4,6},{5,7},{6,8},{7,9},{8,10},{9,11},{10,... | collective-permute-start | bytes 1572872 | tf_op jit(solution)/shard_map/ppermute | solution.py:30
  121.8 20.4 %collective-permute-start.11 = (bf16[64,4096]{1,0:T(8,128)(2,1)}, bf16[64,4096]{1,0:T(8,128)(2,1)}, u32[]{:S(2)}, u32[]{:S(2)}) collective-permute-start(bf16[64,4096]{1,0:T(8,128)(2,1)} %get-tuple-element.46), channel_id=1, source_target_pairs={{0,14},{1,15},{2,0},{3,1},{4,2},{5,3},{6,4},{7,5},{8,6},{9,7},{10,... | collective-permute-start | bytes 1572872 | tf_op jit(solution)/shard_map/ppermute | solution.py:30
  125.1 1.1 copy-start.13
  129.7 1.0 copy-start.9
  130.6 0.7 copy-start.15
  131.3 38.3 %all-to-all-start.1 = ((bf16[8,128,512]{2,1,0:T(8,128)(2,1)}), bf16[8,128,512]{2,1,0:T(8,128)(2,1)S(1)}, u32[]{:S(2)}, u32[]{:S(2)}) async-start(bf16[8,128,512]{2,1,0:T(8,128)(2,1)} %copy-done.9), calls=%async_computation.1 | async-start | bytes 2097152 | tf_op jit(solution)/shard_map/all_to_all | solution.py:242
  137.2 7.6 %copy-start.11 = (bf16[5,128,512]{2,1,0:T(8,128)(2,1)S(1)}, bf16[5,128,512]{2,1,0:T(8,128)(2,1)}, u32[]{:S(2)}) copy-start(bf16[5,128,512]{2,1,0:T(8,128)(2,1)} %copy-done.10) | copy-start | bytes 1966084
  137.2 7.6 %copy-start.16 = (bf16[2,128,512]{2,1,0:T(8,128)(2,1)S(1)}, bf16[2,128,512]{2,1,0:T(8,128)(2,1)}, u32[]{:S(2)}) copy-start(bf16[2,128,512]{2,1,0:T(8,128)(2,1)} %copy-done.15) | copy-start | bytes 786436
  146.2 23.4 %collective-permute-start.12 = (bf16[128,512]{1,0:T(8,128)(2,1)S(1)}, bf16[128,512]{1,0:T(8,128)(2,1)S(1)}, u32[]{:S(2)}, u32[]{:S(2)}) collective-permute-start(bf16[128,512]{1,0:T(8,128)(2,1)S(1)} %get-tuple-element.52), channel_id=1, source_target_pairs={{0,8},{1,9},{2,10},{3,11},{4,12},{5,13},{6,14},{7,15},{8,0},{9,1},... | collective-permute-start | bytes 393224 | tf_op jit(solution)/shard_map/ppermute | solution.py:30
  147.4 21.2 %collective-permute-start.13 = (bf16[2,256,256]{2,1,0:T(8,128)(2,1)S(1)}, bf16[2,256,256]{2,1,0:T(8,128)(2,1)S(1)}, u32[]{:S(2)}, u32[]{:S(2)}) collective-permute-start(bf16[2,256,256]{2,1,0:T(8,128)(2,1)S(1)} %pad_maximum_fusion.2), channel_id=1, source_target_pairs={{0,1},{1,0},{2,3},{3,2},{4,5},{5,4},{6,7},{7,6},{8,9},{9,8},{10,11... | collective-permute-start | bytes 786440 | tf_op jit(solution)/shard_map/ppermute | solution.py:34
  148.3 11.0 %collective-permute-start.17 = (bf16[2,64,256]{2,1,0:T(8,128)(2,1)S(1)}, bf16[2,64,256]{2,1,0:T(8,128)(2,1)S(1)}, u32[]{:S(2)}, u32[]{:S(2)}) collective-permute-start(bf16[2,64,256]{2,1,0:T(8,128)(2,1)S(1)} %pad_maximum_fusion.6), channel_id=1, source_target_pairs={{16,1},{17,0},{18,3},{19,2},{20,5},{21,4},{22,7},{23,6},{24,9},{25... | collective-permute-start | bytes 196616 | tf_op jit(solution)/shard_map/ppermute | solution.py:311
  155.4 6.3 %collective-permute-start.16 = (bf16[2,64,256]{2,1,0:T(8,128)(2,1)S(1)}, bf16[2,64,256]{2,1,0:T(8,128)(2,1)S(1)}, u32[]{:S(2)}, u32[]{:S(2)}) collective-permute-start(bf16[2,64,256]{2,1,0:T(8,128)(2,1)S(1)} %pad_maximum_fusion.5), channel_id=1, source_target_pairs={{16,0},{32,16},{48,32},{64,48},{80,64},{96,80},{112,96},{128,112},... | collective-permute-start | bytes 196616 | tf_op jit(solution)/shard_map/ppermute | solution.py:39
  157.4 8.9 %collective-permute-start.15 = (bf16[2,64,256]{2,1,0:T(8,128)(2,1)S(1)}, bf16[2,64,256]{2,1,0:T(8,128)(2,1)S(1)}, u32[]{:S(2)}, u32[]{:S(2)}) collective-permute-start(bf16[2,64,256]{2,1,0:T(8,128)(2,1)S(1)} %pad_maximum_fusion.4), channel_id=1, source_target_pairs={{0,17},{1,16},{2,19},{3,18},{4,21},{5,20},{6,23},{7,22},{8,25},{9,... | collective-permute-start | bytes 196616 | tf_op jit(solution)/shard_map/ppermute | solution.py:311
  159.4 9.2 %collective-permute-start.14 = (bf16[2,64,256]{2,1,0:T(8,128)(2,1)S(1)}, bf16[2,64,256]{2,1,0:T(8,128)(2,1)S(1)}, u32[]{:S(2)}, u32[]{:S(2)}) collective-permute-start(bf16[2,64,256]{2,1,0:T(8,128)(2,1)S(1)} %pad_maximum_fusion.3), channel_id=1, source_target_pairs={{0,16},{16,32},{32,48},{48,64},{64,80},{80,96},{96,112},{112,128},... | collective-permute-start | bytes 196616 | tf_op jit(solution)/shard_map/ppermute | solution.py:39
  169.6 1.2 copy-start.8

commit v4 on v3

--- a/solution.py
+++ b/solution.py
@@ -13,6 +13,7 @@
 SCALE = 0.5
 LINES = 2
 PAD = 16
+MOVED = 2**20
 FEATURES = (((1,), (1,)), ((), ()))
 BF16, F32, I32 = jnp.bfloat16, jnp.float32, jnp.int32
 
@@ -39,16 +40,52 @@
     return lax.ppermute(value, "section", route)
 
 
-def hosted_slot(placement, section, code):
-    plan = lax.dynamic_index_in_dim(placement, section, 0, keepdims=False)
-    return jnp.sum(jnp.where(plan[:, 0] == code, plan[:, 1], 0))
+def hosted_slot(plan, section, code):
+    first, slot = section * (2 * JOBS), 0
+    for j in range(JOBS):
+        slot = slot + jnp.where(plan[first + 2 * j] == code, plan[first + 2 * j + 1], 0)
+    return slot
+
+
+def guest_slots(place, plan):
+    s, sections = place[2], plan.shape[0] // (2 * JOBS)
+    return (
+        hosted_slot(plan, jnp.maximum(s - 1, 0), 2),
+        hosted_slot(plan, jnp.minimum(s + 1, sections - 1), 0),
+    )
+
+
+def maps_kernel(place, plan, down, up, to_below, to_above, sems):
+    copies = []
+    for slot, out in zip(guest_slots(place, plan), (to_below, to_above)):
+        for i, maps in enumerate((down, up)):
+            copies.append(
+                pltpu.make_async_copy(maps.at[slot], out.at[pl.ds(i * RANK, RANK)], sems.at[len(copies)])
+            )
+    for copy in copies:
+        copy.start()
+    for copy in copies:
+        copy.wait()
+
+
+def copy_call(kernel, outs, copies, scalars, arrays):
+    vmem, smem = pl.BlockSpec(memory_space=pltpu.VMEM), pl.BlockSpec(memory_space=pltpu.SMEM)
+    return pl.pallas_call(
+        kernel,
+        out_shape=tuple(jax.ShapeDtypeStruct(shape, BF16) for shape in outs),
+        in_specs=[smem] * len(scalars) + [pl.BlockSpec(memory_space=pl.ANY)] * len(arrays),
+        out_specs=tuple(vmem for _ in outs),
+        scratch_shapes=[pltpu.SemaphoreType.DMA((copies,))],
+        compiler_params=pltpu.CompilerParams(vmem_limit_bytes=40 * 2**20),
+        cost_estimate=pl.CostEstimate(flops=1024, bytes_accessed=1024, transcendentals=0),
+    )(*scalars, *arrays)
 
 
 def in_order(values, *others):
     return lax.optimization_barrier((tuple(values), others))[0]
 
 
-def kernel_call(kernel, outs, scalars, arrays):
+def kernel_call(kernel, outs, scalars, arrays, moved=1024):
     vmem, smem = pl.BlockSpec(memory_space=pltpu.VMEM), pl.BlockSpec(memory_space=pltpu.SMEM)
     return pl.pallas_call(
         kernel,
@@ -56,7 +93,7 @@
         in_specs=[smem] * len(scalars) + [vmem] * len(arrays),
         out_specs=tuple(vmem for _ in outs),
         compiler_params=pltpu.CompilerParams(vmem_limit_bytes=40 * 2**20),
-        cost_estimate=pl.CostEstimate(flops=1024, bytes_accessed=1024, transcendentals=0),
+        cost_estimate=pl.CostEstimate(flops=1024, bytes_accessed=moved, transcendentals=0),
     )(*scalars, *arrays)
 
 
@@ -142,24 +179,16 @@
         columns[i] = b[:, pl.ds(at, wide)]
 
 
-def halves_kernel(f3, r3, first, second):
-    first[...] = f3[...]
-    second[...] = r3[...]
-
-
-def halves(f3, r3):
-    half, width = f3.shape[0] // 2, f3.shape[1]
-    tile = width // 4
-    shape = jax.ShapeDtypeStruct((half, width), f3.dtype)
-    at = lambda i: pl.BlockSpec((half, tile), lambda j: (i, j))
-    return pl.pallas_call(
-        halves_kernel,
-        grid=(width // tile,),
-        out_shape=(shape, shape),
-        in_specs=[at(0), at(1)],
-        out_specs=(at(0), at(0)),
-        cost_estimate=pl.CostEstimate(flops=1024, bytes_accessed=1024, transcendentals=0),
-    )(f3, r3)
+def halves_kernel(f3, r3, first, second, sems):
+    half = first.shape[0]
+    copies = (
+        pltpu.make_async_copy(f3.at[pl.ds(0, half)], first, sems.at[0]),
+        pltpu.make_async_copy(r3.at[pl.ds(half, half)], second, sems.at[1]),
+    )
+    for copy in copies:
+        copy.start()
+    for copy in copies:
+        copy.wait()
 
 
 def last_kernel(place, first_half, second_half, w_own, w_pair, out, columns):
@@ -173,10 +202,8 @@
     columns[half:] = second_half[:, pl.ds(at, LINES * cols)]
 
 
-def gradient_kernel(of_signals, order, place, line, *refs):
-    blocks, (mine, theirs) = refs[:-2], refs[-2:]
+def gradient_terms(of_signals, order, place, line, blocks):
     depth, rows = line.shape[0], line.shape[1] - PAD
-    cols = mine.shape[1]
     pick = iota((SIX, 2 * RANK), 0) & (RANK - 1)
     pick = (pick + (RANK if of_signals else 0) == iota((SIX, 2 * RANK), 1)).astype(F32).astype(BF16)
     slot = lax.shift_right_logical(iota((SIX, rows), 0), 6)
@@ -188,21 +215,23 @@
         lhs.append(jnp.where(slot == ids, spread, 0.0).astype(BF16))
     values = jnp.concatenate([b[...].reshape(-1, b.shape[-1]) for b in blocks], axis=0)
     total = dot32(jnp.concatenate(lhs, axis=1), values)
-    if not of_signals:
-        total = SCALE * total
+    cols = total.shape[1] // LINES
+    left, right = total[:, :cols], total[:, cols:]
     first = place[1] == 0
-    mine[...] = jnp.where(first, total[:, :cols], total[:, cols:])
-    theirs[...] = jnp.where(first, total[:, cols:], total[:, :cols]).astype(BF16)
-
-
-def gradient(of_signals, order, place, line, blocks):
-    cols = blocks[0].shape[-1] // LINES
-    return kernel_call(
-        functools.partial(gradient_kernel, of_signals, order),
-        [((SIX, cols), F32), ((SIX, cols), BF16)],
-        [place],
-        [line, *blocks],
-    )
+    return jnp.where(first, left, right), jnp.where(first, right, left)
+
+
+def up_gradient_kernel(order, place, line, cot_line, mine, theirs):
+    here, there = gradient_terms(False, order, place, line, [cot_line])
+    mine[...] = SCALE * here
+    theirs[...] = (SCALE * there).astype(BF16)
+
+
+def down_gradient_kernel(order, place, line, *refs):
+    blocks, (mine, theirs) = refs[:-2], refs[-2:]
+    here, there = gradient_terms(True, order, place, line, blocks)
+    mine[...] = here
+    theirs[...] = there.astype(BF16)
 
 
 def finish_kernel(place, adapted, results, last, out):
@@ -227,8 +256,8 @@
     far = depth // 2
     s = lax.axis_index("section")
     d = lax.axis_index("dp")
-    z, x = d // LINES, d % LINES
-    place = jnp.stack([z, x, s]).astype(I32)
+    place = jnp.stack([lax.shift_right_logical(d, 1), d & (LINES - 1), s]).astype(I32)
+    plan = placement.reshape(-1)
     lines = [[k * LINES + i for k in range(depth)] for i in range(LINES)]
     rows, width = handed.shape[1:]
     half = rows // 2
@@ -246,24 +275,24 @@
     step = lambda pair: (along_z(pair[0], 1, depth), along_z(pair[1], -1, depth))
     ring_1 = step((own, own))
 
-    slot_below = hosted_slot(placement, jnp.maximum(s - 1, 0), 2)
-    slot_above = hosted_slot(placement, jnp.minimum(s + 1, sections - 1), 0)
-    maps = lambda k: jnp.concatenate([lax.dynamic_index_in_dim(w[0], k, 0, keepdims=False) for w in (down, up)])
-    to_below, to_above = in_order((maps(slot_below), maps(slot_above)), own)
+    to_below, to_above = in_order(
+        copy_call(maps_kernel, [(2 * RANK, width)] * 2, 4, [place, plan], [down[0], up[0]]), own
+    )
     from_above = section_shift(to_below, -1, sections)
     from_below = section_shift(to_above, 1, sections)
     own_down = down[0].reshape(JOBS * RANK, width)
     own_up = up[0].reshape(JOBS * RANK, width)
 
     w_own = frozen[0]
-    w_pair = across_x(in_order((w_own,), own)[0], devices)
-
+    w_pair = across_x(in_order((w_own,), to_below)[0], devices)
+
+    ring_1 = in_order(ring_1, cot_line)
     ring_2 = step(ring_1)
     (own_,) = in_order((own,), ring_1, cot_line, w_pair)
     adapted, sent = kernel_call(
         rows_kernel,
         [((rows, width), BF16), ((depth, rows + PAD, 2 * RANK), BF16)],
-        [place, lengths.reshape(-1), placement.reshape(-1)],
+        [place, lengths.reshape(-1), plan],
         [own_, cot, own_down, own_up, from_above, from_below],
     )
     line = to_line(sent)
@@ -279,7 +308,7 @@
     )
 
     ring_3 = in_order(ring_3, near_columns)
-    half_f, half_r = halves(*ring_3)
+    half_f, half_r = copy_call(halves_kernel, [(half, width)] * 2, 2, [], ring_3)
     last = along_z(half_f, 1, depth), along_z(half_r, -1, depth)
     ring_3 = in_order(ring_3, half_f)
     results, next_columns = kernel_call(
@@ -290,35 +319,41 @@
     )
     (line_,) = in_order((line,), results)
     results = to_line(results)
-    up_parts = gradient(False, tuple(range(depth)), place, line_, [cot_line])
-    last = in_order(last, up_parts)
-    last, far_columns = kernel_call(last_kernel, [((rows, wide), BF16)] * 2, [place], [*last, w_own, w_pair])
+    terms = ((SIX, cols), F32)
+    up_mine, up_theirs = kernel_call(
+        functools.partial(up_gradient_kernel, tuple(range(depth))),
+        [terms, ((SIX, cols), BF16)],
+        [place],
+        [line_, cot_line],
+    )
+    up_theirs = across_x(up_theirs, devices)
+    last = in_order(last, up_mine)
+    last, far_columns = kernel_call(last_kernel, [((rows, wide), BF16)] * 2, [place], [*last, w_own, w_pair], MOVED)
     result_last = along_z(last, far, depth)
-    down_parts = gradient(
-        True, order + (far,), place, line, [near_columns, next_columns, far_columns]
-    )
-
-    (down_mine, down_theirs), (up_mine, up_theirs) = down_parts, up_parts
-    own_rows = JOBS * RANK
-    both = lambda v, w, first, last: jnp.stack([v[first:last], w[first:last]]).astype(BF16)
-    from_pair = across_x(both(down_theirs, up_theirs, 0, own_rows), devices)
-
-    def to_host(first, by):
-        here = both(down_mine, up_mine, first, first + RANK)
-        there = both(down_theirs, up_theirs, first, first + RANK)
-        moves = [(i, i + by) for i in range(sections) if 0 <= i + by < sections]
-        route = [(i * devices + k, j * devices + (k ^ 1)) for i, j in moves for k in range(devices)]
-        return section_shift(here, by, sections).astype(F32) + lax.ppermute(
-            there, ("section", "dp"), route
-        ).astype(F32)
-
-    of_below = to_host(own_rows, 1)
-    of_above = to_host(own_rows + RANK, -1)
+    down_mine, down_theirs = kernel_call(
+        functools.partial(down_gradient_kernel, order + (far,)),
+        [terms, ((SIX, cols), BF16)],
+        [place],
+        [line, near_columns, next_columns, far_columns],
+    )
+    down_theirs = across_x(down_theirs, devices)
+
+    over_pair = lambda mine, theirs: (mine + theirs.astype(F32)).reshape(JOBS + 2, RANK, cols)
+    up_sum, down_sum = over_pair(up_mine, up_theirs), over_pair(down_mine, down_theirs)
+    next_rows, prev_rows = (jnp.stack([down_sum[k], up_sum[k]]).astype(BF16) for k in (JOBS, JOBS + 1))
+    of_below = section_shift(next_rows, 1, sections).astype(F32)
+    of_above = section_shift(prev_rows, -1, sections).astype(F32)
     slots = jnp.arange(JOBS, dtype=I32)[:, None, None]
+
+    def hosted(section, code):
+        jobs = lax.dynamic_index_in_dim(placement, section, 0, keepdims=False)
+        return jnp.sum(jnp.where(jobs[:, 0] == code, jobs[:, 1], 0))
+
+    slot_below, slot_above = hosted(jnp.maximum(s - 1, 0), 2), hosted(jnp.minimum(s + 1, sections - 1), 0)
 
     def gathered(mine, i):
         return (
-            (mine[:own_rows] + from_pair[i].astype(F32)).reshape(JOBS, RANK, cols)
+            mine[:JOBS]
             + jnp.where(slots == slot_below, of_below[i][None], 0.0)
             + jnp.where(slots == slot_above, of_above[i][None], 0.0)
         )[None]
@@ -326,7 +361,7 @@
     (passed,) = kernel_call(
         finish_kernel, [((rows, width), BF16)], [place], [adapted, results, result_last]
     )
-    return passed[None], gathered(down_mine, 0), gathered(up_mine, 1)
+    return passed[None], gathered(down_sum, 0), gathered(up_sum, 1)
 
 
 def solution(mesh):

time: 176 us -> 177 us (level)
  the two profiles are of different devices: /device:TPU:6 before, /device:TPU:25 now
where the time goes in v4:
time: 177 us; the launch traced here: 176 us
  waiting for transfers between devices  63.7 us (36%)
  starting transfers between devices  63.4 us (36%)
  Pallas kernels  27.4 us (15%)
  local copies, waits for them, and re-layouts  16.4 us (9%)
  other arithmetic  4.12 us (2%)
    ppermute x9, waiting for transfers between devices, along_z(): return lax.ppermute(value, 'dp', route)  36.4 us
    pallas_call x8, Pallas kernels, kernel_call(): pl.pallas_call(kernel, out_shape=tuple((jax.ShapeDtypeStruct(shape, dtype...  23.1 us
    all_to_all x3, starting transfers between devices, to_line(): lax.all_to_all(value, 'dp', 0, 0, axis_index_groups=lines, tiled=True)  21.5 us
    ppermute x4, starting transfers between devices, section_shift(): return lax.ppermute(value, 'section', route)  19 us
    ppermute x9, starting transfers between devices, along_z(): return lax.ppermute(value, 'dp', route)  18.3 us
    unnamed x43, local copies, waits for them, and re-layouts  15.9 us
    ppermute x4, waiting for transfers between devices, section_shift(): return lax.ppermute(value, 'section', route)  13.2 us
    all_to_all x3, waiting for transfers between devices, to_line(): lax.all_to_all(value, 'dp', 0, 0, axis_index_groups=lines, tiled=True)  9.29 us
  transfers between devices with their start and end apart: 20, of which 8 were waited for; matrix products, arithmetic and copies ran while one was open for 3% of the time, Pallas kernels for 14%

profile of v4, /device:TPU:25, one launch (start us, length us, event | category | flops | bytes accessed | tf_op | source)
XLA Modules:
  0.0 175.9 jit_solution(2975992878347982775)
XLA Ops:
  0.6 3.0 %collective-permute-start = (bf16[128,4096]{1,0:T(8,128)(2,1)}, bf16[128,4096]{1,0:T(8,128)(2,1)S(1)}, u32[]{:S(2)}, u32[]{:S(2)}) collective-permute-start(bf16[128,4096]{1,0:T(8,128)(2,1)} %bitcast.48), channel_id=1, source_target_pairs={{0,16},{16,32},{32,48},{48,64},{64,80},{80,96},{96,112},{112,128},... | collective-permute-start | bytes 3145736 | tf_op jit(solution)/shard_map/ppermute | solution.py:268
  3.7 1.2 copy-done.5
  4.9 1.0 shard_map.94
  5.9 8.2 %all-to-all-start = ((bf16[8,128,512]{2,1,0:T(8,128)(2,1)}), bf16[8,128,512]{2,1,0:T(8,128)(2,1)}, u32[]{:S(2)}, u32[]{:S(2)}) async-start(bf16[8,128,512]{2,1,0:T(8,128)(2,1)} %shard_map.94), calls=%async_computation | async-start | bytes 2097152 | tf_op jit(solution)/shard_map/all_to_all | solution.py:271
  14.5 1.6 copy-done.1
  16.1 1.6 copy-done.3
  17.7 2.1 %shard_map.95 = (bf16[128,4096]{1,0:T(8,128)(2,1)}, bf16[128,4096]{1,0:T(8,128)(2,1)}) custom-call(s32[3]{0:T(128)S(1)} %pad_add_fusion.place, s32[128]{0:T(128)S(1)} %reshape.81.plan, bf16[4,64,4096]{2,1,0:T(8,128)(2,1)S(1)} %bitcast.36, bf16[4,64,4096]{2,1,0:T(8,128)(2,1)S(1)} %bitcast.38), custom_call_target="tpu_custom_call" | custom-call | flops 1024 | bytes 1024 | tf_op jit(solution)/shard_map/pallas_call | solution.py:73
  20.2 1.5 collective-permute-start.1
  21.7 1.2 collective-permute-start.2
  22.9 2.2 %collective-permute-start.4 = (bf16[128,4096]{1,0:T(8,128)(2,1)}, bf16[128,4096]{1,0:T(8,128)(2,1)}, u32[]{:S(2)}, u32[]{:S(2)}) collective-permute-start(bf16[128,4096]{1,0:T(8,128)(2,1)} %get-tuple-element.38), channel_id=1, source_target_pairs={{16,0},{32,16},{48,32},{64,48},{80,64},{96,80},{112,96},{128,112},... | collective-permute-start | bytes 3145736 | tf_op jit(solution)/shard_map/ppermute | solution.py:40
  25.1 7.5 %collective-permute-start.5 = (bf16[128,4096]{1,0:T(8,128)(2,1)}, bf16[128,4096]{1,0:T(8,128)(2,1)}, u32[]{:S(2)}, u32[]{:S(2)}) collective-permute-start(bf16[128,4096]{1,0:T(8,128)(2,1)} %get-tuple-element.41), channel_id=1, source_target_pairs={{0,16},{16,32},{32,48},{48,64},{64,80},{80,96},{96,112},{112,128},... | collective-permute-start | bytes 3145736 | tf_op jit(solution)/shard_map/ppermute | solution.py:40
  32.6 9.3 %all-to-all-done.cot_line = bf16[8,128,512]{2,1,0:T(8,128)(2,1)} async-done(((bf16[8,128,512]{2,1,0:T(8,128)(2,1)}), bf16[8,128,512]{2,1,0:T(8,128)(2,1)}, u32[]{:S(2)}, u32[]{:S(2)}) %all-to-all-start) | async-done | bytes 1048608 | tf_op jit(solution)/shard_map/all_to_all | solution.py:271
  41.9 19.6 %collective-permute-done.1.refs_1_ = bf16[128,4096]{1,0:T(8,128)(2,1)} collective-permute-done((bf16[128,4096]{1,0:T(8,128)(2,1)S(1)}, bf16[128,4096]{1,0:T(8,128)(2,1)}, u32[]{:S(2)}, u32[]{:S(2)}) %collective-permute-start.1) | collective-permute-done | bytes 1048608 | tf_op jit(solution)/shard_map/ppermute | solution.py:31
  61.7 2.4 %collective-permute-start.7 = (bf16[128,4096]{1,0:T(8,128)(2,1)}, bf16[128,4096]{1,0:T(8,128)(2,1)}, u32[]{:S(2)}, u32[]{:S(2)}) collective-permute-start(bf16[128,4096]{1,0:T(8,128)(2,1)} %collective-permute-done.2.refs_2_), channel_id=1, source_target_pairs={{0,14},{1,15},{2,0},{3,1},{4,2},{5,3},{6,4},{7,5},{8,6},{9,7},{10,... | collective-permute-start | bytes 3145736 | tf_op jit(solution)/shard_map/ppermute | solution.py:31
  64.2 2.0 %collective-permute-done.3.refs_6_.w_pair = bf16[4096,256]{1,0:T(8,128)(2,1)} collective-permute-done((bf16[4096,256]{1,0:T(8,128)(2,1)S(1)}, bf16[4096,256]{1,0:T(8,128)(2,1)}, u32[]{:S(2)}, u32[]{:S(2)}) %collective-permute-start.3) | collective-permute-done | bytes 2097184 | tf_op jit(solution)/shard_map/ppermute | solution.py:35
  66.1 13.2 %collective-permute-done.4.above = bf16[128,4096]{1,0:T(8,128)(2,1)} collective-permute-done((bf16[128,4096]{1,0:T(8,128)(2,1)}, bf16[128,4096]{1,0:T(8,128)(2,1)}, u32[]{:S(2)}, u32[]{:S(2)}) %collective-permute-start.4) | collective-permute-done | bytes 1048608 | tf_op jit(solution)/shard_map/ppermute | solution.py:40
  79.4 1.6 copy-done.2
  81.0 1.6 copy-done.4
  82.6 1.2 copy-done.6
  83.8 4.1 %shard_map.96 = (bf16[128,4096]{1,0:T(8,128)(2,1)S(1)}, bf16[8,144,128]{2,1,0:T(8,128)(2,1)S(1)}) custom-call(s32[3]{0:T(128)S(1)} %pad_add_fusion.place, s32[4]{0:T(128)S(1)} %bitcast.42, s32[128]{0:T(128)S(1)} %reshape.81.plan, bf16[128,4096]{1,0:T(8,128)(2,1)S(1)} %collective-permute-done.own_x.refs_0_, bf16[128,4096]{1,0:T(8,128)(2,1)S(1)} %bitcast.41, ...), custom_call_target="tpu_custom_call" | custom-call | flops 1024 | bytes 1024 | tf_op jit(solution)/shard_map/pallas_call | solution.py:90
  87.9 1.0 copy-done.7
  89.6 1.5 collective-permute-start.8
  91.1 1.3 collective-permute-start.9
  92.4 6.6 %all-to-all-start.2 = ((bf16[8,144,128]{2,1,0:T(8,128)(2,1)}), bf16[8,144,128]{2,1,0:T(8,128)(2,1)S(1)}, u32[]{:S(2)}, u32[]{:S(2)}) async-start(bf16[8,144,128]{2,1,0:T(8,128)(2,1)} %copy-done.16), calls=%async_computation.2 | async-start | bytes 589824 | tf_op jit(solution)/shard_map/all_to_all | solution.py:271
  98.9 5.7 %shard_map.97 = (bf16[5,128,512]{2,1,0:T(8,128)(2,1)S(1)}, bf16[5,128,512]{2,1,0:T(8,128)(2,1)S(1)}) custom-call(s32[3]{0:T(128)S(1)} %pad_add_fusion.place, bf16[128,4096]{1,0:T(8,128)(2,1)S(1)} %collective-permute-done.own_x.refs_0_, bf16[128,4096]{1,0:T(8,128)(2,1)} %collective-permute-done.1.refs_1_, bf16[128,4096]{1,0:T(8,128)(2,1)} %collective-permute-done.2.refs_2_, ...), custom_call_target="tpu_custom_call" | custom-call | flops 1024 | bytes 1024 | tf_op jit(solution)/shard_map/pallas_call | solution.py:90
  104.7 0.8 copy-done.10
  105.5 0.8 copy-done.12
  106.4 10.2 %collective-permute-done.8.f3 = bf16[128,4096]{1,0:T(8,128)(2,1)} collective-permute-done((bf16[128,4096]{1,0:T(8,128)(2,1)}, bf16[128,4096]{1,0:T(8,128)(2,1)}, u32[]{:S(2)}, u32[]{:S(2)}) %collective-permute-start.8) | collective-permute-done | bytes 1048608 | tf_op jit(solution)/shard_map/ppermute | solution.py:31
  117.1 2.2 %shard_map.98 = (bf16[64,4096]{1,0:T(8,128)(2,1)}, bf16[64,4096]{1,0:T(8,128)(2,1)}) custom-call(bf16[128,4096]{1,0:T(8,128)(2,1)} %collective-permute-done.8.f3, bf16[128,4096]{1,0:T(8,128)(2,1)} %collective-permute-done.9.r3), custom_call_target="tpu_custom_call" | custom-call | flops 1024 | bytes 1024 | tf_op jit(solution)/shard_map/pallas_call | solution.py:73
  119.3 1.6 collective-permute-start.10
  120.9 2.9 %collective-permute-start.11 = (bf16[64,4096]{1,0:T(8,128)(2,1)}, bf16[64,4096]{1,0:T(8,128)(2,1)}, u32[]{:S(2)}, u32[]{:S(2)}) collective-permute-start(bf16[64,4096]{1,0:T(8,128)(2,1)} %get-tuple-element.54), channel_id=1, source_target_pairs={{0,14},{1,15},{2,0},{3,1},{4,2},{5,3},{6,4},{7,5},{8,6},{9,7},{10,... | collective-permute-start | bytes 1572872 | tf_op jit(solution)/shard_map/ppermute | solution.py:31
  124.1 1.1 copy-done.13
  125.2 3.5 %shard_map.99 = (bf16[8,128,512]{2,1,0:T(8,128)(2,1)S(1)}, bf16[2,128,512]{2,1,0:T(8,128)(2,1)S(1)}) custom-call(s32[3]{0:T(128)S(1)} %pad_add_fusion.place, bf16[5,128,512]{2,1,0:T(8,128)(2,1)S(1)} %copy-done.13, bf16[128,4096]{1,0:T(8,128)(2,1)} %collective-permute-done.8.f3, bf16[128,4096]{1,0:T(8,128)(2,1)} %collective-permute-done.9.r3, ...), custom_call_target="tpu_custom_call" | custom-call | flops 1024 | bytes 1024 | tf_op jit(solution)/shard_map/pallas_call | solution.py:90
  128.7 1.0 copy-done.9
  130.4 2.7 %shard_map.100 = (f32[384,256]{1,0:T(8,128)S(1)}, bf16[384,256]{1,0:T(8,128)(2,1)}) custom-call(s32[3]{0:T(128)S(1)} %pad_add_fusion.place, bf16[8,144,128]{2,1,0:T(8,128)(2,1)S(1)} %all-to-all-done.2.line, bf16[8,128,512]{2,1,0:T(8,128)(2,1)} %all-to-all-done.cot_line), custom_call_target="tpu_custom_call" | custom-call | flops 1024 | bytes 1024 | tf_op jit(solution)/shard_map/pallas_call | solution.py:90
  133.1 0.8 copy-done.14
  134.5 6.8 %all-to-all-start.1 = ((bf16[8,128,512]{2,1,0:T(8,128)(2,1)}), bf16[8,128,512]{2,1,0:T(8,128)(2,1)S(1)}, u32[]{:S(2)}, u32[]{:S(2)}) async-start(bf16[8,128,512]{2,1,0:T(8,128)(2,1)} %copy-done.9), calls=%async_computation.1 | async-start | bytes 2097152 | tf_op jit(solution)/shard_map/all_to_all | solution.py:271
  142.1 2.7 %shard_map.101 = (bf16[128,512]{1,0:T(8,128)(2,1)S(1)}, bf16[128,512]{1,0:T(8,128)(2,1)S(1)}) custom-call(s32[3]{0:T(128)S(1)} %pad_add_fusion.place, bf16[64,4096]{1,0:T(8,128)(2,1)} %collective-permute-done.10.first_half, bf16[64,4096]{1,0:T(8,128)(2,1)} %collective-permute-done.11.second_half, bf16[4096,256]{1,0:T(8,128)(2,1)S(1)} %bitcast.35, ...), custom_call_target="tpu_custom_call" | custom-call | flops 1024 | bytes 1048576 | tf_op jit(solution)/shard_map/pallas_call | solution.py:90
  144.9 1.3 shard_map.103
  146.2 1.1 collective-permute-start.13
  147.3 1.0 fusion.3
  148.3 2.8 %collective-permute-done.13 = bf16[384,256]{1,0:T(8,128)(2,1)S(1)} collective-permute-done((bf16[384,256]{1,0:T(8,128)(2,1)S(1)}, bf16[384,256]{1,0:T(8,128)(2,1)S(1)}, u32[]{:S(2)}, u32[]{:S(2)}) %collective-permute-start.13) | collective-permute-done | bytes 196640 | tf_op jit(solution)/shard_map/ppermute | solution.py:35
  151.2 2.1 %collective-permute-start.16 = (bf16[2,64,256]{2,1,0:T(8,128)(2,1)S(1)}, bf16[2,64,256]{2,1,0:T(8,128)(2,1)S(1)}, u32[]{:S(2)}, u32[]{:S(2)}) collective-permute-start(bf16[2,64,256]{2,1,0:T(8,128)(2,1)S(1)} %pad_maximum_fusion.1), channel_id=1, source_target_pairs={{16,0},{32,16},{48,32},{64,48},{80,64},{96,80},{112,96},{128,112},... | collective-permute-start | bytes 196616 | tf_op jit(solution)/shard_map/ppermute | solution.py:40
  153.3 7.3 %collective-permute-start.15 = (bf16[2,64,256]{2,1,0:T(8,128)(2,1)S(1)}, bf16[2,64,256]{2,1,0:T(8,128)(2,1)S(1)}, u32[]{:S(2)}, u32[]{:S(2)}) collective-permute-start(bf16[2,64,256]{2,1,0:T(8,128)(2,1)S(1)} %pad_maximum_fusion), channel_id=1, source_target_pairs={{0,16},{16,32},{32,48},{48,64},{64,80},{80,96},{96,112},{112,128},... | collective-permute-start | bytes 196616 | tf_op jit(solution)/shard_map/ppermute | solution.py:40
  161.2 5.7 %collective-permute-start.12 = (bf16[128,512]{1,0:T(8,128)(2,1)S(1)}, bf16[128,512]{1,0:T(8,128)(2,1)S(1)}, u32[]{:S(2)}, u32[]{:S(2)}) collective-permute-start(bf16[128,512]{1,0:T(8,128)(2,1)S(1)} %get-tuple-element.59), channel_id=1, source_target_pairs={{0,8},{1,9},{2,10},{3,11},{4,12},{5,13},{6,14},{7,15},{8,0},{9,1},... | collective-permute-start | bytes 393224 | tf_op jit(solution)/shard_map/ppermute | solution.py:31
  167.0 0.9 select_add_fusion
  168.0 6.1 %collective-permute-done.12.last = bf16[128,512]{1,0:T(8,128)(2,1)S(1)} collective-permute-done((bf16[128,512]{1,0:T(8,128)(2,1)S(1)}, bf16[128,512]{1,0:T(8,128)(2,1)S(1)}, u32[]{:S(2)}, u32[]{:S(2)}) %collective-permute-start.12) | collective-permute-done | bytes 131104 | tf_op jit(solution)/shard_map/ppermute | solution.py:31
  174.0 1.9 %shard_map.102 = bf16[128,4096]{1,0:T(8,128)(2,1)} custom-call(s32[3]{0:T(128)S(1)} %pad_add_fusion.place, bf16[128,4096]{1,0:T(8,128)(2,1)S(1)} %copy-done.8, bf16[8,128,512]{2,1,0:T(8,128)(2,1)S(1)} %all-to-all-done.1.results, bf16[128,512]{1,0:T(8,128)(2,1)S(1)} %collective-permute-done.12.last), custom_call_target="tpu_custom_call" | custom-call | flops 1024 | bytes 1024 | tf_op jit(solution)/shard_map/pallas_call | solution.py:90
  (65 shorter events, 5.5 us)
Async XLA Ops:
  0.6 19.2 %collective-permute-start = (bf16[128,4096]{1,0:T(8,128)(2,1)}, bf16[128,4096]{1,0:T(8,128)(2,1)S(1)}, u32[]{:S(2)}, u32[]{:S(2)}) collective-permute-start(bf16[128,4096]{1,0:T(8,128)(2,1)} %bitcast.48), channel_id=1, source_target_pairs={{0,16},{16,32},{32,48},{48,64},{64,80},{80,96},{96,112},{112,128},... | collective-permute-start | bytes 3145736 | tf_op jit(solution)/shard_map/ppermute | solution.py:268
  3.7 1.2 copy-start.5
  4.9 9.2 %copy-start.20 = (s32[16,4,2]{0,2,1:T(2,128)S(1)}, s32[16,4,2]{0,2,1:T(2,128)}, u32[]{:S(2)}) copy-start(s32[16,4,2]{0,2,1:T(2,128)} %param.9) | copy-start | bytes 1540
  5.9 36.0 %all-to-all-start = ((bf16[8,128,512]{2,1,0:T(8,128)(2,1)}), bf16[8,128,512]{2,1,0:T(8,128)(2,1)}, u32[]{:S(2)}, u32[]{:S(2)}) async-start(bf16[8,128,512]{2,1,0:T(8,128)(2,1)} %shard_map.94), calls=%async_computation | async-start | bytes 2097152 | tf_op jit(solution)/shard_map/all_to_all | solution.py:271
  14.5 1.6 copy-start.1
  16.1 1.6 copy-start.3
  17.7 2.2 %copy-start = (bf16[1,4096,256]{2,1,0:T(8,128)(2,1)S(1)}, bf16[1,4096,256]{2,1,0:T(8,128)(2,1)}, u32[]{:S(2)}) copy-start(bf16[1,4096,256]{2,1,0:T(8,128)(2,1)} %param.10) | copy-start | bytes 6291460
  17.7 61.7 %copy-start.19 = (s32[1,1,4]{2,1,0:T(1,128)S(1)}, s32[1,1,4]{2,1,0:T(1,128)}, u32[]{:S(2)}) copy-start(s32[1,1,4]{2,1,0:T(1,128)} %param.8) | copy-start | bytes 52
  19.8 46.3 %collective-permute-start.3 = (bf16[4096,256]{1,0:T(8,128)(2,1)S(1)}, bf16[4096,256]{1,0:T(8,128)(2,1)}, u32[]{:S(2)}, u32[]{:S(2)}) collective-permute-start(bf16[4096,256]{1,0:T(8,128)(2,1)S(1)} %bitcast.32), channel_id=1, source_target_pairs={{0,1},{1,0},{2,3},{3,2},{4,5},{5,4},{6,7},{7,6},{8,9},{9,8},{10,11... | collective-permute-start | bytes 6291464 | tf_op jit(solution)/shard_map/ppermute | solution.py:35
  20.2 41.2 %collective-permute-start.1 = (bf16[128,4096]{1,0:T(8,128)(2,1)S(1)}, bf16[128,4096]{1,0:T(8,128)(2,1)}, u32[]{:S(2)}, u32[]{:S(2)}) collective-permute-start(bf16[128,4096]{1,0:T(8,128)(2,1)S(1)} %collective-permute-done.own_x.refs_0_), channel_id=1, source_target_pairs={{0,2},{1,3},{2,4},{3,5},{4,6},{5,7},{6,8},{7,9},{8,10},{9,11},{10,... | collective-permute-start | bytes 3145736 | tf_op jit(solution)/shard_map/ppermute | solution.py:31
  21.7 39.8 %collective-permute-start.2 = (bf16[128,4096]{1,0:T(8,128)(2,1)S(1)}, bf16[128,4096]{1,0:T(8,128)(2,1)}, u32[]{:S(2)}, u32[]{:S(2)}) collective-permute-start(bf16[128,4096]{1,0:T(8,128)(2,1)S(1)} %collective-permute-done.own_x.refs_0_), channel_id=1, source_target_pairs={{0,14},{1,15},{2,0},{3,1},{4,2},{5,3},{6,4},{7,5},{8,6},{9,7},{10,... | collective-permute-start | bytes 3145736 | tf_op jit(solution)/shard_map/ppermute | solution.py:31
  22.9 56.5 %collective-permute-start.4 = (bf16[128,4096]{1,0:T(8,128)(2,1)}, bf16[128,4096]{1,0:T(8,128)(2,1)}, u32[]{:S(2)}, u32[]{:S(2)}) collective-permute-start(bf16[128,4096]{1,0:T(8,128)(2,1)} %get-tuple-element.38), channel_id=1, source_target_pairs={{16,0},{32,16},{48,32},{64,48},{80,64},{96,80},{112,96},{128,112},... | collective-permute-start | bytes 3145736 | tf_op jit(solution)/shard_map/ppermute | solution.py:40
  25.1 54.3 %collective-permute-start.5 = (bf16[128,4096]{1,0:T(8,128)(2,1)}, bf16[128,4096]{1,0:T(8,128)(2,1)}, u32[]{:S(2)}, u32[]{:S(2)}) collective-permute-start(bf16[128,4096]{1,0:T(8,128)(2,1)} %get-tuple-element.41), channel_id=1, source_target_pairs={{0,16},{16,32},{32,48},{48,64},{64,80},{80,96},{96,112},{112,128},... | collective-permute-start | bytes 3145736 | tf_op jit(solution)/shard_map/ppermute | solution.py:40
  61.5 28.1 %collective-permute-start.6 = (bf16[128,4096]{1,0:T(8,128)(2,1)}, bf16[128,4096]{1,0:T(8,128)(2,1)}, u32[]{:S(2)}, u32[]{:S(2)}) collective-permute-start(bf16[128,4096]{1,0:T(8,128)(2,1)} %collective-permute-done.1.refs_1_), channel_id=1, source_target_pairs={{0,2},{1,3},{2,4},{3,5},{4,6},{5,7},{6,8},{7,9},{8,10},{9,11},{10,... | collective-permute-start | bytes 3145736 | tf_op jit(solution)/shard_map/ppermute | solution.py:31
  61.7 27.9 %collective-permute-start.7 = (bf16[128,4096]{1,0:T(8,128)(2,1)}, bf16[128,4096]{1,0:T(8,128)(2,1)}, u32[]{:S(2)}, u32[]{:S(2)}) collective-permute-start(bf16[128,4096]{1,0:T(8,128)(2,1)} %collective-permute-done.2.refs_2_), channel_id=1, source_target_pairs={{0,14},{1,15},{2,0},{3,1},{4,2},{5,3},{6,4},{7,5},{8,6},{9,7},{10,... | collective-permute-start | bytes 3145736 | tf_op jit(solution)/shard_map/ppermute | solution.py:31
  79.4 1.6 copy-start.2
  81.0 1.6 copy-start.4
  82.5 1.2 copy-start.6
  87.9 1.0 copy-start.7
  88.9 0.7 copy-start.16
  89.6 27.0 %collective-permute-start.8 = (bf16[128,4096]{1,0:T(8,128)(2,1)}, bf16[128,4096]{1,0:T(8,128)(2,1)}, u32[]{:S(2)}, u32[]{:S(2)}) collective-permute-start(bf16[128,4096]{1,0:T(8,128)(2,1)} %collective-permute-done.6.refs_3_), channel_id=1, source_target_pairs={{0,2},{1,3},{2,4},{3,5},{4,6},{5,7},{6,8},{7,9},{8,10},{9,11},{10,... | collective-permute-start | bytes 3145736 | tf_op jit(solution)/shard_map/ppermute | solution.py:31
  91.1 26.0 %collective-permute-start.9 = (bf16[128,4096]{1,0:T(8,128)(2,1)}, bf16[128,4096]{1,0:T(8,128)(2,1)}, u32[]{:S(2)}, u32[]{:S(2)}) collective-permute-start(bf16[128,4096]{1,0:T(8,128)(2,1)} %collective-permute-done.7.refs_4_), channel_id=1, source_target_pairs={{0,14},{1,15},{2,0},{3,1},{4,2},{5,3},{6,4},{7,5},{8,6},{9,7},{10,... | collective-permute-start | bytes 3145736 | tf_op jit(solution)/shard_map/ppermute | solution.py:31
  92.4 38.0 %all-to-all-start.2 = ((bf16[8,144,128]{2,1,0:T(8,128)(2,1)}), bf16[8,144,128]{2,1,0:T(8,128)(2,1)S(1)}, u32[]{:S(2)}, u32[]{:S(2)}) async-start(bf16[8,144,128]{2,1,0:T(8,128)(2,1)} %copy-done.16), calls=%async_computation.2 | async-start | bytes 589824 | tf_op jit(solution)/shard_map/all_to_all | solution.py:271
  104.7 0.8 copy-start.10
  105.5 0.8 copy-start.12
  119.3 22.8 %collective-permute-start.10 = (bf16[64,4096]{1,0:T(8,128)(2,1)}, bf16[64,4096]{1,0:T(8,128)(2,1)}, u32[]{:S(2)}, u32[]{:S(2)}) collective-permute-start(bf16[64,4096]{1,0:T(8,128)(2,1)} %get-tuple-element.50), channel_id=1, source_target_pairs={{0,2},{1,3},{2,4},{3,5},{4,6},{5,7},{6,8},{7,9},{8,10},{9,11},{10,... | collective-permute-start | bytes 1572872 | tf_op jit(solution)/shard_map/ppermute | solution.py:31
  120.9 21.2 %collective-permute-start.11 = (bf16[64,4096]{1,0:T(8,128)(2,1)}, bf16[64,4096]{1,0:T(8,128)(2,1)}, u32[]{:S(2)}, u32[]{:S(2)}) collective-permute-start(bf16[64,4096]{1,0:T(8,128)(2,1)} %get-tuple-element.54), channel_id=1, source_target_pairs={{0,14},{1,15},{2,0},{3,1},{4,2},{5,3},{6,4},{7,5},{8,6},{9,7},{10,... | collective-permute-start | bytes 1572872 | tf_op jit(solution)/shard_map/ppermute | solution.py:31
  124.1 1.1 copy-start.13
  128.7 1.0 copy-start.9
  129.7 0.7 copy-start.17
  133.1 0.8 copy-start.14
  133.8 13.5 %collective-permute-start.14 = (bf16[384,256]{1,0:T(8,128)(2,1)}, bf16[384,256]{1,0:T(8,128)(2,1)}, u32[]{:S(2)}, u32[]{:S(2)}) collective-permute-start(bf16[384,256]{1,0:T(8,128)(2,1)} %get-tuple-element.64), channel_id=1, source_target_pairs={{0,1},{1,0},{2,3},{3,2},{4,5},{5,4},{6,7},{7,6},{8,9},{9,8},{10,11... | collective-permute-start | bytes 589832 | tf_op jit(solution)/shard_map/ppermute | solution.py:35
  134.5 39.5 %all-to-all-start.1 = ((bf16[8,128,512]{2,1,0:T(8,128)(2,1)}), bf16[8,128,512]{2,1,0:T(8,128)(2,1)S(1)}, u32[]{:S(2)}, u32[]{:S(2)}) async-start(bf16[8,128,512]{2,1,0:T(8,128)(2,1)} %copy-done.9), calls=%async_computation.1 | async-start | bytes 2097152 | tf_op jit(solution)/shard_map/all_to_all | solution.py:271
  142.1 2.8 %copy-start.11 = (bf16[5,128,512]{2,1,0:T(8,128)(2,1)S(1)}, bf16[5,128,512]{2,1,0:T(8,128)(2,1)}, u32[]{:S(2)}) copy-start(bf16[5,128,512]{2,1,0:T(8,128)(2,1)} %copy-done.10) | copy-start | bytes 1966084
  142.1 2.8 %copy-start.18 = (bf16[2,128,512]{2,1,0:T(8,128)(2,1)S(1)}, bf16[2,128,512]{2,1,0:T(8,128)(2,1)}, u32[]{:S(2)}) copy-start(bf16[2,128,512]{2,1,0:T(8,128)(2,1)} %copy-done.17) | copy-start | bytes 786436
  142.1 5.2 %copy-start.15 = (f32[384,256]{1,0:T(8,128)S(1)}, f32[384,256]{1,0:T(8,128)}, u32[]{:S(2)}) copy-start(f32[384,256]{1,0:T(8,128)} %copy-done.14) | copy-start | bytes 1179652
  146.2 4.9 %collective-permute-start.13 = (bf16[384,256]{1,0:T(8,128)(2,1)S(1)}, bf16[384,256]{1,0:T(8,128)(2,1)S(1)}, u32[]{:S(2)}, u32[]{:S(2)}) collective-permute-start(bf16[384,256]{1,0:T(8,128)(2,1)S(1)} %get-tuple-element.63), channel_id=1, source_target_pairs={{0,1},{1,0},{2,3},{3,2},{4,5},{5,4},{6,7},{7,6},{8,9},{9,8},{10,11... | collective-permute-start | bytes 589832 | tf_op jit(solution)/shard_map/ppermute | solution.py:35
  151.1 22.9 %copy-start.8 = (bf16[128,4096]{1,0:T(8,128)(2,1)S(1)}, bf16[128,4096]{1,0:T(8,128)(2,1)}, u32[]{:S(2)}) copy-start(bf16[128,4096]{1,0:T(8,128)(2,1)} %copy-done.7) | copy-start | bytes 3145732
  151.2 15.7 %collective-permute-start.16 = (bf16[2,64,256]{2,1,0:T(8,128)(2,1)S(1)}, bf16[2,64,256]{2,1,0:T(8,128)(2,1)S(1)}, u32[]{:S(2)}, u32[]{:S(2)}) collective-permute-start(bf16[2,64,256]{2,1,0:T(8,128)(2,1)S(1)} %pad_maximum_fusion.1), channel_id=1, source_target_pairs={{16,0},{32,16},{48,32},{64,48},{80,64},{96,80},{112,96},{128,112},... | collective-permute-start | bytes 196616 | tf_op jit(solution)/shard_map/ppermute | solution.py:40
  153.3 13.7 %collective-permute-start.15 = (bf16[2,64,256]{2,1,0:T(8,128)(2,1)S(1)}, bf16[2,64,256]{2,1,0:T(8,128)(2,1)S(1)}, u32[]{:S(2)}, u32[]{:S(2)}) collective-permute-start(bf16[2,64,256]{2,1,0:T(8,128)(2,1)S(1)} %pad_maximum_fusion), channel_id=1, source_target_pairs={{0,16},{16,32},{32,48},{48,64},{64,80},{80,96},{96,112},{112,128},... | collective-permute-start | bytes 196616 | tf_op jit(solution)/shard_map/ppermute | solution.py:40
  161.2 12.8 %collective-permute-start.12 = (bf16[128,512]{1,0:T(8,128)(2,1)S(1)}, bf16[128,512]{1,0:T(8,128)(2,1)S(1)}, u32[]{:S(2)}, u32[]{:S(2)}) collective-permute-start(bf16[128,512]{1,0:T(8,128)(2,1)S(1)} %get-tuple-element.59), channel_id=1, source_target_pairs={{0,8},{1,9},{2,10},{3,11},{4,12},{5,13},{6,14},{7,15},{8,0},{9,1},... | collective-permute-start | bytes 393224 | tf_op jit(solution)/shard_map/ppermute | solution.py:31

commit v5 on v4

--- a/solution.py
+++ b/solution.py
@@ -228,10 +228,16 @@
 
 
 def down_gradient_kernel(order, place, line, *refs):
-    blocks, (mine, theirs) = refs[:-2], refs[-2:]
+    blocks, (up_mine, up_theirs, mine, pair, *guests) = refs[:-8], refs[-8:]
     here, there = gradient_terms(True, order, place, line, blocks)
     mine[...] = here
-    theirs[...] = there.astype(BF16)
+    own = JOBS * RANK
+    pair[0] = there[:own].astype(BF16)
+    pair[1] = up_theirs[:own]
+    for i, (kept, sent) in enumerate((guests[:2], guests[2:])):
+        rows = slice(own + i * RANK, own + (i + 1) * RANK)
+        kept[0], kept[1] = here[rows].astype(BF16), up_mine[rows].astype(BF16)
+        sent[0], sent[1] = there[rows].astype(BF16), up_theirs[rows]
 
 
 def finish_kernel(place, adapted, results, last, out):
@@ -284,7 +290,7 @@
     own_up = up[0].reshape(JOBS * RANK, width)
 
     w_own = frozen[0]
-    w_pair = across_x(in_order((w_own,), to_below)[0], devices)
+    w_pair = across_x(in_order((w_own,), own)[0], devices)
 
     ring_1 = in_order(ring_1, cot_line)
     ring_2 = step(ring_1)
@@ -326,23 +332,27 @@
         [place],
         [line_, cot_line],
     )
-    up_theirs = across_x(up_theirs, devices)
     last = in_order(last, up_mine)
     last, far_columns = kernel_call(last_kernel, [((rows, wide), BF16)] * 2, [place], [*last, w_own, w_pair], MOVED)
     result_last = along_z(last, far, depth)
-    down_mine, down_theirs = kernel_call(
+    own_rows = JOBS * RANK
+    guest = ((2, RANK, cols), BF16)
+    down_mine, pair, next_here, next_there, prev_here, prev_there = kernel_call(
         functools.partial(down_gradient_kernel, order + (far,)),
-        [terms, ((SIX, cols), BF16)],
+        [terms, ((2, own_rows, cols), BF16)] + [guest] * 4,
         [place],
-        [line, near_columns, next_columns, far_columns],
-    )
-    down_theirs = across_x(down_theirs, devices)
-
-    over_pair = lambda mine, theirs: (mine + theirs.astype(F32)).reshape(JOBS + 2, RANK, cols)
-    up_sum, down_sum = over_pair(up_mine, up_theirs), over_pair(down_mine, down_theirs)
-    next_rows, prev_rows = (jnp.stack([down_sum[k], up_sum[k]]).astype(BF16) for k in (JOBS, JOBS + 1))
-    of_below = section_shift(next_rows, 1, sections).astype(F32)
-    of_above = section_shift(prev_rows, -1, sections).astype(F32)
+        [line, near_columns, next_columns, far_columns, up_mine, up_theirs],
+        MOVED,
+    )
+
+    def to_host(here, there, by):
+        moves = [(i, i + by) for i in range(sections) if 0 <= i + by < sections]
+        route = [(i * devices + k, j * devices + (k ^ 1)) for i, j in moves for k in range(devices)]
+        return section_shift(here, by, sections), lax.ppermute(there, ("section", "dp"), route)
+
+    from_pair = across_x(pair, devices).astype(F32)
+    of_below = sum(v.astype(F32) for v in to_host(next_here, next_there, 1))
+    of_above = sum(v.astype(F32) for v in to_host(prev_here, prev_there, -1))
     slots = jnp.arange(JOBS, dtype=I32)[:, None, None]
 
     def hosted(section, code):
@@ -353,7 +363,7 @@
 
     def gathered(mine, i):
         return (
-            mine[:JOBS]
+            (mine[:own_rows] + from_pair[i]).reshape(JOBS, RANK, cols)
             + jnp.where(slots == slot_below, of_below[i][None], 0.0)
             + jnp.where(slots == slot_above, of_above[i][None], 0.0)
         )[None]
@@ -361,7 +371,7 @@
     (passed,) = kernel_call(
         finish_kernel, [((rows, width), BF16)], [place], [adapted, results, result_last]
     )
-    return passed[None], gathered(down_sum, 0), gathered(up_sum, 1)
+    return passed[None], gathered(down_mine, 0), gathered(up_mine, 1)
 
 
 def solution(mesh):

time: 177 us -> 173 us (0.977)
  the two profiles are of different devices: /device:TPU:25 before, /device:TPU:6 now
where the time goes in v5:
time: 173 us; the launch traced here: 172 us
  waiting for transfers between devices  65.1 us (38%)
  starting transfers between devices  61.6 us (36%)
  Pallas kernels  25.7 us (15%)
  local copies, waits for them, and re-layouts  15.5 us (9%)
  other arithmetic  3.2 us (2%)
    ppermute x9, waiting for transfers between devices, along_z(): return lax.ppermute(value, 'dp', route)  31.5 us
    ppermute x9, starting transfers between devices, along_z(): return lax.ppermute(value, 'dp', route)  24.2 us
    pallas_call x8, Pallas kernels, kernel_call(): pl.pallas_call(kernel, out_shape=tuple((jax.ShapeDtypeStruct(shape, dtype...  21.4 us
    all_to_all x3, starting transfers between devices, to_line(): lax.all_to_all(value, 'dp', 0, 0, axis_index_groups=lines, tiled=True)  18.1 us
    unnamed x41, local copies, waits for them, and re-layouts  15 us
    ppermute x4, waiting for transfers between devices, section_shift(): return lax.ppermute(value, 'section', route)  14.7 us
    ppermute x4, starting transfers between devices, section_shift(): return lax.ppermute(value, 'section', route)  12.4 us
    ppermute x1, waiting for transfers between devices, on_device(): lax.ppermute(handed[0], 'section', [(i, (i + 1) % sections) for i in rang...  7.28 us
  transfers between devices with their start and end apart: 21, of which 11 were waited for; matrix products, arithmetic and copies ran while one was open for 2% of the time, Pallas kernels for 14%

profile of v5, /device:TPU:6, one launch (start us, length us, event | category | flops | bytes accessed | tf_op | source)
XLA Modules:
  0.0 172.0 jit_solution(7508974997520827005)
XLA Ops:
  0.7 1.2 copy-done.5
  2.0 1.0 copy-done.7
  3.0 8.5 %all-to-all-start = ((bf16[8,128,512]{2,1,0:T(8,128)(2,1)}), bf16[8,128,512]{2,1,0:T(8,128)(2,1)}, u32[]{:S(2)}, u32[]{:S(2)}) async-start(bf16[8,128,512]{2,1,0:T(8,128)(2,1)} %copy-done.7), calls=%async_computation | async-start | bytes 2097152 | tf_op jit(solution)/shard_map/all_to_all | solution.py:277
  11.5 7.3 %collective-permute-done.own_x.refs_0_ = bf16[128,4096]{1,0:T(8,128)(2,1)S(1)} collective-permute-done((bf16[128,4096]{1,0:T(8,128)(2,1)}, bf16[128,4096]{1,0:T(8,128)(2,1)S(1)}, u32[]{:S(2)}, u32[]{:S(2)}) %collective-permute-start) | collective-permute-done | bytes 1048608 | tf_op jit(solution)/shard_map/ppermute | solution.py:274
  18.8 0.8 collective-permute-start.3
  19.6 1.9 %collective-permute-start.1 = (bf16[128,4096]{1,0:T(8,128)(2,1)S(1)}, bf16[128,4096]{1,0:T(8,128)(2,1)}, u32[]{:S(2)}, u32[]{:S(2)}) collective-permute-start(bf16[128,4096]{1,0:T(8,128)(2,1)S(1)} %collective-permute-done.own_x.refs_0_), channel_id=1, source_target_pairs={{0,2},{1,3},{2,4},{3,5},{4,6},{5,7},{6,8},{7,9},{8,10},{9,11},{10,... | collective-permute-start | bytes 3145736 | tf_op jit(solution)/shard_map/ppermute | solution.py:31
  21.5 3.9 %collective-permute-start.2 = (bf16[128,4096]{1,0:T(8,128)(2,1)S(1)}, bf16[128,4096]{1,0:T(8,128)(2,1)}, u32[]{:S(2)}, u32[]{:S(2)}) collective-permute-start(bf16[128,4096]{1,0:T(8,128)(2,1)S(1)} %collective-permute-done.own_x.refs_0_), channel_id=1, source_target_pairs={{0,14},{1,15},{2,0},{3,1},{4,2},{5,3},{6,4},{7,5},{8,6},{9,7},{10,... | collective-permute-start | bytes 3145736 | tf_op jit(solution)/shard_map/ppermute | solution.py:31
  25.8 1.6 copy-done.1
  27.4 1.6 copy-done.3
  29.0 2.1 %shard_map.95 = (bf16[128,4096]{1,0:T(8,128)(2,1)}, bf16[128,4096]{1,0:T(8,128)(2,1)}) custom-call(s32[3]{0:T(128)S(1)} %pad_add_fusion.place, s32[128]{0:T(128)S(1)} %reshape.75.plan, bf16[4,64,4096]{2,1,0:T(8,128)(2,1)S(1)} %bitcast.36, bf16[4,64,4096]{2,1,0:T(8,128)(2,1)S(1)} %bitcast.38), custom_call_target="tpu_custom_call" | custom-call | flops 1024 | bytes 1024 | tf_op jit(solution)/shard_map/pallas_call | solution.py:73
  31.1 1.9 %collective-permute-start.4 = (bf16[128,4096]{1,0:T(8,128)(2,1)}, bf16[128,4096]{1,0:T(8,128)(2,1)}, u32[]{:S(2)}, u32[]{:S(2)}) collective-permute-start(bf16[128,4096]{1,0:T(8,128)(2,1)} %get-tuple-element.44), channel_id=1, source_target_pairs={{16,0},{32,16},{48,32},{64,48},{80,64},{96,80},{112,96},{128,112},... | collective-permute-start | bytes 3145736 | tf_op jit(solution)/shard_map/ppermute | solution.py:40
  33.0 2.4 %collective-permute-start.5 = (bf16[128,4096]{1,0:T(8,128)(2,1)}, bf16[128,4096]{1,0:T(8,128)(2,1)}, u32[]{:S(2)}, u32[]{:S(2)}) collective-permute-start(bf16[128,4096]{1,0:T(8,128)(2,1)} %get-tuple-element.45), channel_id=1, source_target_pairs={{0,16},{16,32},{32,48},{48,64},{64,80},{80,96},{96,112},{112,128},... | collective-permute-start | bytes 3145736 | tf_op jit(solution)/shard_map/ppermute | solution.py:40
  35.4 6.6 %all-to-all-done.cot_line = bf16[8,128,512]{2,1,0:T(8,128)(2,1)} async-done(((bf16[8,128,512]{2,1,0:T(8,128)(2,1)}), bf16[8,128,512]{2,1,0:T(8,128)(2,1)}, u32[]{:S(2)}, u32[]{:S(2)}) %all-to-all-start) | async-done | bytes 1048608 | tf_op jit(solution)/shard_map/all_to_all | solution.py:277
  42.0 19.2 %collective-permute-done.1.refs_1_ = bf16[128,4096]{1,0:T(8,128)(2,1)} collective-permute-done((bf16[128,4096]{1,0:T(8,128)(2,1)S(1)}, bf16[128,4096]{1,0:T(8,128)(2,1)}, u32[]{:S(2)}, u32[]{:S(2)}) %collective-permute-start.1) | collective-permute-done | bytes 1048608 | tf_op jit(solution)/shard_map/ppermute | solution.py:31
  61.4 3.0 %collective-permute-start.7 = (bf16[128,4096]{1,0:T(8,128)(2,1)}, bf16[128,4096]{1,0:T(8,128)(2,1)}, u32[]{:S(2)}, u32[]{:S(2)}) collective-permute-start(bf16[128,4096]{1,0:T(8,128)(2,1)} %collective-permute-done.2.refs_2_), channel_id=1, source_target_pairs={{0,14},{1,15},{2,0},{3,1},{4,2},{5,3},{6,4},{7,5},{8,6},{9,7},{10,... | collective-permute-start | bytes 3145736 | tf_op jit(solution)/shard_map/ppermute | solution.py:31
  64.4 7.3 %collective-permute-done.4.above = bf16[128,4096]{1,0:T(8,128)(2,1)} collective-permute-done((bf16[128,4096]{1,0:T(8,128)(2,1)}, bf16[128,4096]{1,0:T(8,128)(2,1)}, u32[]{:S(2)}, u32[]{:S(2)}) %collective-permute-start.4) | collective-permute-done | bytes 1048608 | tf_op jit(solution)/shard_map/ppermute | solution.py:40
  71.7 5.1 %collective-permute-done.5.below = bf16[128,4096]{1,0:T(8,128)(2,1)} collective-permute-done((bf16[128,4096]{1,0:T(8,128)(2,1)}, bf16[128,4096]{1,0:T(8,128)(2,1)}, u32[]{:S(2)}, u32[]{:S(2)}) %collective-permute-start.5) | collective-permute-done | bytes 1048608 | tf_op jit(solution)/shard_map/ppermute | solution.py:40
  76.8 1.6 copy-done.2
  78.4 1.6 copy-done.4
  80.0 1.2 copy-done.6
  81.2 4.1 %shard_map.96 = (bf16[128,4096]{1,0:T(8,128)(2,1)S(1)}, bf16[8,144,128]{2,1,0:T(8,128)(2,1)S(1)}) custom-call(s32[3]{0:T(128)S(1)} %pad_add_fusion.place, s32[4]{0:T(128)S(1)} %bitcast.42, s32[128]{0:T(128)S(1)} %reshape.75.plan, bf16[128,4096]{1,0:T(8,128)(2,1)S(1)} %collective-permute-done.own_x.refs_0_, bf16[128,4096]{1,0:T(8,128)(2,1)S(1)} %bitcast.41, ...), custom_call_target="tpu_custom_call" | custom-call | flops 1024 | bytes 1024 | tf_op jit(solution)/shard_map/pallas_call | solution.py:90
  85.4 1.0 copy-done.8
  87.0 0.9 collective-permute-done.6.refs_3_
  87.9 1.1 collective-permute-start.8
  89.1 3.9 %collective-permute-start.9 = (bf16[128,4096]{1,0:T(8,128)(2,1)}, bf16[128,4096]{1,0:T(8,128)(2,1)}, u32[]{:S(2)}, u32[]{:S(2)}) collective-permute-start(bf16[128,4096]{1,0:T(8,128)(2,1)} %collective-permute-done.7.refs_4_), channel_id=1, source_target_pairs={{0,14},{1,15},{2,0},{3,1},{4,2},{5,3},{6,4},{7,5},{8,6},{9,7},{10,... | collective-permute-start | bytes 3145736 | tf_op jit(solution)/shard_map/ppermute | solution.py:31
  93.0 5.8 %all-to-all-start.2 = ((bf16[8,144,128]{2,1,0:T(8,128)(2,1)}), bf16[8,144,128]{2,1,0:T(8,128)(2,1)S(1)}, u32[]{:S(2)}, u32[]{:S(2)}) async-start(bf16[8,144,128]{2,1,0:T(8,128)(2,1)} %copy-done.15), calls=%async_computation.2 | async-start | bytes 589824 | tf_op jit(solution)/shard_map/all_to_all | solution.py:277
  98.8 5.7 %shard_map.97 = (bf16[5,128,512]{2,1,0:T(8,128)(2,1)S(1)}, bf16[5,128,512]{2,1,0:T(8,128)(2,1)S(1)}) custom-call(s32[3]{0:T(128)S(1)} %pad_add_fusion.place, bf16[128,4096]{1,0:T(8,128)(2,1)S(1)} %collective-permute-done.own_x.refs_0_, bf16[128,4096]{1,0:T(8,128)(2,1)} %collective-permute-done.1.refs_1_, bf16[128,4096]{1,0:T(8,128)(2,1)} %collective-permute-done.2.refs_2_, ...), custom_call_target="tpu_custom_call" | custom-call | flops 1024 | bytes 1024 | tf_op jit(solution)/shard_map/pallas_call | solution.py:90
  104.5 0.8 copy-done.11
  106.2 11.2 %collective-permute-done.8.f3 = bf16[128,4096]{1,0:T(8,128)(2,1)} collective-permute-done((bf16[128,4096]{1,0:T(8,128)(2,1)}, bf16[128,4096]{1,0:T(8,128)(2,1)}, u32[]{:S(2)}, u32[]{:S(2)}) %collective-permute-start.8) | collective-permute-done | bytes 1048608 | tf_op jit(solution)/shard_map/ppermute | solution.py:31
  117.5 2.2 %shard_map.98 = (bf16[64,4096]{1,0:T(8,128)(2,1)}, bf16[64,4096]{1,0:T(8,128)(2,1)}) custom-call(bf16[128,4096]{1,0:T(8,128)(2,1)} %collective-permute-done.8.f3, bf16[128,4096]{1,0:T(8,128)(2,1)} %collective-permute-done.9.r3), custom_call_target="tpu_custom_call" | custom-call | flops 1024 | bytes 1024 | tf_op jit(solution)/shard_map/pallas_call | solution.py:73
  119.7 1.2 collective-permute-start.10
  120.9 2.9 %collective-permute-start.11 = (bf16[64,4096]{1,0:T(8,128)(2,1)}, bf16[64,4096]{1,0:T(8,128)(2,1)}, u32[]{:S(2)}, u32[]{:S(2)}) collective-permute-start(bf16[64,4096]{1,0:T(8,128)(2,1)} %get-tuple-element.58), channel_id=1, source_target_pairs={{0,14},{1,15},{2,0},{3,1},{4,2},{5,3},{6,4},{7,5},{8,6},{9,7},{10,... | collective-permute-start | bytes 1572872 | tf_op jit(solution)/shard_map/ppermute | solution.py:31
  123.8 3.5 %shard_map.99 = (bf16[8,128,512]{2,1,0:T(8,128)(2,1)S(1)}, bf16[2,128,512]{2,1,0:T(8,128)(2,1)S(1)}) custom-call(s32[3]{0:T(128)S(1)} %pad_add_fusion.place, bf16[5,128,512]{2,1,0:T(8,128)(2,1)S(1)} %copy-done.14, bf16[128,4096]{1,0:T(8,128)(2,1)} %collective-permute-done.8.f3, bf16[128,4096]{1,0:T(8,128)(2,1)} %collective-permute-done.9.r3, ...), custom_call_target="tpu_custom_call" | custom-call | flops 1024 | bytes 1024 | tf_op jit(solution)/shard_map/pallas_call | solution.py:90
  127.3 1.0 copy-done.10
  129.0 3.9 %all-to-all-start.1 = ((bf16[8,128,512]{2,1,0:T(8,128)(2,1)}), bf16[8,128,512]{2,1,0:T(8,128)(2,1)S(1)}, u32[]{:S(2)}, u32[]{:S(2)}) async-start(bf16[8,128,512]{2,1,0:T(8,128)(2,1)} %copy-done.10), calls=%async_computation.1 | async-start | bytes 2097152 | tf_op jit(solution)/shard_map/all_to_all | solution.py:277
  134.5 2.0 %shard_map.100 = (f32[384,256]{1,0:T(8,128)S(1)}, bf16[384,256]{1,0:T(8,128)(2,1)S(1)}) custom-call(s32[3]{0:T(128)S(1)} %pad_add_fusion.place, bf16[8,144,128]{2,1,0:T(8,128)(2,1)S(1)} %all-to-all-done.2.line, bf16[8,128,512]{2,1,0:T(8,128)(2,1)} %all-to-all-done.cot_line), custom_call_target="tpu_custom_call" | custom-call | flops 1024 | bytes 1024 | tf_op jit(solution)/shard_map/pallas_call | solution.py:90
  136.7 2.7 %shard_map.101 = (bf16[128,512]{1,0:T(8,128)(2,1)S(1)}, bf16[128,512]{1,0:T(8,128)(2,1)S(1)}) custom-call(s32[3]{0:T(128)S(1)} %pad_add_fusion.place, bf16[64,4096]{1,0:T(8,128)(2,1)} %collective-permute-done.10.first_half, bf16[64,4096]{1,0:T(8,128)(2,1)} %collective-permute-done.11.second_half, bf16[4096,256]{1,0:T(8,128)(2,1)S(1)} %bitcast.35, ...), custom_call_target="tpu_custom_call" | custom-call | flops 1024 | bytes 1048576 | tf_op jit(solution)/shard_map/pallas_call | solution.py:90
  139.5 1.3 shard_map.103
  140.8 2.0 %collective-permute-start.17 = (bf16[2,64,256]{2,1,0:T(8,128)(2,1)S(1)}, bf16[2,64,256]{2,1,0:T(8,128)(2,1)S(1)}, u32[]{:S(2)}, u32[]{:S(2)}) collective-permute-start(bf16[2,64,256]{2,1,0:T(8,128)(2,1)S(1)} %get-tuple-element.72), channel_id=1, source_target_pairs={{16,1},{17,0},{18,3},{19,2},{20,5},{21,4},{22,7},{23,6},{24,9},{25... | collective-permute-start | bytes 196616 | tf_op jit(solution)/shard_map/ppermute | solution.py:351
  142.9 6.1 %collective-permute-start.16 = (bf16[2,64,256]{2,1,0:T(8,128)(2,1)S(1)}, bf16[2,64,256]{2,1,0:T(8,128)(2,1)S(1)}, u32[]{:S(2)}, u32[]{:S(2)}) collective-permute-start(bf16[2,64,256]{2,1,0:T(8,128)(2,1)S(1)} %get-tuple-element.71), channel_id=1, source_target_pairs={{16,0},{32,16},{48,32},{64,48},{80,64},{96,80},{112,96},{128,112},... | collective-permute-start | bytes 196616 | tf_op jit(solution)/shard_map/ppermute | solution.py:40
  149.7 5.9 %collective-permute-start.12 = (bf16[128,512]{1,0:T(8,128)(2,1)S(1)}, bf16[128,512]{1,0:T(8,128)(2,1)S(1)}, u32[]{:S(2)}, u32[]{:S(2)}) collective-permute-start(bf16[128,512]{1,0:T(8,128)(2,1)S(1)} %get-tuple-element.63), channel_id=1, source_target_pairs={{0,8},{1,9},{2,10},{3,11},{4,12},{5,13},{6,14},{7,15},{8,0},{9,1},... | collective-permute-start | bytes 393224 | tf_op jit(solution)/shard_map/ppermute | solution.py:31
  155.6 2.1 %collective-permute-start.13 = (bf16[2,256,256]{2,1,0:T(8,128)(2,1)S(1)}, bf16[2,256,256]{2,1,0:T(8,128)(2,1)S(1)}, u32[]{:S(2)}, u32[]{:S(2)}) collective-permute-start(bf16[2,256,256]{2,1,0:T(8,128)(2,1)S(1)} %get-tuple-element.68), channel_id=1, source_target_pairs={{0,1},{1,0},{2,3},{3,2},{4,5},{5,4},{6,7},{7,6},{8,9},{9,8},{10,11... | collective-permute-start | bytes 786440 | tf_op jit(solution)/shard_map/ppermute | solution.py:35
  157.7 1.9 %collective-permute-start.15 = (bf16[2,64,256]{2,1,0:T(8,128)(2,1)S(1)}, bf16[2,64,256]{2,1,0:T(8,128)(2,1)S(1)}, u32[]{:S(2)}, u32[]{:S(2)}) collective-permute-start(bf16[2,64,256]{2,1,0:T(8,128)(2,1)S(1)} %get-tuple-element.70), channel_id=1, source_target_pairs={{0,17},{1,16},{2,19},{3,18},{4,21},{5,20},{6,23},{7,22},{8,25},{9,... | collective-permute-start | bytes 196616 | tf_op jit(solution)/shard_map/ppermute | solution.py:351
  159.6 1.9 %collective-permute-start.14 = (bf16[2,64,256]{2,1,0:T(8,128)(2,1)S(1)}, bf16[2,64,256]{2,1,0:T(8,128)(2,1)S(1)}, u32[]{:S(2)}, u32[]{:S(2)}) collective-permute-start(bf16[2,64,256]{2,1,0:T(8,128)(2,1)S(1)} %get-tuple-element.69), channel_id=1, source_target_pairs={{0,16},{16,32},{32,48},{48,64},{64,80},{80,96},{96,112},{112,128},... | collective-permute-start | bytes 196616 | tf_op jit(solution)/shard_map/ppermute | solution.py:40
  161.6 5.0 %collective-permute-done.15 = bf16[2,64,256]{2,1,0:T(8,128)(2,1)S(1)} collective-permute-done((bf16[2,64,256]{2,1,0:T(8,128)(2,1)S(1)}, bf16[2,64,256]{2,1,0:T(8,128)(2,1)S(1)}, u32[]{:S(2)}, u32[]{:S(2)}) %collective-permute-start.15) | collective-permute-done | bytes 65568 | tf_op jit(solution)/shard_map/ppermute | solution.py:351
  166.6 2.2 %collective-permute-done.14 = bf16[2,64,256]{2,1,0:T(8,128)(2,1)S(1)} collective-permute-done((bf16[2,64,256]{2,1,0:T(8,128)(2,1)S(1)}, bf16[2,64,256]{2,1,0:T(8,128)(2,1)S(1)}, u32[]{:S(2)}, u32[]{:S(2)}) %collective-permute-start.14) | collective-permute-done | bytes 65568 | tf_op jit(solution)/shard_map/ppermute | solution.py:40
  169.0 0.9 select_add_fusion
  170.1 1.9 %shard_map.102 = bf16[128,4096]{1,0:T(8,128)(2,1)} custom-call(s32[3]{0:T(128)S(1)} %pad_add_fusion.place, bf16[128,4096]{1,0:T(8,128)(2,1)S(1)} %copy-done.9, bf16[8,128,512]{2,1,0:T(8,128)(2,1)S(1)} %all-to-all-done.1.results, bf16[128,512]{1,0:T(8,128)(2,1)S(1)} %collective-permute-done.12.last), custom_call_target="tpu_custom_call" | custom-call | flops 1024 | bytes 1024 | tf_op jit(solution)/shard_map/pallas_call | solution.py:90
  (60 shorter events, 5.9 us)
Async XLA Ops:
  0.6 18.1 %collective-permute-start = (bf16[128,4096]{1,0:T(8,128)(2,1)}, bf16[128,4096]{1,0:T(8,128)(2,1)S(1)}, u32[]{:S(2)}, u32[]{:S(2)}) collective-permute-start(bf16[128,4096]{1,0:T(8,128)(2,1)} %bitcast.48), channel_id=1, source_target_pairs={{0,16},{16,32},{32,48},{48,64},{64,80},{80,96},{96,112},{112,128},... | collective-permute-start | bytes 3145736 | tf_op jit(solution)/shard_map/ppermute | solution.py:274
  0.7 1.2 copy-start.5
  1.9 16.8 %copy-start = (bf16[1,4096,256]{2,1,0:T(8,128)(2,1)S(1)}, bf16[1,4096,256]{2,1,0:T(8,128)(2,1)}, u32[]{:S(2)}) copy-start(bf16[1,4096,256]{2,1,0:T(8,128)(2,1)} %param.10) | copy-start | bytes 6291460
  2.0 23.5 %copy-start.19 = (s32[16,4,2]{0,2,1:T(2,128)S(1)}, s32[16,4,2]{0,2,1:T(2,128)}, u32[]{:S(2)}) copy-start(s32[16,4,2]{0,2,1:T(2,128)} %param.9) | copy-start | bytes 1540
  2.0 1.0 copy-start.7
  3.0 39.0 %all-to-all-start = ((bf16[8,128,512]{2,1,0:T(8,128)(2,1)}), bf16[8,128,512]{2,1,0:T(8,128)(2,1)}, u32[]{:S(2)}, u32[]{:S(2)}) async-start(bf16[8,128,512]{2,1,0:T(8,128)(2,1)} %copy-done.7), calls=%async_computation | async-start | bytes 2097152 | tf_op jit(solution)/shard_map/all_to_all | solution.py:277
  18.8 45.6 %collective-permute-start.3 = (bf16[4096,256]{1,0:T(8,128)(2,1)S(1)}, bf16[4096,256]{1,0:T(8,128)(2,1)}, u32[]{:S(2)}, u32[]{:S(2)}) collective-permute-start(bf16[4096,256]{1,0:T(8,128)(2,1)S(1)} %bitcast.32), channel_id=1, source_target_pairs={{0,1},{1,0},{2,3},{3,2},{4,5},{5,4},{6,7},{7,6},{8,9},{9,8},{10,11... | collective-permute-start | bytes 6291464 | tf_op jit(solution)/shard_map/ppermute | solution.py:35
  19.6 41.6 %collective-permute-start.1 = (bf16[128,4096]{1,0:T(8,128)(2,1)S(1)}, bf16[128,4096]{1,0:T(8,128)(2,1)}, u32[]{:S(2)}, u32[]{:S(2)}) collective-permute-start(bf16[128,4096]{1,0:T(8,128)(2,1)S(1)} %collective-permute-done.own_x.refs_0_), channel_id=1, source_target_pairs={{0,2},{1,3},{2,4},{3,5},{4,6},{5,7},{6,8},{7,9},{8,10},{9,11},{10,... | collective-permute-start | bytes 3145736 | tf_op jit(solution)/shard_map/ppermute | solution.py:31
  21.5 39.7 %collective-permute-start.2 = (bf16[128,4096]{1,0:T(8,128)(2,1)S(1)}, bf16[128,4096]{1,0:T(8,128)(2,1)}, u32[]{:S(2)}, u32[]{:S(2)}) collective-permute-start(bf16[128,4096]{1,0:T(8,128)(2,1)S(1)} %collective-permute-done.own_x.refs_0_), channel_id=1, source_target_pairs={{0,14},{1,15},{2,0},{3,1},{4,2},{5,3},{6,4},{7,5},{8,6},{9,7},{10,... | collective-permute-start | bytes 3145736 | tf_op jit(solution)/shard_map/ppermute | solution.py:31
  25.8 1.6 copy-start.1
  27.4 1.6 copy-start.3
  29.0 47.9 %copy-start.18 = (s32[1,1,4]{2,1,0:T(1,128)S(1)}, s32[1,1,4]{2,1,0:T(1,128)}, u32[]{:S(2)}) copy-start(s32[1,1,4]{2,1,0:T(1,128)} %param.8) | copy-start | bytes 52
  31.1 40.6 %collective-permute-start.4 = (bf16[128,4096]{1,0:T(8,128)(2,1)}, bf16[128,4096]{1,0:T(8,128)(2,1)}, u32[]{:S(2)}, u32[]{:S(2)}) collective-permute-start(bf16[128,4096]{1,0:T(8,128)(2,1)} %get-tuple-element.44), channel_id=1, source_target_pairs={{16,0},{32,16},{48,32},{64,48},{80,64},{96,80},{112,96},{128,112},... | collective-permute-start | bytes 3145736 | tf_op jit(solution)/shard_map/ppermute | solution.py:40
  33.0 43.8 %collective-permute-start.5 = (bf16[128,4096]{1,0:T(8,128)(2,1)}, bf16[128,4096]{1,0:T(8,128)(2,1)}, u32[]{:S(2)}, u32[]{:S(2)}) collective-permute-start(bf16[128,4096]{1,0:T(8,128)(2,1)} %get-tuple-element.45), channel_id=1, source_target_pairs={{0,16},{16,32},{32,48},{48,64},{64,80},{80,96},{96,112},{112,128},... | collective-permute-start | bytes 3145736 | tf_op jit(solution)/shard_map/ppermute | solution.py:40
  61.2 26.8 %collective-permute-start.6 = (bf16[128,4096]{1,0:T(8,128)(2,1)}, bf16[128,4096]{1,0:T(8,128)(2,1)}, u32[]{:S(2)}, u32[]{:S(2)}) collective-permute-start(bf16[128,4096]{1,0:T(8,128)(2,1)} %collective-permute-done.1.refs_1_), channel_id=1, source_target_pairs={{0,2},{1,3},{2,4},{3,5},{4,6},{5,7},{6,8},{7,9},{8,10},{9,11},{10,... | collective-permute-start | bytes 3145736 | tf_op jit(solution)/shard_map/ppermute | solution.py:31
  61.4 26.5 %collective-permute-start.7 = (bf16[128,4096]{1,0:T(8,128)(2,1)}, bf16[128,4096]{1,0:T(8,128)(2,1)}, u32[]{:S(2)}, u32[]{:S(2)}) collective-permute-start(bf16[128,4096]{1,0:T(8,128)(2,1)} %collective-permute-done.2.refs_2_), channel_id=1, source_target_pairs={{0,14},{1,15},{2,0},{3,1},{4,2},{5,3},{6,4},{7,5},{8,6},{9,7},{10,... | collective-permute-start | bytes 3145736 | tf_op jit(solution)/shard_map/ppermute | solution.py:31
  76.8 1.6 copy-start.2
  78.4 1.6 copy-start.4
  80.0 1.2 copy-start.6
  85.4 1.0 copy-start.8
  86.3 0.7 copy-start.15
  87.9 29.5 %collective-permute-start.8 = (bf16[128,4096]{1,0:T(8,128)(2,1)}, bf16[128,4096]{1,0:T(8,128)(2,1)}, u32[]{:S(2)}, u32[]{:S(2)}) collective-permute-start(bf16[128,4096]{1,0:T(8,128)(2,1)} %collective-permute-done.6.refs_3_), channel_id=1, source_target_pairs={{0,2},{1,3},{2,4},{3,5},{4,6},{5,7},{6,8},{7,9},{8,10},{9,11},{10,... | collective-permute-start | bytes 3145736 | tf_op jit(solution)/shard_map/ppermute | solution.py:31
  89.1 28.4 %collective-permute-start.9 = (bf16[128,4096]{1,0:T(8,128)(2,1)}, bf16[128,4096]{1,0:T(8,128)(2,1)}, u32[]{:S(2)}, u32[]{:S(2)}) collective-permute-start(bf16[128,4096]{1,0:T(8,128)(2,1)} %collective-permute-done.7.refs_4_), channel_id=1, source_target_pairs={{0,14},{1,15},{2,0},{3,1},{4,2},{5,3},{6,4},{7,5},{8,6},{9,7},{10,... | collective-permute-start | bytes 3145736 | tf_op jit(solution)/shard_map/ppermute | solution.py:31
  93.0 36.0 %all-to-all-start.2 = ((bf16[8,144,128]{2,1,0:T(8,128)(2,1)}), bf16[8,144,128]{2,1,0:T(8,128)(2,1)S(1)}, u32[]{:S(2)}, u32[]{:S(2)}) async-start(bf16[8,144,128]{2,1,0:T(8,128)(2,1)} %copy-done.15), calls=%async_computation.2 | async-start | bytes 589824 | tf_op jit(solution)/shard_map/all_to_all | solution.py:277
  104.5 0.9 copy-start.11
  105.4 0.8 copy-start.13
  117.4 6.4 %copy-start.14 = (bf16[5,128,512]{2,1,0:T(8,128)(2,1)S(1)}, bf16[5,128,512]{2,1,0:T(8,128)(2,1)}, u32[]{:S(2)}) copy-start(bf16[5,128,512]{2,1,0:T(8,128)(2,1)} %copy-done.13) | copy-start | bytes 1966084
  119.7 16.8 %collective-permute-start.10 = (bf16[64,4096]{1,0:T(8,128)(2,1)}, bf16[64,4096]{1,0:T(8,128)(2,1)}, u32[]{:S(2)}, u32[]{:S(2)}) collective-permute-start(bf16[64,4096]{1,0:T(8,128)(2,1)} %get-tuple-element.54), channel_id=1, source_target_pairs={{0,2},{1,3},{2,4},{3,5},{4,6},{5,7},{6,8},{7,9},{8,10},{9,11},{10,... | collective-permute-start | bytes 1572872 | tf_op jit(solution)/shard_map/ppermute | solution.py:31
  120.9 15.8 %collective-permute-start.11 = (bf16[64,4096]{1,0:T(8,128)(2,1)}, bf16[64,4096]{1,0:T(8,128)(2,1)}, u32[]{:S(2)}, u32[]{:S(2)}) collective-permute-start(bf16[64,4096]{1,0:T(8,128)(2,1)} %get-tuple-element.58), channel_id=1, source_target_pairs={{0,14},{1,15},{2,0},{3,1},{4,2},{5,3},{6,4},{7,5},{8,6},{9,7},{10,... | collective-permute-start | bytes 1572872 | tf_op jit(solution)/shard_map/ppermute | solution.py:31
  127.3 1.0 copy-start.10
  128.3 0.7 copy-start.16
  129.0 41.0 %all-to-all-start.1 = ((bf16[8,128,512]{2,1,0:T(8,128)(2,1)}), bf16[8,128,512]{2,1,0:T(8,128)(2,1)S(1)}, u32[]{:S(2)}, u32[]{:S(2)}) async-start(bf16[8,128,512]{2,1,0:T(8,128)(2,1)} %copy-done.10), calls=%async_computation.1 | async-start | bytes 2097152 | tf_op jit(solution)/shard_map/all_to_all | solution.py:277
  136.7 2.7 %copy-start.12 = (bf16[5,128,512]{2,1,0:T(8,128)(2,1)S(1)}, bf16[5,128,512]{2,1,0:T(8,128)(2,1)}, u32[]{:S(2)}) copy-start(bf16[5,128,512]{2,1,0:T(8,128)(2,1)} %copy-done.11) | copy-start | bytes 1966084
  136.7 2.7 %copy-start.17 = (bf16[2,128,512]{2,1,0:T(8,128)(2,1)S(1)}, bf16[2,128,512]{2,1,0:T(8,128)(2,1)}, u32[]{:S(2)}) copy-start(bf16[2,128,512]{2,1,0:T(8,128)(2,1)} %copy-done.16) | copy-start | bytes 786436
  140.8 18.8 %collective-permute-start.17 = (bf16[2,64,256]{2,1,0:T(8,128)(2,1)S(1)}, bf16[2,64,256]{2,1,0:T(8,128)(2,1)S(1)}, u32[]{:S(2)}, u32[]{:S(2)}) collective-permute-start(bf16[2,64,256]{2,1,0:T(8,128)(2,1)S(1)} %get-tuple-element.72), channel_id=1, source_target_pairs={{16,1},{17,0},{18,3},{19,2},{20,5},{21,4},{22,7},{23,6},{24,9},{25... | collective-permute-start | bytes 196616 | tf_op jit(solution)/shard_map/ppermute | solution.py:351
  142.9 18.7 %collective-permute-start.16 = (bf16[2,64,256]{2,1,0:T(8,128)(2,1)S(1)}, bf16[2,64,256]{2,1,0:T(8,128)(2,1)S(1)}, u32[]{:S(2)}, u32[]{:S(2)}) collective-permute-start(bf16[2,64,256]{2,1,0:T(8,128)(2,1)S(1)} %get-tuple-element.71), channel_id=1, source_target_pairs={{16,0},{32,16},{48,32},{64,48},{80,64},{96,80},{112,96},{128,112},... | collective-permute-start | bytes 196616 | tf_op jit(solution)/shard_map/ppermute | solution.py:40
  149.7 20.3 %collective-permute-start.12 = (bf16[128,512]{1,0:T(8,128)(2,1)S(1)}, bf16[128,512]{1,0:T(8,128)(2,1)S(1)}, u32[]{:S(2)}, u32[]{:S(2)}) collective-permute-start(bf16[128,512]{1,0:T(8,128)(2,1)S(1)} %get-tuple-element.63), channel_id=1, source_target_pairs={{0,8},{1,9},{2,10},{3,11},{4,12},{5,13},{6,14},{7,15},{8,0},{9,1},... | collective-permute-start | bytes 393224 | tf_op jit(solution)/shard_map/ppermute | solution.py:31
  155.6 13.3 %collective-permute-start.13 = (bf16[2,256,256]{2,1,0:T(8,128)(2,1)S(1)}, bf16[2,256,256]{2,1,0:T(8,128)(2,1)S(1)}, u32[]{:S(2)}, u32[]{:S(2)}) collective-permute-start(bf16[2,256,256]{2,1,0:T(8,128)(2,1)S(1)} %get-tuple-element.68), channel_id=1, source_target_pairs={{0,1},{1,0},{2,3},{3,2},{4,5},{5,4},{6,7},{7,6},{8,9},{9,8},{10,11... | collective-permute-start | bytes 786440 | tf_op jit(solution)/shard_map/ppermute | solution.py:35
  157.7 8.9 %collective-permute-start.15 = (bf16[2,64,256]{2,1,0:T(8,128)(2,1)S(1)}, bf16[2,64,256]{2,1,0:T(8,128)(2,1)S(1)}, u32[]{:S(2)}, u32[]{:S(2)}) collective-permute-start(bf16[2,64,256]{2,1,0:T(8,128)(2,1)S(1)} %get-tuple-element.70), channel_id=1, source_target_pairs={{0,17},{1,16},{2,19},{3,18},{4,21},{5,20},{6,23},{7,22},{8,25},{9,... | collective-permute-start | bytes 196616 | tf_op jit(solution)/shard_map/ppermute | solution.py:351
  159.6 9.2 %collective-permute-start.14 = (bf16[2,64,256]{2,1,0:T(8,128)(2,1)S(1)}, bf16[2,64,256]{2,1,0:T(8,128)(2,1)S(1)}, u32[]{:S(2)}, u32[]{:S(2)}) collective-permute-start(bf16[2,64,256]{2,1,0:T(8,128)(2,1)S(1)} %get-tuple-element.69), channel_id=1, source_target_pairs={{0,16},{16,32},{32,48},{48,64},{64,80},{80,96},{96,112},{112,128},... | collective-permute-start | bytes 196616 | tf_op jit(solution)/shard_map/ppermute | solution.py:40
  168.8 1.2 copy-start.9

commit v6 on v5

--- a/solution.py
+++ b/solution.py
@@ -191,15 +191,11 @@
         copy.wait()
 
 
-def last_kernel(place, first_half, second_half, w_own, w_pair, out, columns):
+def last_kernel(first_half, second_half, w_own, w_pair, out):
     lhs = jnp.concatenate([first_half[...], second_half[...]], axis=0)
     cols = w_own.shape[1]
     for w, first in ((w_own, 0), (w_pair, cols)):
         out[:, first : first + cols] = dot32(lhs, w[...]).astype(BF16)
-    at = pl.multiple_of(place[0] * (LINES * cols), LINES * cols)
-    half = first_half.shape[0]
-    columns[:half] = first_half[:, pl.ds(at, LINES * cols)]
-    columns[half:] = second_half[:, pl.ds(at, LINES * cols)]
 
 
 def gradient_terms(of_signals, order, place, line, blocks):
@@ -229,7 +225,11 @@
 
 def down_gradient_kernel(order, place, line, *refs):
     blocks, (up_mine, up_theirs, mine, pair, *guests) = refs[:-8], refs[-8:]
-    here, there = gradient_terms(True, order, place, line, blocks)
+    near, next_, *halves = blocks
+    wide = near.shape[-1]
+    at = pl.multiple_of(place[0] * wide, wide)
+    farthest = jnp.concatenate([half[:, pl.ds(at, wide)] for half in halves], axis=0)
+    here, there = gradient_terms(True, order, place, line, [near, next_, farthest])
     mine[...] = here
     own = JOBS * RANK
     pair[0] = there[:own].astype(BF16)
@@ -333,15 +333,15 @@
         [line_, cot_line],
     )
     last = in_order(last, up_mine)
-    last, far_columns = kernel_call(last_kernel, [((rows, wide), BF16)] * 2, [place], [*last, w_own, w_pair], MOVED)
-    result_last = along_z(last, far, depth)
+    (last_piece,) = kernel_call(last_kernel, [((rows, wide), BF16)], [], [*last, w_own, w_pair], MOVED)
+    result_last = along_z(last_piece, far, depth)
     own_rows = JOBS * RANK
     guest = ((2, RANK, cols), BF16)
     down_mine, pair, next_here, next_there, prev_here, prev_there = kernel_call(
         functools.partial(down_gradient_kernel, order + (far,)),
         [terms, ((2, own_rows, cols), BF16)] + [guest] * 4,
         [place],
-        [line, near_columns, next_columns, far_columns, up_mine, up_theirs],
+        [line, near_columns, next_columns, *last, up_mine, up_theirs],
         MOVED,
     )
 

time: 173 us -> 175 us (1.012)
  local copies, waits for them, and re-layouts: 15.5 us -> 17.5 us
    unnamed x41, local copies, waits for them, and re-layouts: 15 us -> 17.1 us
where the time goes in v6:
time: 175 us; the launch traced here: 174 us
  waiting for transfers between devices  65.2 us (37%)
  starting transfers between devices  61.5 us (35%)
  Pallas kernels  26.3 us (15%)
  local copies, waits for them, and re-layouts  17.5 us (10%)
  other arithmetic  3.09 us (2%)
    ppermute x9, waiting for transfers between devices, along_z(): return lax.ppermute(value, 'dp', route)  31.6 us
    ppermute x9, starting transfers between devices, along_z(): return lax.ppermute(value, 'dp', route)  24.1 us
    pallas_call x8, Pallas kernels, kernel_call(): pl.pallas_call(kernel, out_shape=tuple((jax.ShapeDtypeStruct(shape, dtype...  22 us
    all_to_all x3, starting transfers between devices, to_line(): lax.all_to_all(value, 'dp', 0, 0, axis_index_groups=lines, tiled=True)  18.1 us
    unnamed x41, local copies, waits for them, and re-layouts  17.1 us
    ppermute x4, waiting for transfers between devices, section_shift(): return lax.ppermute(value, 'section', route)  14.7 us
    ppermute x4, starting transfers between devices, section_shift(): return lax.ppermute(value, 'section', route)  12.4 us
    ppermute x1, waiting for transfers between devices, on_device(): lax.ppermute(handed[0], 'section', [(i, (i + 1) % sections) for i in rang...  7.28 us
  transfers between devices with their start and end apart: 21, of which 11 were waited for; matrix products, arithmetic and copies ran while one was open for 2% of the time, Pallas kernels for 14%

profile of v6, /device:TPU:6, one launch (start us, length us, event | category | flops | bytes accessed | tf_op | source)
XLA Modules:
  0.0 174.5 jit_solution(15111643319619843110)
XLA Ops:
  0.7 1.2 copy-done.5
  2.0 1.0 copy-done.7
  3.0 8.5 %all-to-all-start = ((bf16[8,128,512]{2,1,0:T(8,128)(2,1)}), bf16[8,128,512]{2,1,0:T(8,128)(2,1)}, u32[]{:S(2)}, u32[]{:S(2)}) async-start(bf16[8,128,512]{2,1,0:T(8,128)(2,1)} %copy-done.7), calls=%async_computation | async-start | bytes 2097152 | tf_op jit(solution)/shard_map/all_to_all | solution.py:277
  11.5 7.3 %collective-permute-done.own_x.refs_0_ = bf16[128,4096]{1,0:T(8,128)(2,1)S(1)} collective-permute-done((bf16[128,4096]{1,0:T(8,128)(2,1)}, bf16[128,4096]{1,0:T(8,128)(2,1)S(1)}, u32[]{:S(2)}, u32[]{:S(2)}) %collective-permute-start) | collective-permute-done | bytes 1048608 | tf_op jit(solution)/shard_map/ppermute | solution.py:274
  19.6 1.9 %collective-permute-start.1 = (bf16[128,4096]{1,0:T(8,128)(2,1)S(1)}, bf16[128,4096]{1,0:T(8,128)(2,1)}, u32[]{:S(2)}, u32[]{:S(2)}) collective-permute-start(bf16[128,4096]{1,0:T(8,128)(2,1)S(1)} %collective-permute-done.own_x.refs_0_), channel_id=1, source_target_pairs={{0,2},{1,3},{2,4},{3,5},{4,6},{5,7},{6,8},{7,9},{8,10},{9,11},{10,... | collective-permute-start | bytes 3145736 | tf_op jit(solution)/shard_map/ppermute | solution.py:31
  21.5 3.9 %collective-permute-start.2 = (bf16[128,4096]{1,0:T(8,128)(2,1)S(1)}, bf16[128,4096]{1,0:T(8,128)(2,1)}, u32[]{:S(2)}, u32[]{:S(2)}) collective-permute-start(bf16[128,4096]{1,0:T(8,128)(2,1)S(1)} %collective-permute-done.own_x.refs_0_), channel_id=1, source_target_pairs={{0,14},{1,15},{2,0},{3,1},{4,2},{5,3},{6,4},{7,5},{8,6},{9,7},{10,... | collective-permute-start | bytes 3145736 | tf_op jit(solution)/shard_map/ppermute | solution.py:31
  25.8 1.6 copy-done.1
  27.4 1.6 copy-done.3
  29.0 2.1 %shard_map.95 = (bf16[128,4096]{1,0:T(8,128)(2,1)}, bf16[128,4096]{1,0:T(8,128)(2,1)}) custom-call(s32[3]{0:T(128)S(1)} %pad_add_fusion.place, s32[128]{0:T(128)S(1)} %reshape.75.plan, bf16[4,64,4096]{2,1,0:T(8,128)(2,1)S(1)} %bitcast.36, bf16[4,64,4096]{2,1,0:T(8,128)(2,1)S(1)} %bitcast.38), custom_call_target="tpu_custom_call" | custom-call | flops 1024 | bytes 1024 | tf_op jit(solution)/shard_map/pallas_call | solution.py:73
  31.1 1.9 %collective-permute-start.4 = (bf16[128,4096]{1,0:T(8,128)(2,1)}, bf16[128,4096]{1,0:T(8,128)(2,1)}, u32[]{:S(2)}, u32[]{:S(2)}) collective-permute-start(bf16[128,4096]{1,0:T(8,128)(2,1)} %get-tuple-element.42), channel_id=1, source_target_pairs={{16,0},{32,16},{48,32},{64,48},{80,64},{96,80},{112,96},{128,112},... | collective-permute-start | bytes 3145736 | tf_op jit(solution)/shard_map/ppermute | solution.py:40
  33.0 2.4 %collective-permute-start.5 = (bf16[128,4096]{1,0:T(8,128)(2,1)}, bf16[128,4096]{1,0:T(8,128)(2,1)}, u32[]{:S(2)}, u32[]{:S(2)}) collective-permute-start(bf16[128,4096]{1,0:T(8,128)(2,1)} %get-tuple-element.43), channel_id=1, source_target_pairs={{0,16},{16,32},{32,48},{48,64},{64,80},{80,96},{96,112},{112,128},... | collective-permute-start | bytes 3145736 | tf_op jit(solution)/shard_map/ppermute | solution.py:40
  35.4 6.6 %all-to-all-done.cot_line = bf16[8,128,512]{2,1,0:T(8,128)(2,1)} async-done(((bf16[8,128,512]{2,1,0:T(8,128)(2,1)}), bf16[8,128,512]{2,1,0:T(8,128)(2,1)}, u32[]{:S(2)}, u32[]{:S(2)}) %all-to-all-start) | async-done | bytes 1048608 | tf_op jit(solution)/shard_map/all_to_all | solution.py:277
  42.0 19.2 %collective-permute-done.1.refs_1_ = bf16[128,4096]{1,0:T(8,128)(2,1)} collective-permute-done((bf16[128,4096]{1,0:T(8,128)(2,1)S(1)}, bf16[128,4096]{1,0:T(8,128)(2,1)}, u32[]{:S(2)}, u32[]{:S(2)}) %collective-permute-start.1) | collective-permute-done | bytes 1048608 | tf_op jit(solution)/shard_map/ppermute | solution.py:31
  61.4 3.0 %collective-permute-start.7 = (bf16[128,4096]{1,0:T(8,128)(2,1)}, bf16[128,4096]{1,0:T(8,128)(2,1)}, u32[]{:S(2)}, u32[]{:S(2)}) collective-permute-start(bf16[128,4096]{1,0:T(8,128)(2,1)} %collective-permute-done.2.refs_2_), channel_id=1, source_target_pairs={{0,14},{1,15},{2,0},{3,1},{4,2},{5,3},{6,4},{7,5},{8,6},{9,7},{10,... | collective-permute-start | bytes 3145736 | tf_op jit(solution)/shard_map/ppermute | solution.py:31
  64.4 7.3 %collective-permute-done.4.above = bf16[128,4096]{1,0:T(8,128)(2,1)} collective-permute-done((bf16[128,4096]{1,0:T(8,128)(2,1)}, bf16[128,4096]{1,0:T(8,128)(2,1)}, u32[]{:S(2)}, u32[]{:S(2)}) %collective-permute-start.4) | collective-permute-done | bytes 1048608 | tf_op jit(solution)/shard_map/ppermute | solution.py:40
  71.7 5.1 %collective-permute-done.5.below = bf16[128,4096]{1,0:T(8,128)(2,1)} collective-permute-done((bf16[128,4096]{1,0:T(8,128)(2,1)}, bf16[128,4096]{1,0:T(8,128)(2,1)}, u32[]{:S(2)}, u32[]{:S(2)}) %collective-permute-start.5) | collective-permute-done | bytes 1048608 | tf_op jit(solution)/shard_map/ppermute | solution.py:40
  76.8 1.6 copy-done.2
  78.4 1.6 copy-done.4
  80.0 1.2 copy-done.6
  81.2 4.1 %shard_map.96 = (bf16[128,4096]{1,0:T(8,128)(2,1)S(1)}, bf16[8,144,128]{2,1,0:T(8,128)(2,1)S(1)}) custom-call(s32[3]{0:T(128)S(1)} %pad_add_fusion.place, s32[4]{0:T(128)S(1)} %bitcast.42, s32[128]{0:T(128)S(1)} %reshape.75.plan, bf16[128,4096]{1,0:T(8,128)(2,1)S(1)} %collective-permute-done.own_x.refs_0_, bf16[128,4096]{1,0:T(8,128)(2,1)S(1)} %bitcast.41, ...), custom_call_target="tpu_custom_call" | custom-call | flops 1024 | bytes 1024 | tf_op jit(solution)/shard_map/pallas_call | solution.py:90
  85.4 1.0 copy-done.8
  87.0 0.9 collective-permute-done.6.refs_3_
  87.9 1.1 collective-permute-start.8
  89.1 3.9 %collective-permute-start.9 = (bf16[128,4096]{1,0:T(8,128)(2,1)}, bf16[128,4096]{1,0:T(8,128)(2,1)}, u32[]{:S(2)}, u32[]{:S(2)}) collective-permute-start(bf16[128,4096]{1,0:T(8,128)(2,1)} %collective-permute-done.7.refs_4_), channel_id=1, source_target_pairs={{0,14},{1,15},{2,0},{3,1},{4,2},{5,3},{6,4},{7,5},{8,6},{9,7},{10,... | collective-permute-start | bytes 3145736 | tf_op jit(solution)/shard_map/ppermute | solution.py:31
  93.0 5.8 %all-to-all-start.2 = ((bf16[8,144,128]{2,1,0:T(8,128)(2,1)}), bf16[8,144,128]{2,1,0:T(8,128)(2,1)S(1)}, u32[]{:S(2)}, u32[]{:S(2)}) async-start(bf16[8,144,128]{2,1,0:T(8,128)(2,1)} %copy-done.15), calls=%async_computation.2 | async-start | bytes 589824 | tf_op jit(solution)/shard_map/all_to_all | solution.py:277
  98.7 5.7 %shard_map.97 = (bf16[5,128,512]{2,1,0:T(8,128)(2,1)S(1)}, bf16[5,128,512]{2,1,0:T(8,128)(2,1)S(1)}) custom-call(s32[3]{0:T(128)S(1)} %pad_add_fusion.place, bf16[128,4096]{1,0:T(8,128)(2,1)S(1)} %collective-permute-done.own_x.refs_0_, bf16[128,4096]{1,0:T(8,128)(2,1)} %collective-permute-done.1.refs_1_, bf16[128,4096]{1,0:T(8,128)(2,1)} %collective-permute-done.2.refs_2_, ...), custom_call_target="tpu_custom_call" | custom-call | flops 1024 | bytes 1024 | tf_op jit(solution)/shard_map/pallas_call | solution.py:90
  106.2 11.2 %collective-permute-done.8.f3 = bf16[128,4096]{1,0:T(8,128)(2,1)} collective-permute-done((bf16[128,4096]{1,0:T(8,128)(2,1)}, bf16[128,4096]{1,0:T(8,128)(2,1)}, u32[]{:S(2)}, u32[]{:S(2)}) %collective-permute-start.8) | collective-permute-done | bytes 1048608 | tf_op jit(solution)/shard_map/ppermute | solution.py:31
  117.5 2.2 %shard_map.98 = (bf16[64,4096]{1,0:T(8,128)(2,1)}, bf16[64,4096]{1,0:T(8,128)(2,1)}) custom-call(bf16[128,4096]{1,0:T(8,128)(2,1)} %collective-permute-done.8.f3, bf16[128,4096]{1,0:T(8,128)(2,1)} %collective-permute-done.9.r3), custom_call_target="tpu_custom_call" | custom-call | flops 1024 | bytes 1024 | tf_op jit(solution)/shard_map/pallas_call | solution.py:73
  119.7 1.2 collective-permute-start.10
  120.9 2.9 %collective-permute-start.11 = (bf16[64,4096]{1,0:T(8,128)(2,1)}, bf16[64,4096]{1,0:T(8,128)(2,1)}, u32[]{:S(2)}, u32[]{:S(2)}) collective-permute-start(bf16[64,4096]{1,0:T(8,128)(2,1)} %get-tuple-element.56), channel_id=1, source_target_pairs={{0,14},{1,15},{2,0},{3,1},{4,2},{5,3},{6,4},{7,5},{8,6},{9,7},{10,... | collective-permute-start | bytes 1572872 | tf_op jit(solution)/shard_map/ppermute | solution.py:31
  123.8 3.5 %shard_map.99 = (bf16[8,128,512]{2,1,0:T(8,128)(2,1)S(1)}, bf16[2,128,512]{2,1,0:T(8,128)(2,1)S(1)}) custom-call(s32[3]{0:T(128)S(1)} %pad_add_fusion.place, bf16[5,128,512]{2,1,0:T(8,128)(2,1)S(1)} %copy-done.14, bf16[128,4096]{1,0:T(8,128)(2,1)} %collective-permute-done.8.f3, bf16[128,4096]{1,0:T(8,128)(2,1)} %collective-permute-done.9.r3, ...), custom_call_target="tpu_custom_call" | custom-call | flops 1024 | bytes 1024 | tf_op jit(solution)/shard_map/pallas_call | solution.py:90
  127.3 1.0 copy-done.10
  129.0 3.9 %all-to-all-start.1 = ((bf16[8,128,512]{2,1,0:T(8,128)(2,1)}), bf16[8,128,512]{2,1,0:T(8,128)(2,1)S(1)}, u32[]{:S(2)}, u32[]{:S(2)}) async-start(bf16[8,128,512]{2,1,0:T(8,128)(2,1)} %copy-done.10), calls=%async_computation.1 | async-start | bytes 2097152 | tf_op jit(solution)/shard_map/all_to_all | solution.py:277
  134.4 2.0 %shard_map.100 = (f32[384,256]{1,0:T(8,128)S(1)}, bf16[384,256]{1,0:T(8,128)(2,1)S(1)}) custom-call(s32[3]{0:T(128)S(1)} %pad_add_fusion.place, bf16[8,144,128]{2,1,0:T(8,128)(2,1)S(1)} %all-to-all-done.2.line, bf16[8,128,512]{2,1,0:T(8,128)(2,1)} %all-to-all-done.cot_line), custom_call_target="tpu_custom_call" | custom-call | flops 1024 | bytes 1024 | tf_op jit(solution)/shard_map/pallas_call | solution.py:90
  136.7 1.1 copy-done.12
  137.8 0.9 copy-done.17
  138.7 2.0 %shard_map.103 = (f32[384,256]{1,0:T(8,128)S(1)}, bf16[2,256,256]{2,1,0:T(8,128)(2,1)S(1)}, bf16[2,64,256]{2,1,0:T(8,128)(2,1)S(1)}, bf16[2,64,256]{2,1,0:T(8,12...) custom-call(s32[3]{0:T(128)S(1)} %pad_add_fusion.place, ...), custom_call_target="tpu_custom_call" | custom-call | flops 1024 | bytes 1048576 | tf_op jit(solution)/shard_map/pallas_call | solution.py:90
  140.7 2.0 %collective-permute-start.17 = (bf16[2,64,256]{2,1,0:T(8,128)(2,1)S(1)}, bf16[2,64,256]{2,1,0:T(8,128)(2,1)S(1)}, u32[]{:S(2)}, u32[]{:S(2)}) collective-permute-start(bf16[2,64,256]{2,1,0:T(8,128)(2,1)S(1)} %get-tuple-element.68), channel_id=1, source_target_pairs={{16,1},{17,0},{18,3},{19,2},{20,5},{21,4},{22,7},{23,6},{24,9},{25... | collective-permute-start | bytes 196616 | tf_op jit(solution)/shard_map/ppermute | solution.py:351
  142.7 6.1 %collective-permute-start.16 = (bf16[2,64,256]{2,1,0:T(8,128)(2,1)S(1)}, bf16[2,64,256]{2,1,0:T(8,128)(2,1)S(1)}, u32[]{:S(2)}, u32[]{:S(2)}) collective-permute-start(bf16[2,64,256]{2,1,0:T(8,128)(2,1)S(1)} %get-tuple-element.67), channel_id=1, source_target_pairs={{16,0},{32,16},{48,32},{64,48},{80,64},{96,80},{112,96},{128,112},... | collective-permute-start | bytes 196616 | tf_op jit(solution)/shard_map/ppermute | solution.py:40
  149.5 2.6 %shard_map.101 = bf16[128,512]{1,0:T(8,128)(2,1)S(1)} custom-call(bf16[64,4096]{1,0:T(8,128)(2,1)} %collective-permute-done.10.first_half.refs_2_, bf16[64,4096]{1,0:T(8,128)(2,1)} %collective-permute-done.11.second_half.refs_3_, bf16[4096,256]{1,0:T(8,128)(2,1)S(1)} %bitcast.35, bf16[4096,256]{1,0:T(8,128)(2,1)} %collective-permute-done.3.refs_6_.w_pair), custom_call_target="tpu_custom_call" | custom-call | flops 1024 | bytes 1048576 | tf_op jit(solution)/shard_map/pallas_call | solution.py:90
  152.2 5.9 %collective-permute-start.12 = (bf16[128,512]{1,0:T(8,128)(2,1)S(1)}, bf16[128,512]{1,0:T(8,128)(2,1)S(1)}, u32[]{:S(2)}, u32[]{:S(2)}) collective-permute-start(bf16[128,512]{1,0:T(8,128)(2,1)S(1)} %shard_map.101), channel_id=1, source_target_pairs={{0,8},{1,9},{2,10},{3,11},{4,12},{5,13},{6,14},{7,15},{8,0},{9,1},... | collective-permute-start | bytes 393224 | tf_op jit(solution)/shard_map/ppermute | solution.py:31
  158.1 2.1 %collective-permute-start.13 = (bf16[2,256,256]{2,1,0:T(8,128)(2,1)S(1)}, bf16[2,256,256]{2,1,0:T(8,128)(2,1)S(1)}, u32[]{:S(2)}, u32[]{:S(2)}) collective-permute-start(bf16[2,256,256]{2,1,0:T(8,128)(2,1)S(1)} %get-tuple-element.64), channel_id=1, source_target_pairs={{0,1},{1,0},{2,3},{3,2},{4,5},{5,4},{6,7},{7,6},{8,9},{9,8},{10,11... | collective-permute-start | bytes 786440 | tf_op jit(solution)/shard_map/ppermute | solution.py:35
  160.2 1.9 %collective-permute-start.15 = (bf16[2,64,256]{2,1,0:T(8,128)(2,1)S(1)}, bf16[2,64,256]{2,1,0:T(8,128)(2,1)S(1)}, u32[]{:S(2)}, u32[]{:S(2)}) collective-permute-start(bf16[2,64,256]{2,1,0:T(8,128)(2,1)S(1)} %get-tuple-element.66), channel_id=1, source_target_pairs={{0,17},{1,16},{2,19},{3,18},{4,21},{5,20},{6,23},{7,22},{8,25},{9,... | collective-permute-start | bytes 196616 | tf_op jit(solution)/shard_map/ppermute | solution.py:351
  162.1 1.9 %collective-permute-start.14 = (bf16[2,64,256]{2,1,0:T(8,128)(2,1)S(1)}, bf16[2,64,256]{2,1,0:T(8,128)(2,1)S(1)}, u32[]{:S(2)}, u32[]{:S(2)}) collective-permute-start(bf16[2,64,256]{2,1,0:T(8,128)(2,1)S(1)} %get-tuple-element.65), channel_id=1, source_target_pairs={{0,16},{16,32},{32,48},{48,64},{64,80},{80,96},{96,112},{112,128},... | collective-permute-start | bytes 196616 | tf_op jit(solution)/shard_map/ppermute | solution.py:40
  164.1 5.0 %collective-permute-done.15 = bf16[2,64,256]{2,1,0:T(8,128)(2,1)S(1)} collective-permute-done((bf16[2,64,256]{2,1,0:T(8,128)(2,1)S(1)}, bf16[2,64,256]{2,1,0:T(8,128)(2,1)S(1)}, u32[]{:S(2)}, u32[]{:S(2)}) %collective-permute-start.15) | collective-permute-done | bytes 65568 | tf_op jit(solution)/shard_map/ppermute | solution.py:351
  169.1 2.2 %collective-permute-done.14 = bf16[2,64,256]{2,1,0:T(8,128)(2,1)S(1)} collective-permute-done((bf16[2,64,256]{2,1,0:T(8,128)(2,1)S(1)}, bf16[2,64,256]{2,1,0:T(8,128)(2,1)S(1)}, u32[]{:S(2)}, u32[]{:S(2)}) %collective-permute-start.14) | collective-permute-done | bytes 65568 | tf_op jit(solution)/shard_map/ppermute | solution.py:40
  171.5 0.9 select_add_fusion
  172.6 1.9 %shard_map.102 = bf16[128,4096]{1,0:T(8,128)(2,1)} custom-call(s32[3]{0:T(128)S(1)} %pad_add_fusion.place, bf16[128,4096]{1,0:T(8,128)(2,1)S(1)} %copy-done.9, bf16[8,128,512]{2,1,0:T(8,128)(2,1)S(1)} %all-to-all-done.1.results, bf16[128,512]{1,0:T(8,128)(2,1)S(1)} %collective-permute-done.12.last), custom_call_target="tpu_custom_call" | custom-call | flops 1024 | bytes 1024 | tf_op jit(solution)/shard_map/pallas_call | solution.py:90
  (60 shorter events, 7.5 us)
Async XLA Ops:
  0.6 18.1 %collective-permute-start = (bf16[128,4096]{1,0:T(8,128)(2,1)}, bf16[128,4096]{1,0:T(8,128)(2,1)S(1)}, u32[]{:S(2)}, u32[]{:S(2)}) collective-permute-start(bf16[128,4096]{1,0:T(8,128)(2,1)} %bitcast.48), channel_id=1, source_target_pairs={{0,16},{16,32},{32,48},{48,64},{64,80},{80,96},{96,112},{112,128},... | collective-permute-start | bytes 3145736 | tf_op jit(solution)/shard_map/ppermute | solution.py:274
  0.7 1.2 copy-start.5
  1.9 16.8 %copy-start = (bf16[1,4096,256]{2,1,0:T(8,128)(2,1)S(1)}, bf16[1,4096,256]{2,1,0:T(8,128)(2,1)}, u32[]{:S(2)}) copy-start(bf16[1,4096,256]{2,1,0:T(8,128)(2,1)} %param.10) | copy-start | bytes 6291460
  2.0 23.5 %copy-start.19 = (s32[16,4,2]{0,2,1:T(2,128)S(1)}, s32[16,4,2]{0,2,1:T(2,128)}, u32[]{:S(2)}) copy-start(s32[16,4,2]{0,2,1:T(2,128)} %param.9) | copy-start | bytes 1540
  2.0 1.0 copy-start.7
  3.0 39.0 %all-to-all-start = ((bf16[8,128,512]{2,1,0:T(8,128)(2,1)}), bf16[8,128,512]{2,1,0:T(8,128)(2,1)}, u32[]{:S(2)}, u32[]{:S(2)}) async-start(bf16[8,128,512]{2,1,0:T(8,128)(2,1)} %copy-done.7), calls=%async_computation | async-start | bytes 2097152 | tf_op jit(solution)/shard_map/all_to_all | solution.py:277
  18.8 45.6 %collective-permute-start.3 = (bf16[4096,256]{1,0:T(8,128)(2,1)S(1)}, bf16[4096,256]{1,0:T(8,128)(2,1)}, u32[]{:S(2)}, u32[]{:S(2)}) collective-permute-start(bf16[4096,256]{1,0:T(8,128)(2,1)S(1)} %bitcast.32), channel_id=1, source_target_pairs={{0,1},{1,0},{2,3},{3,2},{4,5},{5,4},{6,7},{7,6},{8,9},{9,8},{10,11... | collective-permute-start | bytes 6291464 | tf_op jit(solution)/shard_map/ppermute | solution.py:35
  19.6 41.6 %collective-permute-start.1 = (bf16[128,4096]{1,0:T(8,128)(2,1)S(1)}, bf16[128,4096]{1,0:T(8,128)(2,1)}, u32[]{:S(2)}, u32[]{:S(2)}) collective-permute-start(bf16[128,4096]{1,0:T(8,128)(2,1)S(1)} %collective-permute-done.own_x.refs_0_), channel_id=1, source_target_pairs={{0,2},{1,3},{2,4},{3,5},{4,6},{5,7},{6,8},{7,9},{8,10},{9,11},{10,... | collective-permute-start | bytes 3145736 | tf_op jit(solution)/shard_map/ppermute | solution.py:31
  21.5 39.7 %collective-permute-start.2 = (bf16[128,4096]{1,0:T(8,128)(2,1)S(1)}, bf16[128,4096]{1,0:T(8,128)(2,1)}, u32[]{:S(2)}, u32[]{:S(2)}) collective-permute-start(bf16[128,4096]{1,0:T(8,128)(2,1)S(1)} %collective-permute-done.own_x.refs_0_), channel_id=1, source_target_pairs={{0,14},{1,15},{2,0},{3,1},{4,2},{5,3},{6,4},{7,5},{8,6},{9,7},{10,... | collective-permute-start | bytes 3145736 | tf_op jit(solution)/shard_map/ppermute | solution.py:31
  25.8 1.6 copy-start.1
  27.4 1.6 copy-start.3
  29.0 47.9 %copy-start.18 = (s32[1,1,4]{2,1,0:T(1,128)S(1)}, s32[1,1,4]{2,1,0:T(1,128)}, u32[]{:S(2)}) copy-start(s32[1,1,4]{2,1,0:T(1,128)} %param.8) | copy-start | bytes 52
  31.1 40.6 %collective-permute-start.4 = (bf16[128,4096]{1,0:T(8,128)(2,1)}, bf16[128,4096]{1,0:T(8,128)(2,1)}, u32[]{:S(2)}, u32[]{:S(2)}) collective-permute-start(bf16[128,4096]{1,0:T(8,128)(2,1)} %get-tuple-element.42), channel_id=1, source_target_pairs={{16,0},{32,16},{48,32},{64,48},{80,64},{96,80},{112,96},{128,112},... | collective-permute-start | bytes 3145736 | tf_op jit(solution)/shard_map/ppermute | solution.py:40
  33.0 43.8 %collective-permute-start.5 = (bf16[128,4096]{1,0:T(8,128)(2,1)}, bf16[128,4096]{1,0:T(8,128)(2,1)}, u32[]{:S(2)}, u32[]{:S(2)}) collective-permute-start(bf16[128,4096]{1,0:T(8,128)(2,1)} %get-tuple-element.43), channel_id=1, source_target_pairs={{0,16},{16,32},{32,48},{48,64},{64,80},{80,96},{96,112},{112,128},... | collective-permute-start | bytes 3145736 | tf_op jit(solution)/shard_map/ppermute | solution.py:40
  61.2 26.8 %collective-permute-start.6 = (bf16[128,4096]{1,0:T(8,128)(2,1)}, bf16[128,4096]{1,0:T(8,128)(2,1)}, u32[]{:S(2)}, u32[]{:S(2)}) collective-permute-start(bf16[128,4096]{1,0:T(8,128)(2,1)} %collective-permute-done.1.refs_1_), channel_id=1, source_target_pairs={{0,2},{1,3},{2,4},{3,5},{4,6},{5,7},{6,8},{7,9},{8,10},{9,11},{10,... | collective-permute-start | bytes 3145736 | tf_op jit(solution)/shard_map/ppermute | solution.py:31
  61.4 26.5 %collective-permute-start.7 = (bf16[128,4096]{1,0:T(8,128)(2,1)}, bf16[128,4096]{1,0:T(8,128)(2,1)}, u32[]{:S(2)}, u32[]{:S(2)}) collective-permute-start(bf16[128,4096]{1,0:T(8,128)(2,1)} %collective-permute-done.2.refs_2_), channel_id=1, source_target_pairs={{0,14},{1,15},{2,0},{3,1},{4,2},{5,3},{6,4},{7,5},{8,6},{9,7},{10,... | collective-permute-start | bytes 3145736 | tf_op jit(solution)/shard_map/ppermute | solution.py:31
  76.8 1.6 copy-start.2
  78.4 1.6 copy-start.4
  80.0 1.2 copy-start.6
  85.4 1.0 copy-start.8
  86.3 0.7 copy-start.15
  87.9 29.5 %collective-permute-start.8 = (bf16[128,4096]{1,0:T(8,128)(2,1)}, bf16[128,4096]{1,0:T(8,128)(2,1)}, u32[]{:S(2)}, u32[]{:S(2)}) collective-permute-start(bf16[128,4096]{1,0:T(8,128)(2,1)} %collective-permute-done.6.refs_3_), channel_id=1, source_target_pairs={{0,2},{1,3},{2,4},{3,5},{4,6},{5,7},{6,8},{7,9},{8,10},{9,11},{10,... | collective-permute-start | bytes 3145736 | tf_op jit(solution)/shard_map/ppermute | solution.py:31
  89.1 28.4 %collective-permute-start.9 = (bf16[128,4096]{1,0:T(8,128)(2,1)}, bf16[128,4096]{1,0:T(8,128)(2,1)}, u32[]{:S(2)}, u32[]{:S(2)}) collective-permute-start(bf16[128,4096]{1,0:T(8,128)(2,1)} %collective-permute-done.7.refs_4_), channel_id=1, source_target_pairs={{0,14},{1,15},{2,0},{3,1},{4,2},{5,3},{6,4},{7,5},{8,6},{9,7},{10,... | collective-permute-start | bytes 3145736 | tf_op jit(solution)/shard_map/ppermute | solution.py:31
  93.0 36.0 %all-to-all-start.2 = ((bf16[8,144,128]{2,1,0:T(8,128)(2,1)}), bf16[8,144,128]{2,1,0:T(8,128)(2,1)S(1)}, u32[]{:S(2)}, u32[]{:S(2)}) async-start(bf16[8,144,128]{2,1,0:T(8,128)(2,1)} %copy-done.15), calls=%async_computation.2 | async-start | bytes 589824 | tf_op jit(solution)/shard_map/all_to_all | solution.py:277
  104.5 0.9 copy-start.11
  105.3 0.8 copy-start.13
  117.4 6.4 %copy-start.14 = (bf16[5,128,512]{2,1,0:T(8,128)(2,1)S(1)}, bf16[5,128,512]{2,1,0:T(8,128)(2,1)}, u32[]{:S(2)}) copy-start(bf16[5,128,512]{2,1,0:T(8,128)(2,1)} %copy-done.13) | copy-start | bytes 1966084
  119.7 16.7 %collective-permute-start.10 = (bf16[64,4096]{1,0:T(8,128)(2,1)}, bf16[64,4096]{1,0:T(8,128)(2,1)}, u32[]{:S(2)}, u32[]{:S(2)}) collective-permute-start(bf16[64,4096]{1,0:T(8,128)(2,1)} %get-tuple-element.52), channel_id=1, source_target_pairs={{0,2},{1,3},{2,4},{3,5},{4,6},{5,7},{6,8},{7,9},{8,10},{9,11},{10,... | collective-permute-start | bytes 1572872 | tf_op jit(solution)/shard_map/ppermute | solution.py:31
  120.9 15.8 %collective-permute-start.11 = (bf16[64,4096]{1,0:T(8,128)(2,1)}, bf16[64,4096]{1,0:T(8,128)(2,1)}, u32[]{:S(2)}, u32[]{:S(2)}) collective-permute-start(bf16[64,4096]{1,0:T(8,128)(2,1)} %get-tuple-element.56), channel_id=1, source_target_pairs={{0,14},{1,15},{2,0},{3,1},{4,2},{5,3},{6,4},{7,5},{8,6},{9,7},{10,... | collective-permute-start | bytes 1572872 | tf_op jit(solution)/shard_map/ppermute | solution.py:31
  127.3 1.0 copy-start.10
  128.3 0.7 copy-start.16
  129.0 43.5 %all-to-all-start.1 = ((bf16[8,128,512]{2,1,0:T(8,128)(2,1)}), bf16[8,128,512]{2,1,0:T(8,128)(2,1)S(1)}, u32[]{:S(2)}, u32[]{:S(2)}) async-start(bf16[8,128,512]{2,1,0:T(8,128)(2,1)} %copy-done.10), calls=%async_computation.1 | async-start | bytes 2097152 | tf_op jit(solution)/shard_map/all_to_all | solution.py:277
  136.7 1.1 copy-start.12
  137.8 0.9 copy-start.17
  140.7 21.4 %collective-permute-start.17 = (bf16[2,64,256]{2,1,0:T(8,128)(2,1)S(1)}, bf16[2,64,256]{2,1,0:T(8,128)(2,1)S(1)}, u32[]{:S(2)}, u32[]{:S(2)}) collective-permute-start(bf16[2,64,256]{2,1,0:T(8,128)(2,1)S(1)} %get-tuple-element.68), channel_id=1, source_target_pairs={{16,1},{17,0},{18,3},{19,2},{20,5},{21,4},{22,7},{23,6},{24,9},{25... | collective-permute-start | bytes 196616 | tf_op jit(solution)/shard_map/ppermute | solution.py:351
  142.7 21.4 %collective-permute-start.16 = (bf16[2,64,256]{2,1,0:T(8,128)(2,1)S(1)}, bf16[2,64,256]{2,1,0:T(8,128)(2,1)S(1)}, u32[]{:S(2)}, u32[]{:S(2)}) collective-permute-start(bf16[2,64,256]{2,1,0:T(8,128)(2,1)S(1)} %get-tuple-element.67), channel_id=1, source_target_pairs={{16,0},{32,16},{48,32},{64,48},{80,64},{96,80},{112,96},{128,112},... | collective-permute-start | bytes 196616 | tf_op jit(solution)/shard_map/ppermute | solution.py:40
  152.2 20.3 %collective-permute-start.12 = (bf16[128,512]{1,0:T(8,128)(2,1)S(1)}, bf16[128,512]{1,0:T(8,128)(2,1)S(1)}, u32[]{:S(2)}, u32[]{:S(2)}) collective-permute-start(bf16[128,512]{1,0:T(8,128)(2,1)S(1)} %shard_map.101), channel_id=1, source_target_pairs={{0,8},{1,9},{2,10},{3,11},{4,12},{5,13},{6,14},{7,15},{8,0},{9,1},... | collective-permute-start | bytes 393224 | tf_op jit(solution)/shard_map/ppermute | solution.py:31
  158.1 13.3 %collective-permute-start.13 = (bf16[2,256,256]{2,1,0:T(8,128)(2,1)S(1)}, bf16[2,256,256]{2,1,0:T(8,128)(2,1)S(1)}, u32[]{:S(2)}, u32[]{:S(2)}) collective-permute-start(bf16[2,256,256]{2,1,0:T(8,128)(2,1)S(1)} %get-tuple-element.64), channel_id=1, source_target_pairs={{0,1},{1,0},{2,3},{3,2},{4,5},{5,4},{6,7},{7,6},{8,9},{9,8},{10,11... | collective-permute-start | bytes 786440 | tf_op jit(solution)/shard_map/ppermute | solution.py:35
  160.2 8.9 %collective-permute-start.15 = (bf16[2,64,256]{2,1,0:T(8,128)(2,1)S(1)}, bf16[2,64,256]{2,1,0:T(8,128)(2,1)S(1)}, u32[]{:S(2)}, u32[]{:S(2)}) collective-permute-start(bf16[2,64,256]{2,1,0:T(8,128)(2,1)S(1)} %get-tuple-element.66), channel_id=1, source_target_pairs={{0,17},{1,16},{2,19},{3,18},{4,21},{5,20},{6,23},{7,22},{8,25},{9,... | collective-permute-start | bytes 196616 | tf_op jit(solution)/shard_map/ppermute | solution.py:351
  162.1 9.2 %collective-permute-start.14 = (bf16[2,64,256]{2,1,0:T(8,128)(2,1)S(1)}, bf16[2,64,256]{2,1,0:T(8,128)(2,1)S(1)}, u32[]{:S(2)}, u32[]{:S(2)}) collective-permute-start(bf16[2,64,256]{2,1,0:T(8,128)(2,1)S(1)} %get-tuple-element.65), channel_id=1, source_target_pairs={{0,16},{16,32},{32,48},{48,64},{64,80},{80,96},{96,112},{112,128},... | collective-permute-start | bytes 196616 | tf_op jit(solution)/shard_map/ppermute | solution.py:40
  171.3 1.2 copy-start.9

commit v7 on v5

--- a/solution.py
+++ b/solution.py
@@ -290,7 +290,7 @@
     own_up = up[0].reshape(JOBS * RANK, width)
 
     w_own = frozen[0]
-    w_pair = across_x(in_order((w_own,), own)[0], devices)
+    w_pair = across_x(in_order((w_own,), to_below)[0], devices)
 
     ring_1 = in_order(ring_1, cot_line)
     ring_2 = step(ring_1)

time: 173 us -> 173 us (level)
    ppermute x1, waiting for transfers between devices: 7.28 us -> 1.66 us  [on_device(): lax.ppermute(handed[0], 'section', [(i, (i + 1) % sections) for i in rang...]
    all_to_all x3, waiting for transfers between devices: 6.59 us -> 12.1 us  [to_line(): lax.all_to_all(value, 'dp', 0, 0, axis_index_groups=lines, tiled=True)]
    ppermute x2, starting transfers between devices: 3.96 us -> 8.84 us  [to_host(): lax.ppermute(there, ('section', 'dp'), route)]
    ppermute x4, starting transfers between devices: 12.4 us -> 8.4 us  [section_shift(): return lax.ppermute(value, 'section', route)]
    ppermute x9, waiting for transfers between devices: 31.5 us -> 29.1 us  [along_z(): return lax.ppermute(value, 'dp', route)]
    all_to_all x3, starting transfers between devices: 18.1 us -> 20.3 us  [to_line(): lax.all_to_all(value, 'dp', 0, 0, axis_index_groups=lines, tiled=True)]
    ppermute x9, starting transfers between devices: 24.2 us -> 22 us  [along_z(): return lax.ppermute(value, 'dp', route)]
    ppermute x2, waiting for transfers between devices: 0.01 us -> 1.85 us  [across_x(): return lax.ppermute(value, 'dp', [(d, d ^ 1) for d in range(devices)])]
  transfers between devices with their start and end apart: 21 -> 21, of which waited for: 11 -> 9; matrix products, arithmetic and copies ran while one was open for 2% -> 2% of each run, Pallas kernels for 14% -> 14%
where the time goes in v7:
time: 173 us
  waiting for transfers between devices  65 us (38%)
  starting transfers between devices  61.2 us (35%)
  Pallas kernels  26.6 us (15%)
  local copies, waits for them, and re-layouts  15.6 us (9%)
  other arithmetic  3.08 us (2%)
    ppermute x9, waiting for transfers between devices, along_z(): return lax.ppermute(value, 'dp', route)  29.1 us
    pallas_call x8, Pallas kernels, kernel_call(): pl.pallas_call(kernel, out_shape=tuple((jax.ShapeDtypeStruct(shape, dtype...  22.4 us
    ppermute x9, starting transfers between devices, along_z(): return lax.ppermute(value, 'dp', route)  22 us
    all_to_all x3, starting transfers between devices, to_line(): lax.all_to_all(value, 'dp', 0, 0, axis_index_groups=lines, tiled=True)  20.3 us
    ppermute x4, waiting for transfers between devices, section_shift(): return lax.ppermute(value, 'section', route)  16.1 us
    unnamed x39, local copies, waits for them, and re-layouts  15.2 us
    all_to_all x3, waiting for transfers between devices, to_line(): lax.all_to_all(value, 'dp', 0, 0, axis_index_groups=lines, tiled=True)  12.1 us
    ppermute x2, starting transfers between devices, to_host(): lax.ppermute(there, ('section', 'dp'), route)  8.84 us
  transfers between devices with their start and end apart: 21, of which 9 were waited for; matrix products, arithmetic and copies ran while one was open for 2% of the time, Pallas kernels for 14%

profile of v7, /device:TPU:6, one launch (start us, length us, event | category | flops | bytes accessed | tf_op | source)
XLA Modules:
  0.0 172.5 jit_solution(16880120957183644196)
XLA Ops:
  0.7 1.2 copy-done.5
  2.0 1.1 shard_map.94
  3.0 8.5 %all-to-all-start = ((bf16[8,128,512]{2,1,0:T(8,128)(2,1)}), bf16[8,128,512]{2,1,0:T(8,128)(2,1)}, u32[]{:S(2)}, u32[]{:S(2)}) async-start(bf16[8,128,512]{2,1,0:T(8,128)(2,1)} %shard_map.94), calls=%async_computation | async-start | bytes 2097152 | tf_op jit(solution)/shard_map/all_to_all | solution.py:277
  11.8 1.6 copy-done.1
  13.4 1.6 copy-done.3
  15.0 2.1 %shard_map.95 = (bf16[128,4096]{1,0:T(8,128)(2,1)}, bf16[128,4096]{1,0:T(8,128)(2,1)}) custom-call(s32[3]{0:T(128)S(1)} %pad_add_fusion.place, s32[128]{0:T(128)S(1)} %reshape.75.plan, bf16[4,64,4096]{2,1,0:T(8,128)(2,1)S(1)} %bitcast.36, bf16[4,64,4096]{2,1,0:T(8,128)(2,1)S(1)} %bitcast.38), custom_call_target="tpu_custom_call" | custom-call | flops 1024 | bytes 1024 | tf_op jit(solution)/shard_map/pallas_call | solution.py:73
  17.1 1.7 collective-permute-done.own_x.refs_0_
  19.6 1.9 %collective-permute-start.1 = (bf16[128,4096]{1,0:T(8,128)(2,1)S(1)}, bf16[128,4096]{1,0:T(8,128)(2,1)}, u32[]{:S(2)}, u32[]{:S(2)}) collective-permute-start(bf16[128,4096]{1,0:T(8,128)(2,1)S(1)} %collective-permute-done.own_x.refs_0_), channel_id=1, source_target_pairs={{0,2},{1,3},{2,4},{3,5},{4,6},{5,7},{6,8},{7,9},{8,10},{9,11},{10,... | collective-permute-start | bytes 3145736 | tf_op jit(solution)/shard_map/ppermute | solution.py:31
  21.5 3.9 %collective-permute-start.2 = (bf16[128,4096]{1,0:T(8,128)(2,1)S(1)}, bf16[128,4096]{1,0:T(8,128)(2,1)}, u32[]{:S(2)}, u32[]{:S(2)}) collective-permute-start(bf16[128,4096]{1,0:T(8,128)(2,1)S(1)} %collective-permute-done.own_x.refs_0_), channel_id=1, source_target_pairs={{0,14},{1,15},{2,0},{3,1},{4,2},{5,3},{6,4},{7,5},{8,6},{9,7},{10,... | collective-permute-start | bytes 3145736 | tf_op jit(solution)/shard_map/ppermute | solution.py:31
  25.4 2.5 %collective-permute-start.4 = (bf16[128,4096]{1,0:T(8,128)(2,1)}, bf16[128,4096]{1,0:T(8,128)(2,1)}, u32[]{:S(2)}, u32[]{:S(2)}) collective-permute-start(bf16[128,4096]{1,0:T(8,128)(2,1)} %get-tuple-element.42), channel_id=1, source_target_pairs={{16,0},{32,16},{48,32},{64,48},{80,64},{96,80},{112,96},{128,112},... | collective-permute-start | bytes 3145736 | tf_op jit(solution)/shard_map/ppermute | solution.py:40
  28.0 1.9 %collective-permute-start.5 = (bf16[128,4096]{1,0:T(8,128)(2,1)}, bf16[128,4096]{1,0:T(8,128)(2,1)}, u32[]{:S(2)}, u32[]{:S(2)}) collective-permute-start(bf16[128,4096]{1,0:T(8,128)(2,1)} %get-tuple-element.45), channel_id=1, source_target_pairs={{0,16},{16,32},{32,48},{48,64},{64,80},{80,96},{96,112},{112,128},... | collective-permute-start | bytes 3145736 | tf_op jit(solution)/shard_map/ppermute | solution.py:40
  29.9 12.0 %all-to-all-done.cot_line = bf16[8,128,512]{2,1,0:T(8,128)(2,1)} async-done(((bf16[8,128,512]{2,1,0:T(8,128)(2,1)}), bf16[8,128,512]{2,1,0:T(8,128)(2,1)}, u32[]{:S(2)}, u32[]{:S(2)}) %all-to-all-start) | async-done | bytes 1048608 | tf_op jit(solution)/shard_map/all_to_all | solution.py:277
  42.0 19.2 %collective-permute-done.1.refs_1_ = bf16[128,4096]{1,0:T(8,128)(2,1)} collective-permute-done((bf16[128,4096]{1,0:T(8,128)(2,1)S(1)}, bf16[128,4096]{1,0:T(8,128)(2,1)}, u32[]{:S(2)}, u32[]{:S(2)}) %collective-permute-start.1) | collective-permute-done | bytes 1048608 | tf_op jit(solution)/shard_map/ppermute | solution.py:31
  61.4 3.0 %collective-permute-start.7 = (bf16[128,4096]{1,0:T(8,128)(2,1)}, bf16[128,4096]{1,0:T(8,128)(2,1)}, u32[]{:S(2)}, u32[]{:S(2)}) collective-permute-start(bf16[128,4096]{1,0:T(8,128)(2,1)} %collective-permute-done.2.refs_2_), channel_id=1, source_target_pairs={{0,14},{1,15},{2,0},{3,1},{4,2},{5,3},{6,4},{7,5},{8,6},{9,7},{10,... | collective-permute-start | bytes 3145736 | tf_op jit(solution)/shard_map/ppermute | solution.py:31
  64.4 1.8 %collective-permute-done.3.refs_6_.w_pair = bf16[4096,256]{1,0:T(8,128)(2,1)} collective-permute-done((bf16[4096,256]{1,0:T(8,128)(2,1)S(1)}, bf16[4096,256]{1,0:T(8,128)(2,1)}, u32[]{:S(2)}, u32[]{:S(2)}) %collective-permute-start.3) | collective-permute-done | bytes 2097184 | tf_op jit(solution)/shard_map/ppermute | solution.py:35
  66.2 9.6 %collective-permute-done.4.above = bf16[128,4096]{1,0:T(8,128)(2,1)} collective-permute-done((bf16[128,4096]{1,0:T(8,128)(2,1)}, bf16[128,4096]{1,0:T(8,128)(2,1)}, u32[]{:S(2)}, u32[]{:S(2)}) %collective-permute-start.4) | collective-permute-done | bytes 1048608 | tf_op jit(solution)/shard_map/ppermute | solution.py:40
  75.8 3.6 %collective-permute-done.5.below = bf16[128,4096]{1,0:T(8,128)(2,1)} collective-permute-done((bf16[128,4096]{1,0:T(8,128)(2,1)}, bf16[128,4096]{1,0:T(8,128)(2,1)}, u32[]{:S(2)}, u32[]{:S(2)}) %collective-permute-start.5) | collective-permute-done | bytes 1048608 | tf_op jit(solution)/shard_map/ppermute | solution.py:40
  79.4 1.6 copy-done.2
  81.0 1.6 copy-done.4
  82.6 1.2 copy-done.6
  83.8 4.1 %shard_map.96 = (bf16[128,4096]{1,0:T(8,128)(2,1)S(1)}, bf16[8,144,128]{2,1,0:T(8,128)(2,1)S(1)}) custom-call(s32[3]{0:T(128)S(1)} %pad_add_fusion.place, s32[4]{0:T(128)S(1)} %bitcast.42, s32[128]{0:T(128)S(1)} %reshape.75.plan, bf16[128,4096]{1,0:T(8,128)(2,1)S(1)} %collective-permute-done.own_x.refs_0_, bf16[128,4096]{1,0:T(8,128)(2,1)S(1)} %bitcast.41, ...), custom_call_target="tpu_custom_call" | custom-call | flops 1024 | bytes 1024 | tf_op jit(solution)/shard_map/pallas_call | solution.py:90
  87.9 1.0 copy-done.7
  89.6 2.0 %collective-permute-start.8 = (bf16[128,4096]{1,0:T(8,128)(2,1)}, bf16[128,4096]{1,0:T(8,128)(2,1)}, u32[]{:S(2)}, u32[]{:S(2)}) collective-permute-start(bf16[128,4096]{1,0:T(8,128)(2,1)} %collective-permute-done.6.refs_3_), channel_id=1, source_target_pairs={{0,2},{1,3},{2,4},{3,5},{4,6},{5,7},{6,8},{7,9},{8,10},{9,11},{10,... | collective-permute-start | bytes 3145736 | tf_op jit(solution)/shard_map/ppermute | solution.py:31
  91.6 1.9 %collective-permute-start.9 = (bf16[128,4096]{1,0:T(8,128)(2,1)}, bf16[128,4096]{1,0:T(8,128)(2,1)}, u32[]{:S(2)}, u32[]{:S(2)}) collective-permute-start(bf16[128,4096]{1,0:T(8,128)(2,1)} %collective-permute-done.7.refs_4_), channel_id=1, source_target_pairs={{0,14},{1,15},{2,0},{3,1},{4,2},{5,3},{6,4},{7,5},{8,6},{9,7},{10,... | collective-permute-start | bytes 3145736 | tf_op jit(solution)/shard_map/ppermute | solution.py:31
  93.5 6.6 %all-to-all-start.2 = ((bf16[8,144,128]{2,1,0:T(8,128)(2,1)}), bf16[8,144,128]{2,1,0:T(8,128)(2,1)S(1)}, u32[]{:S(2)}, u32[]{:S(2)}) async-start(bf16[8,144,128]{2,1,0:T(8,128)(2,1)} %copy-done.14), calls=%async_computation.2 | async-start | bytes 589824 | tf_op jit(solution)/shard_map/all_to_all | solution.py:277
  100.1 5.7 %shard_map.97 = (bf16[5,128,512]{2,1,0:T(8,128)(2,1)S(1)}, bf16[5,128,512]{2,1,0:T(8,128)(2,1)S(1)}) custom-call(s32[3]{0:T(128)S(1)} %pad_add_fusion.place, bf16[128,4096]{1,0:T(8,128)(2,1)S(1)} %collective-permute-done.own_x.refs_0_, bf16[128,4096]{1,0:T(8,128)(2,1)} %collective-permute-done.1.refs_1_, bf16[128,4096]{1,0:T(8,128)(2,1)} %collective-permute-done.2.refs_2_, ...), custom_call_target="tpu_custom_call" | custom-call | flops 1024 | bytes 1024 | tf_op jit(solution)/shard_map/pallas_call | solution.py:90
  105.8 0.8 copy-done.10
  106.7 0.8 copy-done.12
  107.5 9.9 %collective-permute-done.8.f3 = bf16[128,4096]{1,0:T(8,128)(2,1)} collective-permute-done((bf16[128,4096]{1,0:T(8,128)(2,1)}, bf16[128,4096]{1,0:T(8,128)(2,1)}, u32[]{:S(2)}, u32[]{:S(2)}) %collective-permute-start.8) | collective-permute-done | bytes 1048608 | tf_op jit(solution)/shard_map/ppermute | solution.py:31
  117.4 2.2 %shard_map.98 = (bf16[64,4096]{1,0:T(8,128)(2,1)}, bf16[64,4096]{1,0:T(8,128)(2,1)}) custom-call(bf16[128,4096]{1,0:T(8,128)(2,1)} %collective-permute-done.8.f3, bf16[128,4096]{1,0:T(8,128)(2,1)} %collective-permute-done.9.r3), custom_call_target="tpu_custom_call" | custom-call | flops 1024 | bytes 1024 | tf_op jit(solution)/shard_map/pallas_call | solution.py:73
  119.6 1.4 collective-permute-start.10
  120.9 2.0 %collective-permute-start.11 = (bf16[64,4096]{1,0:T(8,128)(2,1)}, bf16[64,4096]{1,0:T(8,128)(2,1)}, u32[]{:S(2)}, u32[]{:S(2)}) collective-permute-start(bf16[64,4096]{1,0:T(8,128)(2,1)} %get-tuple-element.58), channel_id=1, source_target_pairs={{0,14},{1,15},{2,0},{3,1},{4,2},{5,3},{6,4},{7,5},{8,6},{9,7},{10,... | collective-permute-start | bytes 1572872 | tf_op jit(solution)/shard_map/ppermute | solution.py:31
  122.9 1.1 copy-done.13
  124.0 3.5 %shard_map.99 = (bf16[8,128,512]{2,1,0:T(8,128)(2,1)S(1)}, bf16[2,128,512]{2,1,0:T(8,128)(2,1)S(1)}) custom-call(s32[3]{0:T(128)S(1)} %pad_add_fusion.place, bf16[5,128,512]{2,1,0:T(8,128)(2,1)S(1)} %copy-done.13, bf16[128,4096]{1,0:T(8,128)(2,1)} %collective-permute-done.8.f3, bf16[128,4096]{1,0:T(8,128)(2,1)} %collective-permute-done.9.r3, ...), custom_call_target="tpu_custom_call" | custom-call | flops 1024 | bytes 1024 | tf_op jit(solution)/shard_map/pallas_call | solution.py:90
  127.5 1.0 copy-done.9
  129.2 5.3 %all-to-all-start.1 = ((bf16[8,128,512]{2,1,0:T(8,128)(2,1)}), bf16[8,128,512]{2,1,0:T(8,128)(2,1)S(1)}, u32[]{:S(2)}, u32[]{:S(2)}) async-start(bf16[8,128,512]{2,1,0:T(8,128)(2,1)} %copy-done.9), calls=%async_computation.1 | async-start | bytes 2097152 | tf_op jit(solution)/shard_map/all_to_all | solution.py:277
  136.0 2.0 %shard_map.100 = (f32[384,256]{1,0:T(8,128)S(1)}, bf16[384,256]{1,0:T(8,128)(2,1)S(1)}) custom-call(s32[3]{0:T(128)S(1)} %pad_add_fusion.place, bf16[8,144,128]{2,1,0:T(8,128)(2,1)S(1)} %all-to-all-done.2.line, bf16[8,128,512]{2,1,0:T(8,128)(2,1)} %all-to-all-done.cot_line), custom_call_target="tpu_custom_call" | custom-call | flops 1024 | bytes 1024 | tf_op jit(solution)/shard_map/pallas_call | solution.py:90
  138.1 2.7 %shard_map.101 = (bf16[128,512]{1,0:T(8,128)(2,1)S(1)}, bf16[128,512]{1,0:T(8,128)(2,1)S(1)}) custom-call(s32[3]{0:T(128)S(1)} %pad_add_fusion.place, bf16[64,4096]{1,0:T(8,128)(2,1)} %collective-permute-done.10.first_half, bf16[64,4096]{1,0:T(8,128)(2,1)} %collective-permute-done.11.second_half, bf16[4096,256]{1,0:T(8,128)(2,1)S(1)} %bitcast.35, ...), custom_call_target="tpu_custom_call" | custom-call | flops 1024 | bytes 1048576 | tf_op jit(solution)/shard_map/pallas_call | solution.py:90
  140.8 1.3 shard_map.103
  142.2 6.2 %collective-permute-start.17 = (bf16[2,64,256]{2,1,0:T(8,128)(2,1)S(1)}, bf16[2,64,256]{2,1,0:T(8,128)(2,1)S(1)}, u32[]{:S(2)}, u32[]{:S(2)}) collective-permute-start(bf16[2,64,256]{2,1,0:T(8,128)(2,1)S(1)} %get-tuple-element.72), channel_id=1, source_target_pairs={{16,1},{17,0},{18,3},{19,2},{20,5},{21,4},{22,7},{23,6},{24,9},{25... | collective-permute-start | bytes 196616 | tf_op jit(solution)/shard_map/ppermute | solution.py:351
  148.4 2.0 %collective-permute-start.16 = (bf16[2,64,256]{2,1,0:T(8,128)(2,1)S(1)}, bf16[2,64,256]{2,1,0:T(8,128)(2,1)S(1)}, u32[]{:S(2)}, u32[]{:S(2)}) collective-permute-start(bf16[2,64,256]{2,1,0:T(8,128)(2,1)S(1)} %get-tuple-element.71), channel_id=1, source_target_pairs={{16,0},{32,16},{48,32},{64,48},{80,64},{96,80},{112,96},{128,112},... | collective-permute-start | bytes 196616 | tf_op jit(solution)/shard_map/ppermute | solution.py:40
  151.0 5.7 %collective-permute-start.12 = (bf16[128,512]{1,0:T(8,128)(2,1)S(1)}, bf16[128,512]{1,0:T(8,128)(2,1)S(1)}, u32[]{:S(2)}, u32[]{:S(2)}) collective-permute-start(bf16[128,512]{1,0:T(8,128)(2,1)S(1)} %get-tuple-element.63), channel_id=1, source_target_pairs={{0,8},{1,9},{2,10},{3,11},{4,12},{5,13},{6,14},{7,15},{8,0},{9,1},... | collective-permute-start | bytes 393224 | tf_op jit(solution)/shard_map/ppermute | solution.py:31
  157.5 2.6 %collective-permute-start.15 = (bf16[2,64,256]{2,1,0:T(8,128)(2,1)S(1)}, bf16[2,64,256]{2,1,0:T(8,128)(2,1)S(1)}, u32[]{:S(2)}, u32[]{:S(2)}) collective-permute-start(bf16[2,64,256]{2,1,0:T(8,128)(2,1)S(1)} %get-tuple-element.70), channel_id=1, source_target_pairs={{0,17},{1,16},{2,19},{3,18},{4,21},{5,20},{6,23},{7,22},{8,25},{9,... | collective-permute-start | bytes 196616 | tf_op jit(solution)/shard_map/ppermute | solution.py:351
  160.2 1.9 %collective-permute-start.14 = (bf16[2,64,256]{2,1,0:T(8,128)(2,1)S(1)}, bf16[2,64,256]{2,1,0:T(8,128)(2,1)S(1)}, u32[]{:S(2)}, u32[]{:S(2)}) collective-permute-start(bf16[2,64,256]{2,1,0:T(8,128)(2,1)S(1)} %get-tuple-element.69), channel_id=1, source_target_pairs={{0,16},{16,32},{32,48},{48,64},{64,80},{80,96},{96,112},{112,128},... | collective-permute-start | bytes 196616 | tf_op jit(solution)/shard_map/ppermute | solution.py:40
  162.2 4.3 %collective-permute-done.15 = bf16[2,64,256]{2,1,0:T(8,128)(2,1)S(1)} collective-permute-done((bf16[2,64,256]{2,1,0:T(8,128)(2,1)S(1)}, bf16[2,64,256]{2,1,0:T(8,128)(2,1)S(1)}, u32[]{:S(2)}, u32[]{:S(2)}) %collective-permute-start.15) | collective-permute-done | bytes 65568 | tf_op jit(solution)/shard_map/ppermute | solution.py:351
  166.4 3.0 %collective-permute-done.14 = bf16[2,64,256]{2,1,0:T(8,128)(2,1)S(1)} collective-permute-done((bf16[2,64,256]{2,1,0:T(8,128)(2,1)S(1)}, bf16[2,64,256]{2,1,0:T(8,128)(2,1)S(1)}, u32[]{:S(2)}, u32[]{:S(2)}) %collective-permute-start.14) | collective-permute-done | bytes 65568 | tf_op jit(solution)/shard_map/ppermute | solution.py:40
  169.6 0.9 select_add_fusion
  170.6 1.9 %shard_map.102 = bf16[128,4096]{1,0:T(8,128)(2,1)} custom-call(s32[3]{0:T(128)S(1)} %pad_add_fusion.place, bf16[128,4096]{1,0:T(8,128)(2,1)S(1)} %copy-done.8, bf16[8,128,512]{2,1,0:T(8,128)(2,1)S(1)} %all-to-all-done.1.results, bf16[128,512]{1,0:T(8,128)(2,1)S(1)} %collective-permute-done.12.last), custom_call_target="tpu_custom_call" | custom-call | flops 1024 | bytes 1024 | tf_op jit(solution)/shard_map/pallas_call | solution.py:90
  (58 shorter events, 6.2 us)
Async XLA Ops:
  0.6 18.1 %collective-permute-start = (bf16[128,4096]{1,0:T(8,128)(2,1)}, bf16[128,4096]{1,0:T(8,128)(2,1)S(1)}, u32[]{:S(2)}, u32[]{:S(2)}) collective-permute-start(bf16[128,4096]{1,0:T(8,128)(2,1)} %bitcast.48), channel_id=1, source_target_pairs={{0,16},{16,32},{32,48},{48,64},{64,80},{80,96},{96,112},{112,128},... | collective-permute-start | bytes 3145736 | tf_op jit(solution)/shard_map/ppermute | solution.py:274
  0.7 1.2 copy-start.5
  1.9 9.5 %copy-start.18 = (s32[16,4,2]{0,2,1:T(2,128)S(1)}, s32[16,4,2]{0,2,1:T(2,128)}, u32[]{:S(2)}) copy-start(s32[16,4,2]{0,2,1:T(2,128)} %param.9) | copy-start | bytes 1540
  3.0 39.0 %all-to-all-start = ((bf16[8,128,512]{2,1,0:T(8,128)(2,1)}), bf16[8,128,512]{2,1,0:T(8,128)(2,1)}, u32[]{:S(2)}, u32[]{:S(2)}) async-start(bf16[8,128,512]{2,1,0:T(8,128)(2,1)} %shard_map.94), calls=%async_computation | async-start | bytes 2097152 | tf_op jit(solution)/shard_map/all_to_all | solution.py:277
  11.8 1.6 copy-start.1
  13.4 1.6 copy-start.3
  15.0 3.8 %copy-start = (bf16[1,4096,256]{2,1,0:T(8,128)(2,1)S(1)}, bf16[1,4096,256]{2,1,0:T(8,128)(2,1)}, u32[]{:S(2)}) copy-start(bf16[1,4096,256]{2,1,0:T(8,128)(2,1)} %param.10) | copy-start | bytes 6291460
  15.0 64.4 %copy-start.17 = (s32[1,1,4]{2,1,0:T(1,128)S(1)}, s32[1,1,4]{2,1,0:T(1,128)}, u32[]{:S(2)}) copy-start(s32[1,1,4]{2,1,0:T(1,128)} %param.8) | copy-start | bytes 52
  18.8 47.5 %collective-permute-start.3 = (bf16[4096,256]{1,0:T(8,128)(2,1)S(1)}, bf16[4096,256]{1,0:T(8,128)(2,1)}, u32[]{:S(2)}, u32[]{:S(2)}) collective-permute-start(bf16[4096,256]{1,0:T(8,128)(2,1)S(1)} %bitcast.32), channel_id=1, source_target_pairs={{0,1},{1,0},{2,3},{3,2},{4,5},{5,4},{6,7},{7,6},{8,9},{9,8},{10,11... | collective-permute-start | bytes 6291464 | tf_op jit(solution)/shard_map/ppermute | solution.py:35
  19.6 41.6 %collective-permute-start.1 = (bf16[128,4096]{1,0:T(8,128)(2,1)S(1)}, bf16[128,4096]{1,0:T(8,128)(2,1)}, u32[]{:S(2)}, u32[]{:S(2)}) collective-permute-start(bf16[128,4096]{1,0:T(8,128)(2,1)S(1)} %collective-permute-done.own_x.refs_0_), channel_id=1, source_target_pairs={{0,2},{1,3},{2,4},{3,5},{4,6},{5,7},{6,8},{7,9},{8,10},{9,11},{10,... | collective-permute-start | bytes 3145736 | tf_op jit(solution)/shard_map/ppermute | solution.py:31
  21.5 39.6 %collective-permute-start.2 = (bf16[128,4096]{1,0:T(8,128)(2,1)S(1)}, bf16[128,4096]{1,0:T(8,128)(2,1)}, u32[]{:S(2)}, u32[]{:S(2)}) collective-permute-start(bf16[128,4096]{1,0:T(8,128)(2,1)S(1)} %collective-permute-done.own_x.refs_0_), channel_id=1, source_target_pairs={{0,14},{1,15},{2,0},{3,1},{4,2},{5,3},{6,4},{7,5},{8,6},{9,7},{10,... | collective-permute-start | bytes 3145736 | tf_op jit(solution)/shard_map/ppermute | solution.py:31
  25.4 50.4 %collective-permute-start.4 = (bf16[128,4096]{1,0:T(8,128)(2,1)}, bf16[128,4096]{1,0:T(8,128)(2,1)}, u32[]{:S(2)}, u32[]{:S(2)}) collective-permute-start(bf16[128,4096]{1,0:T(8,128)(2,1)} %get-tuple-element.42), channel_id=1, source_target_pairs={{16,0},{32,16},{48,32},{64,48},{80,64},{96,80},{112,96},{128,112},... | collective-permute-start | bytes 3145736 | tf_op jit(solution)/shard_map/ppermute | solution.py:40
  28.0 51.4 %collective-permute-start.5 = (bf16[128,4096]{1,0:T(8,128)(2,1)}, bf16[128,4096]{1,0:T(8,128)(2,1)}, u32[]{:S(2)}, u32[]{:S(2)}) collective-permute-start(bf16[128,4096]{1,0:T(8,128)(2,1)} %get-tuple-element.45), channel_id=1, source_target_pairs={{0,16},{16,32},{32,48},{48,64},{64,80},{80,96},{96,112},{112,128},... | collective-permute-start | bytes 3145736 | tf_op jit(solution)/shard_map/ppermute | solution.py:40
  61.2 28.5 %collective-permute-start.6 = (bf16[128,4096]{1,0:T(8,128)(2,1)}, bf16[128,4096]{1,0:T(8,128)(2,1)}, u32[]{:S(2)}, u32[]{:S(2)}) collective-permute-start(bf16[128,4096]{1,0:T(8,128)(2,1)} %collective-permute-done.1.refs_1_), channel_id=1, source_target_pairs={{0,2},{1,3},{2,4},{3,5},{4,6},{5,7},{6,8},{7,9},{8,10},{9,11},{10,... | collective-permute-start | bytes 3145736 | tf_op jit(solution)/shard_map/ppermute | solution.py:31
  61.4 28.2 %collective-permute-start.7 = (bf16[128,4096]{1,0:T(8,128)(2,1)}, bf16[128,4096]{1,0:T(8,128)(2,1)}, u32[]{:S(2)}, u32[]{:S(2)}) collective-permute-start(bf16[128,4096]{1,0:T(8,128)(2,1)} %collective-permute-done.2.refs_2_), channel_id=1, source_target_pairs={{0,14},{1,15},{2,0},{3,1},{4,2},{5,3},{6,4},{7,5},{8,6},{9,7},{10,... | collective-permute-start | bytes 3145736 | tf_op jit(solution)/shard_map/ppermute | solution.py:31
  79.4 1.6 copy-start.2
  81.0 1.6 copy-start.4
  82.6 1.2 copy-start.6
  87.9 1.0 copy-start.7
  88.9 0.7 copy-start.14
  89.6 27.8 %collective-permute-start.8 = (bf16[128,4096]{1,0:T(8,128)(2,1)}, bf16[128,4096]{1,0:T(8,128)(2,1)}, u32[]{:S(2)}, u32[]{:S(2)}) collective-permute-start(bf16[128,4096]{1,0:T(8,128)(2,1)} %collective-permute-done.6.refs_3_), channel_id=1, source_target_pairs={{0,2},{1,3},{2,4},{3,5},{4,6},{5,7},{6,8},{7,9},{8,10},{9,11},{10,... | collective-permute-start | bytes 3145736 | tf_op jit(solution)/shard_map/ppermute | solution.py:31
  91.6 25.8 %collective-permute-start.9 = (bf16[128,4096]{1,0:T(8,128)(2,1)}, bf16[128,4096]{1,0:T(8,128)(2,1)}, u32[]{:S(2)}, u32[]{:S(2)}) collective-permute-start(bf16[128,4096]{1,0:T(8,128)(2,1)} %collective-permute-done.7.refs_4_), channel_id=1, source_target_pairs={{0,14},{1,15},{2,0},{3,1},{4,2},{5,3},{6,4},{7,5},{8,6},{9,7},{10,... | collective-permute-start | bytes 3145736 | tf_op jit(solution)/shard_map/ppermute | solution.py:31
  93.5 35.7 %all-to-all-start.2 = ((bf16[8,144,128]{2,1,0:T(8,128)(2,1)}), bf16[8,144,128]{2,1,0:T(8,128)(2,1)S(1)}, u32[]{:S(2)}, u32[]{:S(2)}) async-start(bf16[8,144,128]{2,1,0:T(8,128)(2,1)} %copy-done.14), calls=%async_computation.2 | async-start | bytes 589824 | tf_op jit(solution)/shard_map/all_to_all | solution.py:277
  105.8 0.9 copy-start.10
  106.7 0.8 copy-start.12
  119.6 18.5 %collective-permute-start.10 = (bf16[64,4096]{1,0:T(8,128)(2,1)}, bf16[64,4096]{1,0:T(8,128)(2,1)}, u32[]{:S(2)}, u32[]{:S(2)}) collective-permute-start(bf16[64,4096]{1,0:T(8,128)(2,1)} %get-tuple-element.54), channel_id=1, source_target_pairs={{0,2},{1,3},{2,4},{3,5},{4,6},{5,7},{6,8},{7,9},{8,10},{9,11},{10,... | collective-permute-start | bytes 1572872 | tf_op jit(solution)/shard_map/ppermute | solution.py:31
  120.9 17.1 %collective-permute-start.11 = (bf16[64,4096]{1,0:T(8,128)(2,1)}, bf16[64,4096]{1,0:T(8,128)(2,1)}, u32[]{:S(2)}, u32[]{:S(2)}) collective-permute-start(bf16[64,4096]{1,0:T(8,128)(2,1)} %get-tuple-element.58), channel_id=1, source_target_pairs={{0,14},{1,15},{2,0},{3,1},{4,2},{5,3},{6,4},{7,5},{8,6},{9,7},{10,... | collective-permute-start | bytes 1572872 | tf_op jit(solution)/shard_map/ppermute | solution.py:31
  122.9 1.1 copy-start.13
  127.5 1.0 copy-start.9
  128.5 0.7 copy-start.15
  129.2 41.4 %all-to-all-start.1 = ((bf16[8,128,512]{2,1,0:T(8,128)(2,1)}), bf16[8,128,512]{2,1,0:T(8,128)(2,1)S(1)}, u32[]{:S(2)}, u32[]{:S(2)}) async-start(bf16[8,128,512]{2,1,0:T(8,128)(2,1)} %copy-done.9), calls=%async_computation.1 | async-start | bytes 2097152 | tf_op jit(solution)/shard_map/all_to_all | solution.py:277
  138.1 2.7 %copy-start.11 = (bf16[5,128,512]{2,1,0:T(8,128)(2,1)S(1)}, bf16[5,128,512]{2,1,0:T(8,128)(2,1)}, u32[]{:S(2)}) copy-start(bf16[5,128,512]{2,1,0:T(8,128)(2,1)} %copy-done.10) | copy-start | bytes 1966084
  138.1 2.7 %copy-start.16 = (bf16[2,128,512]{2,1,0:T(8,128)(2,1)S(1)}, bf16[2,128,512]{2,1,0:T(8,128)(2,1)}, u32[]{:S(2)}) copy-start(bf16[2,128,512]{2,1,0:T(8,128)(2,1)} %copy-done.15) | copy-start | bytes 786436
  142.2 18.0 %collective-permute-start.17 = (bf16[2,64,256]{2,1,0:T(8,128)(2,1)S(1)}, bf16[2,64,256]{2,1,0:T(8,128)(2,1)S(1)}, u32[]{:S(2)}, u32[]{:S(2)}) collective-permute-start(bf16[2,64,256]{2,1,0:T(8,128)(2,1)S(1)} %get-tuple-element.72), channel_id=1, source_target_pairs={{16,1},{17,0},{18,3},{19,2},{20,5},{21,4},{22,7},{23,6},{24,9},{25... | collective-permute-start | bytes 196616 | tf_op jit(solution)/shard_map/ppermute | solution.py:351
  148.4 13.8 %collective-permute-start.16 = (bf16[2,64,256]{2,1,0:T(8,128)(2,1)S(1)}, bf16[2,64,256]{2,1,0:T(8,128)(2,1)S(1)}, u32[]{:S(2)}, u32[]{:S(2)}) collective-permute-start(bf16[2,64,256]{2,1,0:T(8,128)(2,1)S(1)} %get-tuple-element.71), channel_id=1, source_target_pairs={{16,0},{32,16},{48,32},{64,48},{80,64},{96,80},{112,96},{128,112},... | collective-permute-start | bytes 196616 | tf_op jit(solution)/shard_map/ppermute | solution.py:40
  151.0 19.5 %collective-permute-start.12 = (bf16[128,512]{1,0:T(8,128)(2,1)S(1)}, bf16[128,512]{1,0:T(8,128)(2,1)S(1)}, u32[]{:S(2)}, u32[]{:S(2)}) collective-permute-start(bf16[128,512]{1,0:T(8,128)(2,1)S(1)} %get-tuple-element.63), channel_id=1, source_target_pairs={{0,8},{1,9},{2,10},{3,11},{4,12},{5,13},{6,14},{7,15},{8,0},{9,1},... | collective-permute-start | bytes 393224 | tf_op jit(solution)/shard_map/ppermute | solution.py:31
  156.8 12.7 %collective-permute-start.13 = (bf16[2,256,256]{2,1,0:T(8,128)(2,1)S(1)}, bf16[2,256,256]{2,1,0:T(8,128)(2,1)S(1)}, u32[]{:S(2)}, u32[]{:S(2)}) collective-permute-start(bf16[2,256,256]{2,1,0:T(8,128)(2,1)S(1)} %get-tuple-element.68), channel_id=1, source_target_pairs={{0,1},{1,0},{2,3},{3,2},{4,5},{5,4},{6,7},{7,6},{8,9},{9,8},{10,11... | collective-permute-start | bytes 786440 | tf_op jit(solution)/shard_map/ppermute | solution.py:35
  157.5 8.9 %collective-permute-start.15 = (bf16[2,64,256]{2,1,0:T(8,128)(2,1)S(1)}, bf16[2,64,256]{2,1,0:T(8,128)(2,1)S(1)}, u32[]{:S(2)}, u32[]{:S(2)}) collective-permute-start(bf16[2,64,256]{2,1,0:T(8,128)(2,1)S(1)} %get-tuple-element.70), channel_id=1, source_target_pairs={{0,17},{1,16},{2,19},{3,18},{4,21},{5,20},{6,23},{7,22},{8,25},{9,... | collective-permute-start | bytes 196616 | tf_op jit(solution)/shard_map/ppermute | solution.py:351
  160.2 9.2 %collective-permute-start.14 = (bf16[2,64,256]{2,1,0:T(8,128)(2,1)S(1)}, bf16[2,64,256]{2,1,0:T(8,128)(2,1)S(1)}, u32[]{:S(2)}, u32[]{:S(2)}) collective-permute-start(bf16[2,64,256]{2,1,0:T(8,128)(2,1)S(1)} %get-tuple-element.69), channel_id=1, source_target_pairs={{0,16},{16,32},{32,48},{48,64},{64,80},{80,96},{96,112},{112,128},... | collective-permute-start | bytes 196616 | tf_op jit(solution)/shard_map/ppermute | solution.py:40
  169.4 1.2 copy-start.8
